TPU v7x, 128 devices: a whole 4x4x4 slice. The times are simulated.
128 devices in a mesh: seq: 64 (over x, y, z), mlp: 2 (over core).
Axes of the slice: x: 4, y: 4, z: 4, core: 2. Of those that a mesh axis runs over, the one named last changes fastest.
Arguments:
- inputs: bfloat16 [8192, 2048], P(('seq', 'mlp')), may hold values from -6 to 6
- offsets: int32 [8192], P('seq'), may hold values from 0 to 4095, as said below
- norm1_gain: float32 [2048], replicated, may hold values from 0.5 to 1.5
- query_weight: bfloat16 [2048, 2048], P('seq', 'mlp'), may hold values from -0.125 to 0.125
- key_weight: bfloat16 [2048, 2048], P('seq', 'mlp'), may hold values from -0.125 to 0.125
- value_weight: bfloat16 [2048, 2048], P('seq', 'mlp'), may hold values from -0.125 to 0.125
- gate_weight: bfloat16 [2048, 2048], P('seq', 'mlp'), may hold values from -0.125 to 0.125
- out_weight: bfloat16 [2048, 2048], P('mlp', 'seq'), may hold values from -0.1875 to 0.1875
- low_down: bfloat16 [2048, 16], replicated, may hold values from -0.125 to 0.125
- low_up: bfloat16 [16, 256], replicated, may hold values from -1.5 to 1.5
- forget_bias: float32 [256], replicated, may hold values from 1.1 to 8.4
- head_gain: float32 [512], replicated, may hold values from 0.5 to 1.5
- norm2_gain: float32 [2048], replicated, may hold values from 0.5 to 1.5
- ffn_gate: bfloat16 [2048, 5632], P('seq', 'mlp'), may hold values from -0.125 to 0.125
- ffn_up: bfloat16 [2048, 5632], P('seq', 'mlp'), may hold values from -0.125 to 0.125
- ffn_down: bfloat16 [2048, 5632], P('seq', 'mlp'), may hold values from -0.078125 to 0.078125
- cotangent: bfloat16 [8192, 2048], P(('seq', 'mlp')), may hold values from -6 to 6
Outputs:
- output: bfloat16 [8192, 2048], P(('seq', 'mlp'))
- d_inputs: float32 [8192, 2048], P(('seq', 'mlp'))
- d_norm1_gain: float32 [2048], replicated
- d_query_weight: float32 [2048, 2048], P('seq', 'mlp')
- d_key_weight: float32 [2048, 2048], P('seq', 'mlp')
- d_value_weight: float32 [2048, 2048], P('seq', 'mlp')
- d_gate_weight: float32 [2048, 2048], P('seq', 'mlp')
- d_out_weight: float32 [2048, 2048], P('mlp', 'seq')
- d_low_down: float32 [2048, 16], replicated
- d_low_up: float32 [16, 256], replicated
- d_forget_bias: float32 [256], replicated
- d_head_gain: float32 [512], replicated
- d_norm2_gain: float32 [2048], replicated
- d_ffn_gate: float32 [2048, 5632], P('seq', 'mlp')
- d_ffn_up: float32 [2048, 5632], P('seq', 'mlp')
- d_ffn_down: float32 [2048, 5632], P('seq', 'mlp')
Inputs may be any that keep to these rules, and one draw needn't show every extreme that they name: offsets rise by one from token to token within a sequence and restart at 0 where a new sequence begins; the first token has offset 0; a sequence has at most 4096 tokens, and one has exactly 4096.
All inputs are finite; a program needn't handle non-finite values.
Results may differ from a plain program's by a relative error of at most 0.023.
Values may be sent and summed in bfloat16 or wider, within the bound.
A program may use at most 384 MiB of HBM per device.

v0:
```python
import jax
import jax.numpy as jnp
from jax import lax
from jax.sharding import PartitionSpec as P

DK = 512
SLOTS = 64
GROUP = 64


EPS = 1e-06
GATE_NORMALIZER = 8.0
LOGIT_SCALING = 0.125
HIGH_PRECISION_MODE = lax.Precision.HIGHEST


def entering(value, axis, join, neutral):
    count, mine = (lax.axis_size(axis), lax.axis_index(axis))
    pieces = jax.tree.map(lambda part: lax.all_gather(part, axis), value)
    subtotal = jax.tree.map(
        lambda part, zero: jnp.full_like(part, 0) + jnp.asarray(zero, part.dtype), value, neutral
    )

    def entering_hop(position, subtotal):
        longer = join(subtotal, jax.tree.map(lambda part: part[position], pieces))
        return jax.tree.map(lambda new, old: jnp.where(position < mine, new, old), longer, subtotal)

    return lax.fori_loop(0, count - 1, entering_hop, subtotal)


def carried_in(array, axis, combine, identity):
    count, position = (lax.axis_size(axis), lax.axis_index(axis))
    everything = jax.tree.map(
        lambda part, kind: lax.all_gather(part.astype(kind), axis),
        array,
        jax.tree.map(lambda a: jnp.bfloat16 if a.dtype == jnp.float32 else a.dtype, array),
    )
    start = jax.tree.map(
        lambda part, zero: jnp.broadcast_to(jnp.asarray(zero, part.dtype), part.shape),
        array,
        identity,
    )

    def carried_hop(k, before):
        at = count - 1 - k
        reached = at > position
        new = combine(
            before, jax.tree.map(lambda part, own: part[at].astype(own.dtype), everything, array)
        )
        return jax.tree.map(lambda a, b: jnp.where(reached, a, b), new, before)

    return lax.fori_loop(0, count, carried_hop, start)


def rms_scale(value_vectors, gain):
    return (
        value_vectors
        * lax.rsqrt(jnp.mean(value_vectors * value_vectors, axis=-1, keepdims=True) + EPS)
        * gain
    )


def swiglu(gate_act, up_act):
    return jax.nn.silu(gate_act) * up_act


def mixer_tail(mixed, gate_lin, gain):
    normed = rms_scale(mixed, gain)
    return normed.reshape(gate_lin.shape) * jax.nn.silu(gate_lin)


def product(left, right):
    return jnp.dot(left, right, preferred_element_type=jnp.float32)


def rows_inner(left, right):
    return lax.dot_general(
        left, right, (((0,), (0,)), ((), ())), preferred_element_type=jnp.float32
    )


def against(left, right):
    return lax.dot_general(
        left, right, (((1,), (1,)), ((), ())), preferred_element_type=jnp.float32
    )


def advance(key_vectors, value_vectors, decay_log, offsets, key_slot_state, value_slot_state):
    length = offsets.shape[0]
    place = jnp.arange(length, dtype=jnp.int32)
    cumulative_decay = jnp.cumsum(decay_log, axis=0)
    write = -jnp.expm1(decay_log)
    final = offsets[length - 1]
    keep = (final > length - 1).astype(jnp.float32)
    tail = (final - offsets == length - 1 - place).astype(jnp.float32)
    ending_state = (
        jnp.exp(cumulative_decay[length - 1][None] - cumulative_decay) * write * tail[:, None, None]
    )
    decay_factor = keep * jnp.exp(cumulative_decay[length - 1])
    updated_key_state = decay_factor[:, :, None] * key_slot_state + jnp.einsum(
        "aqo,aqf->qof", ending_state, key_vectors, precision=HIGH_PRECISION_MODE
    )
    updated_value_state = decay_factor[:, :, None] * value_slot_state + jnp.einsum(
        "aqo,aqf->qof", ending_state, value_vectors, precision=HIGH_PRECISION_MODE
    )
    return (updated_key_state, updated_value_state, decay_factor)


def slot_group(
    query_vectors, key_vectors, value_vectors, logits, offsets, key_slot_state, value_slot_state
):
    decay_log = jax.nn.log_sigmoid(logits) / GATE_NORMALIZER
    length = offsets.shape[0]
    place = jnp.arange(length, dtype=jnp.int32)
    cumulative_decay = jnp.cumsum(decay_log, axis=0)
    write = -jnp.expm1(decay_log)
    carried_over = (offsets > place).astype(jnp.float32)
    causal = (place[:, None] >= place[None, :]) & (
        offsets[:, None] - offsets[None, :] == place[:, None] - place[None, :]
    )
    spread = cumulative_decay[:, None] - cumulative_decay[None, :]
    weights = jnp.exp(jnp.where(causal[:, :, None, None], spread, -1e30)) * write[None]
    affinity = (
        jnp.einsum("thd,ihd->thi", query_vectors, key_vectors, precision=HIGH_PRECISION_MODE)
        * LOGIT_SCALING
    )
    scores = jnp.einsum("thi,tihm->thm", affinity, weights, precision=HIGH_PRECISION_MODE)
    earlier_tokens = (
        jnp.einsum("vbn,bgn->vbg", query_vectors, key_slot_state, precision=HIGH_PRECISION_MODE)
        * LOGIT_SCALING
    )
    scores = scores + carried_over[:, None, None] * jnp.exp(cumulative_decay) * earlier_tokens
    slot_probabilities = jax.nn.softmax(scores, axis=-1)
    mixing = jnp.einsum("thm,tihm->thi", slot_probabilities, weights, precision=HIGH_PRECISION_MODE)
    output = jnp.einsum("thi,ihd->thd", mixing, value_vectors, precision=HIGH_PRECISION_MODE)
    output = output + carried_over[:, None, None] * jnp.einsum(
        "gnw,nwv->gnv",
        slot_probabilities * jnp.exp(cumulative_decay),
        value_slot_state,
        precision=HIGH_PRECISION_MODE,
    )
    updated_key_state, updated_value_state, decay_factor = advance(
        key_vectors, value_vectors, decay_log, offsets, key_slot_state, value_slot_state
    )
    return (output, updated_key_state, updated_value_state)


def split_blocks(key_vectors, value_vectors, logits, offsets):
    count = offsets.shape[0] // GROUP
    heads_here = key_vectors.shape[1]
    return (
        key_vectors.reshape(count, GROUP, heads_here, DK),
        value_vectors.reshape(count, GROUP, heads_here, DK),
        logits.reshape(count, GROUP, heads_here, SLOTS),
        offsets.reshape(count, GROUP),
    )


def local_end(key_vectors, value_vectors, logits, offsets):
    blocks = split_blocks(key_vectors, value_vectors, logits, offsets)
    heads_here = key_vectors.shape[1]

    def step(carry, block):
        decay_log = jax.nn.log_sigmoid(block[2]) / GATE_NORMALIZER
        updated_key_state, updated_value_state, decay_factor = advance(
            block[0], block[1], decay_log, block[3], carry[0], carry[1]
        )
        return ((updated_key_state, updated_value_state, carry[2] * decay_factor), None)

    start = (
        jnp.zeros((heads_here, SLOTS, DK), jnp.float32),
        jnp.zeros((heads_here, SLOTS, DK), jnp.float32),
        jnp.ones((heads_here, SLOTS), jnp.float32),
    )
    final, _ = lax.scan(jax.checkpoint(step), start, blocks)
    return (final[2], final[0], final[1])


def local_out(
    query_vectors, key_vectors, value_vectors, logits, offsets, key_slot_state, value_slot_state
):
    count = offsets.shape[0] // GROUP
    rest = split_blocks(key_vectors, value_vectors, logits, offsets)
    blocks = (query_vectors.reshape(count, GROUP, key_vectors.shape[1], DK),) + rest

    def step(carry, block):
        output, updated_key_state, updated_value_state = slot_group(
            block[0], block[1], block[2], block[3], block[4], carry[0], carry[1]
        )
        return ((updated_key_state, updated_value_state), output)

    _, outputs = lax.scan(jax.checkpoint(step), (key_slot_state, value_slot_state), blocks)
    return outputs.reshape(offsets.shape[0], key_vectors.shape[1], DK)


def compose(earlier_tokens, later):
    return (
        earlier_tokens[0] * later[0],
        later[0] * earlier_tokens[1] + later[1],
        later[0] * earlier_tokens[2] + later[2],
    )


def compose_back(earlier_tokens, later):
    return (
        earlier_tokens[0] * later[0],
        later[1] + later[0] * earlier_tokens[1],
        later[2] + later[0] * earlier_tokens[2],
    )


def body(
    inputs,
    offsets,
    norm1_gain,
    query_weight,
    key_weight,
    value_weight,
    gate_weight,
    out_weight,
    low_down,
    low_up,
    forget_bias,
    head_gain,
    norm2_gain,
    ffn_gate,
    ffn_up,
    ffn_down,
    cotangent,
):
    rows = inputs.shape[0]
    pair_count = offsets.shape[0]
    first_own = lax.axis_index("mlp") * rows
    mixer_full = (
        lax.all_gather(query_weight, "seq", axis=0, tiled=True),
        lax.all_gather(key_weight, "seq", axis=0, tiled=True),
        lax.all_gather(value_weight, "seq", axis=0, tiled=True),
        lax.all_gather(gate_weight, "seq", axis=0, tiled=True),
        lax.all_gather(out_weight, "seq", axis=1, tiled=True),
    )
    full_query, full_key, full_value, full_gate, full_out = mixer_full
    width = full_query.shape[1]
    heads_here = width // DK
    head_first = lax.axis_index("mlp") * heads_here

    def own_rows(value_vectors):
        return lax.dynamic_slice_in_dim(value_vectors, first_own, rows, 0)

    pair_inputs = lax.all_gather(inputs, "mlp", axis=0, tiled=True)
    resid = pair_inputs.astype(jnp.float32)
    first_b = rms_scale(resid, norm1_gain).astype(jnp.bfloat16)
    first_f = first_b.astype(jnp.float32)
    query_own = product(first_b, full_query).astype(jnp.bfloat16)
    key_own = product(first_b, full_key).astype(jnp.bfloat16)
    value_own = product(first_b, full_value).astype(jnp.bfloat16)
    up_cols = lax.dynamic_slice_in_dim(
        low_up.astype(jnp.float32), head_first * SLOTS, heads_here * SLOTS, 1
    )
    bias_cols = lax.dynamic_slice_in_dim(forget_bias, head_first * SLOTS, heads_here * SLOTS, 0)
    lowrank = jnp.dot(first_f, low_down.astype(jnp.float32), precision=HIGH_PRECISION_MODE)
    logit_own = (jnp.dot(lowrank, up_cols, precision=HIGH_PRECISION_MODE) + bias_cols).astype(
        jnp.bfloat16
    )
    query_all = query_own.astype(jnp.float32).reshape(pair_count, heads_here, DK)
    key_all = key_own.astype(jnp.float32).reshape(pair_count, heads_here, DK)
    value_all = value_own.astype(jnp.float32).reshape(pair_count, heads_here, DK)
    logit_all = logit_own.astype(jnp.float32).reshape(pair_count, heads_here, SLOTS)

    def end_part(key_vectors, value_vectors, logits):
        return local_end(key_vectors, value_vectors, logits, offsets)

    (decay_factor, end_k, end_v), back_end = jax.vjp(end_part, key_all, value_all, logit_all)
    neutral = (
        jnp.ones((heads_here, SLOTS, 1), jnp.float32),
        jnp.zeros((heads_here, SLOTS, DK), jnp.float32),
        jnp.zeros((heads_here, SLOTS, DK), jnp.float32),
    )
    carried_over = entering((decay_factor[:, :, None], end_k, end_v), "seq", compose, neutral)
    start_k, start_v = (carried_over[1], carried_over[2])

    def out_part(
        query_vectors, key_vectors, value_vectors, logits, key_slot_state, value_slot_state
    ):
        return local_out(
            query_vectors,
            key_vectors,
            value_vectors,
            logits,
            offsets,
            key_slot_state,
            value_slot_state,
        )

    mixed_all, back_out = jax.vjp(
        out_part, query_all, key_all, value_all, logit_all, start_k, start_v
    )
    gate_lin = product(first_b, full_gate)
    branch, back_tail = jax.vjp(mixer_tail, mixed_all, gate_lin, head_gain)
    branch_b = branch.astype(jnp.bfloat16)
    resid1 = resid + lax.psum(product(branch_b, full_out).astype(jnp.bfloat16), "mlp").astype(
        jnp.float32
    )
    normed2, back_norm2 = jax.vjp(rms_scale, resid1, norm2_gain)
    second_all = normed2.astype(jnp.bfloat16)
    ffn_full = (
        lax.all_gather(ffn_gate, "seq", axis=0, tiled=True),
        lax.all_gather(ffn_up, "seq", axis=0, tiled=True),
        lax.all_gather(ffn_down, "seq", axis=0, tiled=True),
    )
    gate_cols, up_cols_ffn, down_cols = ffn_full
    act_gate = product(second_all, gate_cols)
    act_up = product(second_all, up_cols_ffn)
    hidden, back_act = jax.vjp(swiglu, act_gate, act_up)
    hidden_b = hidden.astype(jnp.bfloat16)
    piece = hidden_b
    ffn_out = lax.psum_scatter(
        against(piece, down_cols).astype(jnp.bfloat16), "mlp", scatter_dimension=0, tiled=True
    ).astype(jnp.float32)
    output = (own_rows(resid1) + ffn_out).astype(jnp.bfloat16)
    cot_all = lax.all_gather(cotangent, "mlp", axis=0, tiled=True)
    grad_hidden = product(cot_all, down_cols)
    grad_gate_act, grad_up_act = back_act(grad_hidden)
    grad_gate_b = grad_gate_act.astype(jnp.bfloat16)
    grad_up_b = grad_up_act.astype(jnp.bfloat16)
    grad_down_cols = rows_inner(cot_all, hidden_b)
    grad_gate_cols = rows_inner(second_all, grad_gate_b)
    grad_up_cols = rows_inner(second_all, grad_up_b)
    grad_second = lax.psum(
        (against(grad_gate_b, gate_cols) + against(grad_up_b, up_cols_ffn)).astype(jnp.bfloat16),
        "mlp",
    ).astype(jnp.float32)
    grad_resid1 = back_norm2(grad_second)[0] + cot_all.astype(jnp.float32)
    _, back_norm2_own = jax.vjp(rms_scale, own_rows(resid1), norm2_gain)
    grad_norm2 = back_norm2_own(own_rows(grad_second))[1]
    grad_attn_b = grad_resid1.astype(jnp.bfloat16)
    grad_branch = against(grad_attn_b, full_out)
    grad_mixed, grad_gate_lin, grad_head = back_tail(grad_branch)
    grad_lin_b = grad_gate_lin.astype(jnp.bfloat16)
    mixed_grad = lax.optimization_barrier(grad_mixed.astype(jnp.bfloat16)).astype(jnp.float32)
    part_query, part_key, part_value, part_logit, start_grad_k, start_grad_v = back_out(mixed_grad)
    later = carried_in(
        (decay_factor[:, :, None], start_grad_k, start_grad_v), "seq", compose_back, neutral
    )
    next_k, next_v = (later[1], later[2])
    grad_factor = jnp.sum(next_k * start_k, axis=-1) + jnp.sum(next_v * start_v, axis=-1)
    extra_key, extra_value, extra_logit = back_end((grad_factor, next_k, next_v))
    grad_query_b = part_query.reshape(pair_count, width).astype(jnp.bfloat16)
    grad_key_b = (part_key + extra_key).reshape(pair_count, width).astype(jnp.bfloat16)
    grad_value_b = (part_value + extra_value).reshape(pair_count, width).astype(jnp.bfloat16)
    grad_logit = (part_logit + extra_logit).reshape(pair_count, heads_here * SLOTS)
    grad_lowrank = jnp.dot(grad_logit, up_cols.T, precision=HIGH_PRECISION_MODE)
    low_down_f = low_down.astype(jnp.float32)

    def piece(value_vectors):
        return value_vectors

    total = against(piece(grad_lin_b), full_gate) + against(piece(grad_query_b), full_query)
    total = total + against(piece(grad_key_b), full_key) + against(piece(grad_value_b), full_value)
    grad_first = lax.psum_scatter(
        (total + jnp.dot(piece(grad_lowrank), low_down_f.T, precision=HIGH_PRECISION_MODE)).astype(
            jnp.bfloat16
        ),
        "mlp",
        scatter_dimension=0,
        tiled=True,
    ).astype(jnp.float32)
    _, back_norm1 = jax.vjp(rms_scale, inputs.astype(jnp.float32), norm1_gain)
    grad_resid, grad_norm1 = back_norm1(grad_first)
    grad_inputs = own_rows(grad_resid1) + grad_resid
    zeros_up = jnp.zeros((low_up.shape[0], low_up.shape[1]), jnp.float32)
    grad_low_up = lax.dynamic_update_slice_in_dim(
        zeros_up,
        jnp.dot(lowrank.T, grad_logit, precision=HIGH_PRECISION_MODE),
        head_first * SLOTS,
        1,
    )
    grad_bias = lax.dynamic_update_slice_in_dim(
        jnp.zeros(forget_bias.shape, jnp.float32),
        jnp.sum(grad_logit, axis=0),
        head_first * SLOTS,
        0,
    )
    grad_low_down = jnp.dot(first_f.T, grad_lowrank, precision=HIGH_PRECISION_MODE)
    mixer_sums = lax.psum_scatter(
        jnp.concatenate(
            [
                rows_inner(first_b, grad_query_b),
                rows_inner(first_b, grad_key_b),
                rows_inner(first_b, grad_value_b),
                rows_inner(first_b, grad_lin_b),
                rows_inner(grad_attn_b, branch_b),
            ],
            axis=1,
        ),
        "seq",
        scatter_dimension=0,
        tiled=True,
    )
    ffn_sums = (
        lax.psum_scatter(grad_gate_cols, "seq", scatter_dimension=0, tiled=True),
        lax.psum_scatter(grad_up_cols, "seq", scatter_dimension=0, tiled=True),
        lax.psum_scatter(grad_down_cols, "seq", scatter_dimension=0, tiled=True),
    )
    small_sums = lax.psum(
        (grad_norm1, grad_norm2, grad_head, grad_low_down, grad_low_up, grad_bias), ("seq", "mlp")
    )
    return (
        output,
        grad_inputs,
        small_sums[0],
        mixer_sums[:, 0:width],
        mixer_sums[:, width : 2 * width],
        mixer_sums[:, 2 * width : 3 * width],
        mixer_sums[:, 3 * width : 4 * width],
        mixer_sums[:, 4 * width : 5 * width].T,
        small_sums[3],
        small_sums[4],
        small_sums[5],
        small_sums[2],
        small_sums[1],
        ffn_sums[0],
        ffn_sums[1],
        ffn_sums[2],
    )


def solution(mesh):
    placed = (
        P(("seq", "mlp"), None),
        P("seq"),
        P(),
        P("seq", "mlp"),
        P("seq", "mlp"),
        P("seq", "mlp"),
        P("seq", "mlp"),
        P("mlp", "seq"),
        P(),
        P(),
        P(),
        P(),
        P(),
        P("seq", "mlp"),
        P("seq", "mlp"),
        P("seq", "mlp"),
        P(("seq", "mlp"), None),
    )
    return jax.shard_map(
        body,
        mesh=mesh,
        in_specs=placed,
        out_specs=(
            P(("seq", "mlp"), None),
            P(("seq", "mlp"), None),
            P(),
            P("seq", "mlp"),
            P("seq", "mlp"),
            P("seq", "mlp"),
            P("seq", "mlp"),
            P("mlp", "seq"),
            P(),
            P(),
            P(),
            P(),
            P(),
            P("seq", "mlp"),
            P("seq", "mlp"),
            P("seq", "mlp"),
        ),
        check_vma=False,
    )
```

profile of v0, /device:TPU:1, one launch (start us, length us, event | category | flops | bytes accessed | tf_op | source)
XLA Modules:
  0.0 3219.1 jit_solution(13855077899266522103)
XLA Ops:
  17.4 64.9 %all-gather.21.cloned.1.call-done = bf16[2048,1024]{1,0:T(8,128)(2,1)} async-done(((bf16[32,1024]{1,0:T(8,128)(2,1)}), bf16[2048,1024]{1,0:T(8,128)(2,1)}) %all-gather.21.cloned.1.call-update) | async-done | bytes 4194320 | tf_op jit(solution)/shard_map/all_gather | solution.py:236
  85.8 65.8 %all-gather.23.cloned.1.call-done = bf16[2048,1024]{1,0:T(8,128)(2,1)} async-done(((bf16[32,1024]{1,0:T(8,128)(2,1)}), bf16[2048,1024]{1,0:T(8,128)(2,1)}) %all-gather.23.cloned.1.call-update) | async-done | bytes 4194320 | tf_op jit(solution)/shard_map/all_gather | solution.py:237
  155.3 10.5 while.126
  169.8 145.8 %all-gather.6 = f32[64,2,64]{2,1,0:T(2,128)S(1)} all-gather(f32[1,2,64]{2,1,0:T(2,128)S(1)} %bitcast.802), channel_id=2, replica_groups=mesh['seq'=64,'mlp'=2] {'seq'}, dimensions={0}, use_global_device_ids=true | all-gather | bytes 33280 | tf_op jit(solution)/shard_map/all_gather | solution.py:19
  327.3 107.2 %all-gather.39.cloned.1.call-done = f32[128,64,512]{2,1,0:T(8,128)} async-done(((f32[2,64,512]{2,1,0:T(8,128)}), f32[128,64,512]{2,1,0:T(8,128)}) %all-gather.39.cloned.1.call-update) | async-done | bytes 16777232 | tf_op jit(solution)/shard_map/all_gather | solution.py:19
  434.5 76.1 %while.127 = (s32[]{:T(128)}, f32[2,64,512]{2,1,0:T(8,128)S(1)}, f32[2,64,512]{2,1,0:T(8,128)S(1)}, s32[]{:T(128)}, f32[64,2,64,1]{2,1,3,0:T(2,128)S(1)}, /*inde...) while((s32[]{:T(128)}, f32[2,64,512]{2,1,0:T(8,128)S(1)}, ...), condition=%wide.region_5.6_spmd.clone, body=%wide.region_4.5_spmd.clone.sunk | while | flops 524292 | bytes 1574529 | solution.py:28
  513.3 73.6 %while.125 = (s32[]{:T(128)}, f32[2,64,512]{2,1,0:T(8,128)S(1)}, f32[2,64,512]{2,1,0:T(8,128)S(1)}, f32[2,64,2,512]{3,1,2,0:T(8,128)S(1)}, f32[2,2,64,512]{3,2,1...) while((s32[]{:T(128)}, f32[2,64,512]{2,1,0:T(8,128)S(1)}, ...), condition=%wide.region_10.11_spmd.clone, body=%wide.region_6.10_spmd.clone.sunk | while | flops 317420096 | bytes 16664779 | solution.py:192
  530.6 8.3 fusion.485
  567.4 8.4 fusion.485
  603.8 19.3 all-reduce.9.cloned.1.call-done
  625.7 89.7 %all-gather.31.cloned.1.call-done = bf16[2048,2816]{1,0:T(8,128)(2,1)} async-done(((bf16[32,2816]{1,0:T(8,128)(2,1)}), bf16[2048,2816]{1,0:T(8,128)(2,1)}) %all-gather.31.cloned.1.call-update) | async-done | bytes 11534352 | tf_op jit(solution)/shard_map/all_gather | solution.py:306
  722.5 83.7 %all-gather.33.cloned.1.call-done = bf16[2048,2816]{1,0:T(8,128)(2,1)} async-done(((bf16[32,2816]{1,0:T(8,128)(2,1)}), bf16[2048,2816]{1,0:T(8,128)(2,1)}) %all-gather.33.cloned.1.call-update) | async-done | bytes 11534352 | tf_op jit(solution)/shard_map/all_gather | solution.py:307
  813.3 83.9 %all-gather.35.cloned.1.call-done = bf16[2048,2816]{1,0:T(8,128)(2,1)} async-done(((bf16[32,2816]{1,0:T(8,128)(2,1)}), bf16[2048,2816]{1,0:T(8,128)(2,1)}) %all-gather.35.cloned.1.call-update) | async-done | bytes 11534352 | tf_op jit(solution)/shard_map/all_gather | solution.py:308
  897.2 8.2 multiply_convert_fusion
  905.4 8.6 fusion.246
  921.1 22.1 all-reduce.11.cloned.1.call-done
  956.8 121.7 %while.128 = (s32[]{:T(128)}, f32[2,64,512]{2,1,0:T(8,128)}, f32[2,64,512]{2,1,0:T(8,128)}, bf16[2,64,2,512]{3,1,2,0:T(8,128)(2,1)}, f32[2,64,2,512]{3,1,2,0:T(8...) while((s32[]{:T(128)}, f32[2,64,512]{2,1,0:T(8,128)}, ...), condition=%wide.region_31.33_spmd.clone, body=%wide.region_18.32_spmd.clone.sunk | while | flops 735433216 | bytes 26870560 | solution.py:192
  991.4 7.9 fusion.544
  1082.6 147.7 %all-gather.7 = bf16[64,2,64]{2,1,0:T(2,128)(2,1)S(1)} all-gather(bf16[1,2,64]{2,1,0:T(2,128)(2,1)S(1)} %convert_bitcast_fusion), channel_id=6, replica_groups=mesh['seq'=64,'mlp'=2] {'seq'}, dimensions={0}, use_global_device_ids=true | all-gather | bytes 16640 | tf_op jit(solution)/shard_map/all_gather | solution.py:34
  1230.4 9.5 convolution_convert_fusion
  1249.7 74.5 %while.129 = (s32[]{:T(128)}, f32[2,64,512]{2,1,0:T(8,128)S(1)}, f32[2,64,512]{2,1,0:T(8,128)S(1)}, s32[]{:T(128)}, bf16[64,2,64,512]{3,2,1,0:T(8,128)(2,1)}, /*...) while((s32[]{:T(128)}, f32[2,64,512]{2,1,0:T(8,128)S(1)}, ...), condition=%wide.region_33.35_spmd.clone, body=%wide.region_32.34_spmd.clone.sunk | while | flops 655496 | bytes 1312191 | solution.py:52
  1326.8 18.2 while.124
  1374.0 38.8 %copy.351 = f32[2048,5120]{1,0:T(8,128)} copy(f32[2048,5120]{0,1:T(8,128)} %convolution_dynamic-update-slice_fusion) | data formatting | bytes 83886080
  1414.1 9.5 fusion.248
  1424.7 9.3 fusion.249
  1435.3 9.7 convolution_bitcast_fusion.5
  1445.0 23.4 copy.353
  1475.6 463.8 %all-reduce.4 = (f32[2048]{0:T(1024)}, f32[16,256]{1,0:T(8,128)}, f32[256]{0:T(256)}, f32[512]{0:T(512)}, f32[2048]{0:T(1024)}) all-reduce(f32[2048]{0:T(1024)S(1)} %get-tuple-element.1715, f32[16,256]{1,0:T(8,128)S(1)} %convolution_dynamic-update-slice_fusion.5, ...), channel_id=1, replica_groups=mesh['seq'=64,'mlp'=2] {'seq','mlp'}, use_global_device_ids=true, to_apply=%region_47.49 | all-reduce | flops 8960 | bytes 71680 | tf_op jit(solution)/shard_map/psum | solution.py:404
  1943.3 106.8 %all-reduce.13.cloned.1.call-done = f32[2048,16]{0,1:T(8,128)} async-done(((f32[2048,16]{0,1:T(8,128)}), f32[2048,16]{0,1:T(8,128)}) %all-reduce.13.cloned.1.call-update) | async-done | bytes 131088 | tf_op jit(solution)/shard_map/psum | solution.py:404
  2050.1 356.7 %reduce-scatter.15.cloned.1.call-done = f32[32,2816]{1,0:T(8,128)} async-done(((f32[2048,2816]{1,0:T(8,128)}), f32[32,2816]{1,0:T(8,128)}) %reduce-scatter.15.cloned.1.call-update) | async-done | bytes 360464 | tf_op jit(solution)/shard_map/reduce_scatter | solution.py:400
  2406.8 402.1 %reduce-scatter.17.cloned.1.call-done = f32[32,2816]{1,0:T(8,128)} async-done(((f32[2048,2816]{1,0:T(8,128)}), f32[32,2816]{1,0:T(8,128)}) %reduce-scatter.17.cloned.1.call-update) | async-done | bytes 360464 | tf_op jit(solution)/shard_map/reduce_scatter | solution.py:401
  2809.0 401.5 %reduce-scatter.21.cloned.1.call-done = f32[32,2816]{1,0:T(8,128)} async-done(((f32[2048,2816]{1,0:T(8,128)}), f32[32,2816]{1,0:T(8,128)}) %reduce-scatter.21.cloned.1.call-update) | async-done | bytes 360464
  (842 shorter events, 488.8 us)
Async XLA Ops:
  7.2 75.1 %all-gather.21.cloned.1.call-start = ((), (), s32[]{:S(2)}) async-start(), calls=%async_computation.6 | async-start | bytes 4259840 | tf_op jit(solution)/shard_map/all_gather | solution.py:236
  7.9 143.7 %all-gather.23.cloned.1.call-start = ((), (), s32[]{:S(2)}) async-start(), calls=%async_computation.7 | async-start | bytes 4259840 | tf_op jit(solution)/shard_map/all_gather | solution.py:237
  8.7 306.9 %all-gather.25.cloned.1.call-start = ((), (), s32[]{:S(2)}) async-start(), calls=%async_computation.8 | async-start | bytes 4259840 | tf_op jit(solution)/shard_map/all_gather | solution.py:235
  9.4 317.9 %all-gather.37.cloned.1.call-start = ((), (), s32[]{:S(2)}) async-start(), calls=%async_computation.21 | async-start | bytes 17039360 | tf_op jit(solution)/shard_map/all_gather | solution.py:19
  15.2 574.4 %copy-start.60 = (f32[128]{0:T(128)}, f32[128]{0:T(128)S(1)}, u32[]{:S(2)}) copy-start(f32[128]{0:T(128)S(1)} %add_rsqrt_fusion.1) | copy-start | bytes 1540
  15.2 136.5 %copy-start.39 = (f32[2048]{0:T(1024)S(1)}, f32[2048]{0:T(1024)}, u32[]{:S(2)}) copy-start(f32[2048]{0:T(1024)} %param.32) | copy-start | bytes 24580
  165.8 268.6 %copy-start.26 = (f32[2,2,64,512]{3,2,1,0:T(8,128)}, f32[2,2,64,512]{3,2,1,0:T(8,128)S(1)}, u32[]{:S(2)}) copy-start(f32[2,2,64,512]{3,2,1,0:T(8,128)S(1)} %get-tuple-element.2669) | copy-start | bytes 1572868
  165.8 268.6 %copy-start.57 = (f32[2,64]{1,0:T(2,128)}, f32[2,64]{1,0:T(2,128)S(1)}, u32[]{:S(2)}) copy-start(f32[2,64]{1,0:T(2,128)S(1)} %get-tuple-element.1112) | copy-start | bytes 1540
  166.5 268.0 %all-gather.39.cloned.1.call-start = ((), (), s32[]{:S(2)}) async-start(), calls=%async_computation.22 | async-start | bytes 17039360 | tf_op jit(solution)/shard_map/all_gather | solution.py:19
  167.1 422.5 %all-gather.27.cloned.1.call-start = ((), (), s32[]{:S(2)}) async-start(), calls=%async_computation.9 | async-start | bytes 4259840 | tf_op jit(solution)/shard_map/all_gather | solution.py:238
  167.7 426.3 %all-gather.29.cloned.1.call-start = ((), (), s32[]{:S(2)}) async-start(), calls=%async_computation.10 | async-start | bytes 4259840 | tf_op jit(solution)/shard_map/all_gather | solution.py:239
  168.4 454.7 %all-reduce.9.cloned.1.call-start = ((), (), s32[]{:S(2)}) async-start(), calls=%async_computation.11 | async-start | bytes 1048576 | tf_op jit(solution)/shard_map/psum | solution.py:300
  594.0 30.5 copy-start.59
  598.6 116.8 %all-gather.31.cloned.1.call-start = ((), (), s32[]{:S(2)}) async-start(), calls=%async_computation.12 | async-start | bytes 11714560 | tf_op jit(solution)/shard_map/all_gather | solution.py:306
  599.3 206.9 %all-gather.33.cloned.1.call-start = ((), (), s32[]{:S(2)}) async-start(), calls=%async_computation.13 | async-start | bytes 11714560 | tf_op jit(solution)/shard_map/all_gather | solution.py:307
  599.9 297.3 %all-gather.35.cloned.1.call-start = ((), (), s32[]{:S(2)}) async-start(), calls=%async_computation.14 | async-start | bytes 11714560 | tf_op jit(solution)/shard_map/all_gather | solution.py:308
  600.7 342.5 %all-reduce.11.cloned.1.call-start = ((), (), s32[]{:S(2)}) async-start(), calls=%async_computation.16 | async-start | bytes 1048576 | tf_op jit(solution)/shard_map/psum | solution.py:328
  603.8 340.9 %copy-start.27 = (bf16[128,2048]{1,0:T(8,128)(2,1)}, bf16[128,2048]{1,0:T(8,128)(2,1)S(1)}, u32[]{:S(2)}) copy-start(bf16[128,2048]{1,0:T(8,128)(2,1)S(1)} %all_gather.77) | copy-start | bytes 1572868
  625.7 180.5 %copy-start.7 = (bf16[128,2048]{1,0:T(8,128)(2,1)}, bf16[128,2048]{1,0:T(8,128)(2,1)S(1)}, u32[]{:S(2)}) copy-start(bf16[128,2048]{1,0:T(8,128)(2,1)S(1)} %multiply_convert_fusion.2) | copy-start | bytes 1572868
  918.7 331.0 %all-gather.41.cloned.1.call-start = ((), (), s32[]{:S(2)}) async-start(), calls=%async_computation.23 | async-start | bytes 8519680 | tf_op jit(solution)/shard_map/all_gather | solution.py:34
  1080.2 169.5 %all-gather.43.cloned.1.call-start = ((), (), s32[]{:S(2)}) async-start(), calls=%async_computation.24 | async-start | bytes 8519680 | tf_op jit(solution)/shard_map/all_gather | solution.py:34
  1081.9 389.9 %reduce-scatter.11.cloned.1.call-start = ((), (), s32[]{:S(2)}) async-start(), calls=%async_computation.15 | async-start | bytes 786432 | tf_op jit(solution)/shard_map/reduce_scatter | solution.py:316
  1239.9 234.4 %reduce-scatter.13.cloned.1.call-start = ((), (), s32[]{:S(2)}) async-start(), calls=%async_computation.17 | async-start | bytes 786432 | tf_op jit(solution)/shard_map/reduce_scatter | solution.py:359
  1249.7 74.5 %copy-start.15 = (f32[2,64,512]{2,1,0:T(8,128)S(1)}, f32[2,64,512]{2,1,0:T(8,128)}, u32[]{:S(2)}) copy-start(f32[2,64,512]{2,1,0:T(8,128)} %copy-done.14) | copy-start | bytes 786436
  1249.7 74.5 %copy-start.17 = (f32[2,64,512]{2,1,0:T(8,128)S(1)}, f32[2,64,512]{2,1,0:T(8,128)}, u32[]{:S(2)}) copy-start(f32[2,64,512]{2,1,0:T(8,128)} %copy-done.16) | copy-start | bytes 786436
  1249.7 77.1 %copy-start.25 = (f32[2,2,64,512]{3,2,1,0:T(8,128)S(1)}, f32[2,2,64,512]{3,2,1,0:T(8,128)}, u32[]{:S(2)}) copy-start(f32[2,2,64,512]{3,2,1,0:T(8,128)} %copy-done.24) | copy-start | bytes 1572868
  1249.7 77.1 %copy-start.65 = (f32[2,2,64]{2,1,0:T(2,128)S(1)}, f32[2,2,64]{2,1,0:T(2,128)}, u32[]{:S(2)}) copy-start(f32[2,2,64]{2,1,0:T(2,128)} %get-tuple-element.2670) | copy-start | bytes 3076
  1360.2 581.1 %reduce-scatter.19.cloned.1.call-start = ((), (), s32[]{:S(2)}) async-start(), calls=%async_computation.25 | async-start | bytes 42598400
  1412.8 637.3 %all-reduce.13.cloned.1.call-start = ((), (), s32[]{:S(2)}) async-start(), calls=%async_computation.18 | async-start | bytes 262144 | tf_op jit(solution)/shard_map/psum | solution.py:404
  1414.0 992.8 %reduce-scatter.15.cloned.1.call-start = ((), (), s32[]{:S(2)}) async-start(), calls=%async_computation.19 | async-start | bytes 23429120 | tf_op jit(solution)/shard_map/reduce_scatter | solution.py:400
  1423.6 1385.3 %reduce-scatter.17.cloned.1.call-start = ((), (), s32[]{:S(2)}) async-start(), calls=%async_computation.20 | async-start | bytes 23429120 | tf_op jit(solution)/shard_map/reduce_scatter | solution.py:401
  1434.0 1776.5 %reduce-scatter.21.cloned.1.call-start = ((), (), s32[]{:S(2)}) async-start(), calls=%async_computation.26 | async-start | bytes 23429120
  (82 other events, 516.7 us)
Sparse Core Ops, SparseCore 0:
  10.9 71.3 all-gather.20
  85.2 66.4 all-gather.22
  154.6 66.4 all-gather.24
  224.4 102.8 all-gather.36
  330.6 103.8 all-gather.38
  437.2 67.6 all-gather.26
  507.8 66.5 all-gather.28
  598.7 24.3 all-reduce.8
  626.4 88.9 all-gather.30
  718.5 87.6 all-gather.32
  809.5 87.6 all-gather.34
  918.8 24.2 all-reduce.10
  1080.3 79.6 all-gather.40
  1163.3 78.3 all-gather.42
  1244.5 27.2 reduce-scatter.10
  1360.3 31.6 reduce-scatter.12
  1412.9 464.8 reduce-scatter.18
  1883.0 167.0 all-reduce.12
  2053.2 353.5 reduce-scatter.14
  2409.8 399.1 reduce-scatter.16
  2812.1 398.3 reduce-scatter.20
where the time goes:
time: 3280 us; the launch traced here: 3220 us
  waiting for transfers between devices  1810 us (55%)
  blocking collectives  764 us (23%)
  other arithmetic  238 us (7%)
  matrix products  229 us (7%)
  local copies, waits for them, and re-layouts  146 us (4%)
    psum x1, blocking collectives, body(): lax.psum((grad_norm1, grad_norm2, grad_head, grad_low_down, grad_low_up,...  464 us
    unnamed x23, waiting for transfers between devices  407 us
    reduce_scatter x1, waiting for transfers between devices, body(): lax.psum_scatter(grad_up_cols, 'seq', scatter_dimension=0, tiled=True)  402 us
    reduce_scatter x1, waiting for transfers between devices, body(): lax.psum_scatter(grad_gate_cols, 'seq', scatter_dimension=0, tiled=True)  357 us
    all_gather x1, blocking collectives, carried_in(): lax.all_gather(part.astype(kind), axis)  148 us
    all_gather x1, blocking collectives, entering(): pieces = jax.tree.map(lambda part: lax.all_gather(part, axis), value)  146 us
    all_gather x2, waiting for transfers between devices, entering(): pieces = jax.tree.map(lambda part: lax.all_gather(part, axis), value)  111 us
    psum x1, waiting for transfers between devices, body(): lax.psum((grad_norm1, grad_norm2, grad_head, grad_low_down, grad_low_up,...  107 us
  transfers between devices with their start and end apart: 21, of which 13 were waited for; matrix products, arithmetic and copies ran while one was open for 14% of the time, Pallas kernels for 0%

commit v1 on v0

v1 whole, which is shorter than its diff:
```python
import functools

import jax
import jax.numpy as jnp
from jax import lax
from jax.experimental import pallas as pl
from jax.experimental.pallas import tpu as pltpu
from jax.sharding import Mesh
from jax.sharding import PartitionSpec as P

DK = 512
SLOTS = 64
CHUNK = 64
HALF = 256
UNITS = 704
UNITS_PAD = 768
REACH = 8
EPS = 1e-06
SCALE = 0.125
BF = jnp.bfloat16
F32 = jnp.float32
HIGH = lax.Precision.HIGHEST
MESH = pl.DeviceIdType.MESH
ANY = pl.BlockSpec(memory_space=pl.ANY)
VMEM = pl.BlockSpec(memory_space=pltpu.VMEM)
DMA = pltpu.SemaphoreType.DMA
MIX = 5 * HALF
FFN = 3 * UNITS_PAD


def dot(left, right, dims=((1,), (0,)), precision=None):
    return lax.dot_general(
        left, right, (dims, ((), ())), precision=precision, preferred_element_type=F32
    )


def nt(left, right, precision=None):
    return dot(left, right, ((1,), (1,)), precision)


def tn(left, right, precision=None):
    return dot(left, right, ((0,), (0,)), precision)


def here():
    return tuple(lax.axis_index(a) for a in ("x", "y", "z", "c"))


def wrap(v, n=4):
    return lax.rem(v + n, n)


def greet(peers):
    barrier = pltpu.get_barrier_semaphore()
    for peer in peers:
        pl.semaphore_signal(barrier, inc=1, device_id=peer, device_id_type=MESH)
    pl.semaphore_wait(barrier, len(peers))


def push(src, dst, send, recv, peer):
    copy = pltpu.make_async_remote_copy(
        src_ref=src, dst_ref=dst, send_sem=send, recv_sem=recv, device_id=peer, device_id_type=MESH
    )
    copy.start()
    return copy


def remote_call(kernel, collective_id, operands, out_shape, in_specs, out_specs, scratch):
    return pl.pallas_call(
        kernel,
        out_shape=out_shape,
        in_specs=in_specs,
        out_specs=out_specs,
        scratch_shapes=scratch,
        compiler_params=pltpu.CompilerParams(
            collective_id=collective_id, has_side_effects=True, vmem_limit_bytes=56 * 2**20
        ),
    )(*operands)


def spread_axes(w_ref, sems, cols):
    x, y, z, c = here()
    near_s, near_r, far_s, far_r = sems
    first, second = pl.ds(0, cols // 2), pl.ds(cols // 2, cols // 2)
    sent = []
    for d in range(1, 4):
        block = w_ref.at[x, y, :, first]
        sent.append(
            push(block, block, near_s.at[0, d - 1], near_r.at[0, d - 1], (x, wrap(y + d), z, c))
        )
        block = w_ref.at[x, y, :, second]
        sent.append(
            push(block, block, near_s.at[1, d - 1], near_r.at[1, d - 1], (wrap(x + d), y, z, c))
        )
    for k in range(4):
        row, col = wrap(x - k), wrap(y - k)
        one = w_ref.at[x, col, :, first]
        two = w_ref.at[row, y, :, second]
        if k > 0:
            sent[2 * (k - 1)].wait_recv()
            sent[2 * (k - 1) + 1].wait_recv()
        for d in range(1, 4):
            sent.append(
                push(one, one, far_s.at[0, k, d - 1], far_r.at[0, k, d - 1], (wrap(x + d), y, z, c))
            )
            sent.append(
                push(two, two, far_s.at[1, k, d - 1], far_r.at[1, k, d - 1], (x, wrap(y + d), z, c))
            )
    return sent


def spread_sems():
    return [DMA((2, 3)), DMA((2, 3)), DMA((2, 4, 3)), DMA((2, 4, 3))]


def rows_start(src, out, sems):
    x, y, z, c = here()
    hop_s, hop_r, pair_s, pair_r, own = sems
    mine = pltpu.make_async_copy(src, out.at[c, z], own)
    mine.start()
    hops = [
        push(src, out.at[c, z], hop_s.at[d - 1], hop_r.at[d - 1], (x, y, wrap(z + d), c))
        for d in range(1, 4)
    ]
    pairs = [push(src, out.at[c, z], pair_s.at[0], pair_r.at[0], (x, y, z, 1 - c))]
    return mine, hops, pairs


def rows_finish(started, out, sems):
    x, y, z, c = here()
    hop_s, hop_r, pair_s, pair_r, own = sems
    mine, hops, pairs = started
    for d in range(1, 4):
        hops[d - 1].wait_recv()
        block = out.at[c, wrap(z - d)]
        pairs.append(push(block, block, pair_s.at[d], pair_r.at[d], (x, y, z, 1 - c)))
    mine.wait()
    for copy in hops:
        copy.wait_send()
    for copy in pairs:
        copy.wait()


def rows_sems():
    return [DMA((3,)), DMA((3,)), DMA((4,)), DMA((4,)), DMA(())]


def group_peers():
    x, y, z, c = here()
    return [(x, y, wrap(z + d), k) for d in range(1, 4) for k in range(2)] + [(x, y, z, 1 - c)]


def row_peers():
    x, y, z, c = here()
    return [(x, y, wrap(z + d), c) for d in range(1, 4)] + [(x, y, z, 1 - c)]


def plane_peers():
    x, y, z, c = here()
    return [(wrap(x + d), y, z, c) for d in range(1, 4)] + [
        (x, wrap(y + d), z, c) for d in range(1, 4)
    ]


def gather_kernel(wm, wf, rows_a, rows_b, wide_m, wide_f, all_a, all_b, *sems):
    x, y, z, c = here()
    a_sems, b_sems, m_sems, f_sems = sems[0:5], sems[5:10], sems[10:14], sems[14:18]
    m_send, m_recv, f_send, f_recv, f_own = sems[18:23]
    greet(group_peers() + plane_peers())
    m_sent = []
    for j in range(2):
        for k in range(2):
            to = 2 * c + j
            dst = wide_m.at[x, y, pl.ds(z * 32, 32), :]
            same = jnp.logical_and(to == z, c == k)
            copy = pltpu.make_async_remote_copy(
                src_ref=wm.at[j, k],
                dst_ref=dst,
                send_sem=m_send.at[j, k],
                recv_sem=m_recv.at[z],
                device_id=(x, y, to, k),
                device_id_type=MESH,
            )

            @pl.when(same)
            def _():
                pltpu.make_async_copy(wm.at[j, k], dst, m_recv.at[z]).start()

            @pl.when(jnp.logical_not(same))
            def _():
                copy.start()

            m_sent.append((same, copy))
    f_mine = pltpu.make_async_copy(wf.at[z], wide_f.at[x, y, pl.ds(z * 32, 32), :], f_own)
    f_mine.start()
    f_sent = [
        push(
            wf.at[wrap(z + d)],
            wide_f.at[x, y, pl.ds(z * 32, 32), :],
            f_send.at[d - 1],
            f_recv.at[d - 1],
            (x, y, wrap(z + d), c),
        )
        for d in range(1, 4)
    ]
    a_started = rows_start(rows_a, all_a, a_sems)
    for s in range(4):
        dst = wide_m.at[x, y, pl.ds(s * 32, 32), :]
        pltpu.make_async_copy(wm.at[0, 0], dst, m_recv.at[s]).wait()
    m_spread = spread_axes(wide_m, m_sems, MIX)
    f_mine.wait()
    for copy in f_sent:
        copy.wait_recv()
    b_started = rows_start(rows_b, all_b, b_sems)
    f_spread = spread_axes(wide_f, f_sems, FFN)
    rows_finish(a_started, all_a, a_sems)
    rows_finish(b_started, all_b, b_sems)
    for same, copy in m_sent:

        @pl.when(jnp.logical_not(same))
        def _():
            copy.wait_send()

    for copy in f_sent:
        copy.wait_send()
    for spread in (m_spread, f_spread):
        for copy in spread[:6]:
            copy.wait_send()
        for copy in spread[6:]:
            copy.wait()


def gather_all(wm, wf, rows_a, rows_b, collective_id):
    return remote_call(
        gather_kernel,
        collective_id,
        (wm, wf, rows_a, rows_b),
        [
            jax.ShapeDtypeStruct((4, 4, 128, MIX), BF),
            jax.ShapeDtypeStruct((4, 4, 128, FFN), BF),
            jax.ShapeDtypeStruct((2, 4, 64, 2048), BF),
            jax.ShapeDtypeStruct((2, 4, 64, 2048), BF),
        ],
        [ANY] * 4,
        [ANY] * 4,
        rows_sems()
        + rows_sems()
        + spread_sems()
        + spread_sems()
        + [DMA((2, 2)), DMA((4,)), DMA((3,)), DMA((3,)), DMA(())],
    )


def rows_kernel(src, out, *sems):
    greet(row_peers())
    rows_finish(rows_start(src, out, sems), out, sems)


def gather_rows(rows, collective_id):
    return remote_call(
        rows_kernel,
        collective_id,
        (rows,),
        jax.ShapeDtypeStruct((2, 4, 64, 2048), BF),
        [ANY],
        ANY,
        rows_sems(),
    ).reshape(512, 2048)


def sum_rows_kernel(count, *refs):
    parts, outs = refs[:count], refs[count : 2 * count]
    theirs, sending, landed, pair_s, pair_r, hop_s, hop_r = refs[2 * count :]
    x, y, z, c = here()
    greet(row_peers())
    pairs = []
    for n in range(count):
        for k in range(4):
            to = wrap(z + 1 + k)
            pairs.append(
                push(
                    parts[n].at[1 - c, to],
                    theirs.at[n, k],
                    pair_s.at[n, k],
                    pair_r.at[n, k],
                    (x, y, z, 1 - c),
                )
            )
    hops = []
    for n in range(count):
        for k in range(3):
            to = wrap(z + 1 + k)
            pairs[4 * n + k].wait_recv()
            both = parts[n][c, to].astype(F32) + theirs[n, k].astype(F32)
            sending[n, k] = both.astype(BF)
            hops.append(
                push(sending.at[n, k], landed.at[n, k], hop_s.at[n, k], hop_r.at[n, k], (x, y, to, c))
            )
    for n in range(count):
        pairs[4 * n + 3].wait_recv()
        outs[n][...] = parts[n][c, z].astype(F32) + theirs[n, 3].astype(F32)
    for n in range(count):
        for k in range(3):
            hops[3 * n + k].wait_recv()
            outs[n][...] += landed[n, k].astype(F32)
    for copy in pairs + hops:
        copy.wait_send()


def sum_rows(parts, collective_id):
    count = len(parts)
    return remote_call(
        functools.partial(sum_rows_kernel, count),
        collective_id,
        [part.astype(BF).reshape(2, 4, 64, 2048) for part in parts],
        [jax.ShapeDtypeStruct((64, 2048), F32)] * count,
        [VMEM] * count,
        [VMEM] * count,
        [
            pltpu.VMEM((count, 4, 64, 2048), BF),
            pltpu.VMEM((count, 3, 64, 2048), BF),
            pltpu.VMEM((count, 3, 64, 2048), BF),
            DMA((count, 4)),
            DMA((count, 4)),
            DMA((count, 3)),
            DMA((count, 3)),
        ],
    )


def swap_kernel(src, out, own, send, recv):
    x, y, z, c = here()
    greet([(x, y, z, 1 - c)])
    copy = push(src.at[1 - c], out.at[c], send, recv, (x, y, z, 1 - c))
    mine = pltpu.make_async_copy(src.at[c], out.at[c], own)
    mine.start()
    mine.wait()
    copy.wait()


def swap(value, collective_id):
    return remote_call(
        swap_kernel,
        collective_id,
        (value,),
        jax.ShapeDtypeStruct(value.shape, value.dtype),
        [ANY],
        ANY,
        [DMA(()), DMA(()), DMA(())],
    )


def scan_kernel(
    back, ends, out, every, total, sending, landed, entry, own, pair_s, pair_r, far_s, far_r, last_s, last_r
):
    x, y, z, c = here()
    group = x * 4 + y
    sign = -1 if back else 1

    def member(d):
        at = lax.rem(group + sign * d + 32, 16)
        return (at // 4, lax.rem(at, 4), z, c)

    partner = (x, y, z, 1 - c)
    barrier = pltpu.get_barrier_semaphore()
    pl.semaphore_signal(barrier, inc=1, device_id=partner, device_id_type=MESH)
    for d in range(1, REACH + 1):
        pl.semaphore_signal(barrier, inc=1, device_id=member(-d), device_id_type=MESH)
    pl.semaphore_wait(barrier, REACH + 1)
    pair = push(ends, every.at[c], pair_s, pair_r, partner)
    mine = pltpu.make_async_copy(ends, every.at[c], own)
    mine.start()
    mine.wait()
    pair.wait()
    half = pl.ds(pl.multiple_of(c * DK, DK), DK)
    order = [(n, k) for n in range(4) for k in range(2)]
    if back:
        order = order[::-1]

    def factor(k, n, width):
        return jnp.concatenate([every[k, n, :, 1024:1152]] * (width // 128), axis=1)

    n, k = (order[0][0], order[0][1])
    state = every[k, n, :, half]
    decay = every[k, n, :, 1024:1152]
    for n, k in order[1:]:
        state = factor(k, n, DK) * state + every[k, n, :, half]
        decay = every[k, n, :, 1024:1152] * decay
    sending[:, 0:512] = state.astype(BF)
    high = decay.astype(BF)
    sending[:, 512:640] = high
    sending[:, 640:768] = (decay - high.astype(F32)).astype(BF)
    far = [
        push(sending, landed.at[d - 1], far_s.at[d - 1], far_r.at[d - 1], member(d))
        for d in range(1, REACH + 1)
    ]
    total[...] = jnp.zeros_like(total)
    for d in range(REACH, 0, -1):
        far[d - 1].wait_recv()
        valid = (group + d < 16) if back else (group >= d)
        keep = landed[d - 1, :, 512:640].astype(F32) + landed[d - 1, :, 640:768].astype(F32)
        keep = jnp.concatenate([keep] * 4, axis=1)
        fresh = keep * total[...] + landed[d - 1, :, 0:512].astype(F32)
        total[...] = jnp.where(valid, fresh, 0.0)
    entry[c] = total[...]
    last = push(total, entry.at[c], last_s, last_r, partner)
    last.wait()
    for s in range(2):
        state = entry[s]
        cols = pl.ds(s * DK, DK)
        for n, k in order:

            @pl.when(c == k)
            def _():
                out[n, :, cols] = state

            state = factor(k, n, DK) * state + every[k, n, :, cols]
    for copy in far:
        copy.wait_send()


def scan_states(ends, back, collective_id):
    return remote_call(
        functools.partial(scan_kernel, back),
        collective_id,
        (ends,),
        jax.ShapeDtypeStruct((4, SLOTS, 1024), F32),
        [ANY],
        VMEM,
        [
            pltpu.VMEM((2, 4, SLOTS, 1152), F32),
            pltpu.VMEM((SLOTS, DK), F32),
            pltpu.VMEM((SLOTS, 768), BF),
            pltpu.VMEM((REACH, SLOTS, 768), BF),
            pltpu.VMEM((2, SLOTS, DK), F32),
            DMA(()),
            DMA(()),
            DMA(()),
            DMA((REACH,)),
            DMA((REACH,)),
            DMA(()),
            DMA(()),
        ],
    )


def tri(lower):
    row = lax.broadcasted_iota(jnp.int32, (CHUNK, CHUNK), 0)
    col = lax.broadcasted_iota(jnp.int32, (CHUNK, CHUNK), 1)
    return ((row >= col) if lower else (row <= col)).astype(F32)


def seen_mask(offs):
    row = lax.broadcasted_iota(jnp.int32, (CHUNK, CHUNK), 0)
    col = lax.broadcasted_iota(jnp.int32, (CHUNK, CHUNK), 1)
    return jnp.logical_and(row >= col, offs >= row - col)


def features(ref, which):
    cols = pl.ds(which * HALF, HALF)
    return jnp.concatenate([ref[0, 0, :, cols], ref[1, 0, :, cols]], axis=1)


def tiles(value):
    return [value[8 * b : 8 * b + 8] for b in range(CHUNK // 8)]


def one_row(blocks, i):
    return blocks[i // 8][i % 8 : i % 8 + 1]


def spans(cum, i):
    last = one_row(cum, i)
    return [(b, jnp.exp(jnp.minimum(cum[b] - last, 0.0))) for b in range(i // 8, CHUNK // 8)]


def weigh(cum, write, columns):
    cum, write, cols = tiles(cum), tiles(write), tiles(columns)
    total = [jnp.zeros((8, SLOTS), F32) for _ in range(CHUNK // 8)]
    for i in range(CHUNK):
        scale = one_row(write, i)
        for b, span in spans(cum, i):
            total[b] = total[b] + cols[b][:, i : i + 1] * (span * scale)
    return jnp.concatenate(total, axis=0)


def weigh_slots(cum, write, values):
    cum, write, vals = tiles(cum), tiles(write), tiles(values)
    lane = lax.broadcasted_iota(jnp.int32, (8, CHUNK), 1)
    total = [jnp.zeros((8, CHUNK), F32) for _ in range(CHUNK // 8)]
    for i in range(CHUNK):
        scale = one_row(write, i)
        for b, span in spans(cum, i):
            got = jnp.sum(vals[b] * (span * scale), axis=1, keepdims=True)
            total[b] = jnp.where(lane == i, got, total[b])
    return jnp.concatenate(total, axis=0)


def ends_kernel(qkv, lam, write, offs, ends, cum_ref, near_ref):
    query, key, value = (features(qkv, n) for n in range(3))
    decay = lam[0]
    cum = dot(tri(True), decay, precision=HIGH)
    cum_ref[0] = cum
    offsets = offs[0]
    final = offsets[CHUNK - 1 : CHUNK, :]
    row = lax.broadcasted_iota(jnp.int32, (CHUNK, 1), 0)
    tail = (row >= CHUNK - 1 - final).astype(F32)
    ending = jnp.exp(cum[CHUNK - 1 : CHUNK] - cum) * write[0] * tail
    ending = ending.astype(BF)
    ends[0, :, 0:512] = tn(ending, key)
    ends[0, :, 512:1024] = tn(ending, value)
    keep = (final > CHUNK - 1).astype(F32)
    ends[0, :, 1024:1152] = keep * jnp.exp(tn(decay, jnp.ones((CHUNK, 128), F32), HIGH))
    affinity = jnp.where(seen_mask(offsets), nt(query, key) * SCALE, 0.0)
    near_ref[0] = weigh(cum, write[0], affinity)


def out_kernel(qkv, cum_ref, write, offs, near, states, mixed, probs_ref, mixing_ref, far_ref):
    query, _, value = (features(qkv, n) for n in range(3))
    cum, offsets = cum_ref[0], offs[0]
    row = lax.broadcasted_iota(jnp.int32, (CHUNK, 1), 0)
    carry = jnp.exp(cum) * (offsets > row).astype(F32)
    far = nt(query, states[0, :, 0:512].astype(BF)) * SCALE
    far_ref[0] = far
    scores = near[0] + carry * far
    scores = jnp.exp(scores - jnp.max(scores, axis=1, keepdims=True))
    probs = scores / jnp.sum(scores, axis=1, keepdims=True)
    probs_ref[0] = probs
    mixing = jnp.where(seen_mask(offsets), weigh_slots(cum, write[0], probs), 0.0)
    mixing_ref[0] = mixing
    mixed[0] = dot(mixing.astype(BF), value) + dot(
        (probs * carry).astype(BF), states[0, :, 512:1024].astype(BF)
    )


def back_kernel(
    qkv, grad, cum_ref, write, offs, states, probs_ref, far_ref, decay_in, dmix_ref, dscore_ref, dprob_ref, dfar_ref, ends
):
    query, _, value = (features(qkv, n) for n in range(3))
    g, cum, offsets, probs = grad[0], cum_ref[0], offs[0], probs_ref[0]
    row = lax.broadcasted_iota(jnp.int32, (CHUNK, 1), 0)
    carry = jnp.exp(cum) * (offsets > row).astype(F32)
    dmix = jnp.where(seen_mask(offsets), nt(g, value), 0.0)
    dmix_ref[0] = dmix
    dcarry = nt(g, states[0, :, 512:1024].astype(BF))
    dnear = weigh(cum, write[0], dmix)
    dprob_ref[0] = dnear
    dfar_ref[0] = dcarry
    dprobs = dnear + carry * dcarry
    dscores = probs * (dprobs - jnp.sum(probs * dprobs, axis=1, keepdims=True))
    dscore_ref[0] = dscores
    ends[0, :, 0:512] = tn((SCALE * dscores * carry).astype(BF), query)
    ends[0, :, 512:1024] = tn((probs * carry).astype(BF), g)
    ends[0, :, 1024:1152] = decay_in[0, :, 1024:1152]


def last_kernel(
    qkv, grad, lam, cum_ref, write, slope, offs, states, near, probs_ref, mixing, far, dmix, dscore, dprob, dfar, nexts, dqkv, dlogit
):
    query, key, value = (features(qkv, n) for n in range(3))
    g, cum, offsets, probs, dscores = grad[0], cum_ref[0], offs[0], probs_ref[0], dscore[0]
    row = lax.broadcasted_iota(jnp.int32, (CHUNK, 1), 0)
    carry = jnp.exp(cum) * (offsets > row).astype(F32)
    seen = seen_mask(offsets)
    affinity = jnp.where(seen, nt(query, key) * SCALE, 0.0)
    cums, writes = tiles(cum), tiles(write[0])
    aff, dmx, dsc, prb = tiles(affinity), tiles(dmix[0]), tiles(dscores), tiles(probs)
    lane = lax.broadcasted_iota(jnp.int32, (8, CHUNK), 1)
    daff = [jnp.zeros((8, CHUNK), F32) for _ in range(CHUNK // 8)]
    fresh = []
    for i in range(CHUNK):
        scale = one_row(writes, i)
        gather = jnp.zeros((8, SLOTS), F32)
        for b, span in spans(cums, i):
            got = jnp.sum(dsc[b] * (span * scale), axis=1, keepdims=True)
            daff[b] = jnp.where(lane == i, got, daff[b])
            gather = gather + (dsc[b] * aff[b][:, i : i + 1] + prb[b] * dmx[b][:, i : i + 1]) * span
        fresh.append(jnp.sum(gather, axis=0, keepdims=True))
    fresh = jnp.concatenate(fresh, axis=0)
    daff = jnp.where(seen, jnp.concatenate(daff, axis=0) * SCALE, 0.0).astype(BF)
    final = offsets[CHUNK - 1 : CHUNK, :]
    tail = (row >= CHUNK - 1 - final).astype(F32)
    reach = jnp.exp(cum[CHUNK - 1 : CHUNK] - cum) * tail
    ending = (reach * write[0]).astype(BF)
    next_k, next_v = nexts[0, :, 0:512], nexts[0, :, 512:1024]
    state_k, state_v = states[0, :, 0:512], states[0, :, 512:1024]
    nk, nv = next_k.astype(BF), next_v.astype(BF)
    dq = dot(daff, key) + dot((SCALE * dscores * carry).astype(BF), state_k.astype(BF))
    dk = tn(daff, query) + dot(ending, nk)
    dv = tn(mixing[0].astype(BF), g) + dot(ending, nv)
    for n, part in enumerate((dq, dk, dv)):
        for s in range(2):
            dqkv[s, 0, :, pl.ds(n * HALF, HALF)] = part[:, s * HALF : (s + 1) * HALF].astype(BF)
    dend = (nt(key, nk) + nt(value, nv)) * reach
    ones = jnp.ones((8, DK), F32)
    dkeep = nt(ones, next_k * state_k + next_v * state_v, HIGH)[0:1]
    keep = (final > CHUNK - 1).astype(F32) * jnp.exp(cum[CHUNK - 1 : CHUNK])
    scaled = write[0] * dend
    dcum = (
        dscores * near[0]
        + probs * dprob[0]
        + carry * (dscores * far[0] + probs * dfar[0])
        - write[0] * fresh
        - scaled
    )
    at_end = jnp.sum(scaled, axis=0, keepdims=True) + dkeep * keep
    dcum = dcum + jnp.where(row == CHUNK - 1, at_end, 0.0)
    dlam = dot(tri(False), dcum, precision=HIGH) - jnp.exp(lam[0]) * (fresh + dend)
    dlogit[0] = dlam * slope[0]


def chunk_call(kernel, operands, outs, flops=0):
    def spec(shape, paired):
        if paired:
            return pl.BlockSpec((2, 1) + tuple(shape[2:]), lambda n: (0, n, 0, 0))
        return pl.BlockSpec((1,) + tuple(shape[1:]), lambda n: (n, 0, 0))

    return pl.pallas_call(
        kernel,
        grid=(4,),
        out_shape=[jax.ShapeDtypeStruct(shape, dtype) for shape, dtype in outs],
        in_specs=[spec(v.shape, v.ndim == 4) for v in operands],
        out_specs=[spec(shape, len(shape) == 4) for shape, _ in outs],
        compiler_params=pltpu.CompilerParams(vmem_limit_bytes=48 * 2**20),
    )(*operands)


def scatter_kernel(
    cols, grads, out_m, out_f, own, far, near, landed, ready, total, own_s, far_s, far_r, near_s, near_r, m_send, m_recv, f_send, f_recv, f_own
):
    x, y, z, c = here()
    half = cols // 2
    parts = (pl.ds(0, half), pl.ds(half, half))
    greet(group_peers() + plane_peers())
    order = (1, 2, 3, 0)

    def block(side, k, d):
        if side == 0:
            return grads.at[wrap(x + d), wrap(y + k), :, parts[0]]
        return grads.at[wrap(x + k), wrap(y + d), :, parts[1]]

    def peer(side, d):
        return (wrap(x + d), y, z, c) if side == 0 else (x, wrap(y + d), z, c)

    fars, owns = {}, {}
    for k in order:
        for side in range(2):
            owns[side, k] = pltpu.make_async_copy(
                block(side, k, 0), own.at[side, k], own_s.at[side, k]
            )
            owns[side, k].start()
            for d in range(1, 4):
                fars[side, k, d] = push(
                    block(side, k, d),
                    far.at[side, k, d - 1],
                    far_s.at[side, k, d - 1],
                    far_r.at[side, k, d - 1],
                    peer(side, d),
                )
    nears = {}
    for k in order:
        for side in range(2):
            owns[side, k].wait()
            for d in range(1, 4):
                fars[side, k, d].wait_recv()

            @pl.loop(0, 8)
            def _(r):
                rows = pl.ds(pl.multiple_of(r * 16, 16), 16)
                value = own[side, k, rows, :].astype(F32)
                for d in range(3):
                    value = value + far[side, k, d, rows, :].astype(F32)
                if k > 0:
                    near[side, k - 1, rows, :] = value.astype(BF)
                else:
                    total[side, rows, :] = value

            if k > 0:
                nears[side, k] = push(
                    near.at[side, k - 1],
                    landed.at[side, k - 1],
                    near_s.at[side, k - 1],
                    near_r.at[side, k - 1],
                    peer(1 - side, k),
                )
    for side in range(2):
        for k in range(1, 4):
            nears[side, k].wait_recv()

        @pl.loop(0, 8)
        def _(r):
            rows = pl.ds(pl.multiple_of(r * 16, 16), 16)
            value = total[side, rows, :]
            for k in range(3):
                value = value + landed[side, k, rows, :].astype(F32)
            ready[rows, parts[side]] = value.astype(BF)

    m_sent = []
    for to in range(4):
        src = ready.at[pl.ds(to * 32, 32), pl.ds(0, MIX)]
        dst = out_m.at[lax.rem(z, 2), c]
        same = jnp.logical_and(to == z, c == z // 2)
        copy = pltpu.make_async_remote_copy(
            src_ref=src,
            dst_ref=dst,
            send_sem=m_send.at[to],
            recv_sem=m_recv.at[lax.rem(z, 2), c],
            device_id=(x, y, to, z // 2),
            device_id_type=MESH,
        )

        @pl.when(same)
        def _():
            pltpu.make_async_copy(src, dst, m_recv.at[lax.rem(z, 2), c]).start()

        @pl.when(jnp.logical_not(same))
        def _():
            copy.start()

        m_sent.append((same, copy))

    def ffn_rows(to):
        return ready.at[pl.ds(pl.multiple_of(to * 32, 32), 32), pl.ds(MIX, FFN)]

    f_mine = pltpu.make_async_copy(ffn_rows(z), out_f.at[z], f_own)
    f_mine.start()
    f_sent = [
        push(
            ffn_rows(wrap(z + d)),
            out_f.at[z],
            f_send.at[d - 1],
            f_recv.at[d - 1],
            (x, y, wrap(z + d), c),
        )
        for d in range(1, 4)
    ]
    for j in range(2):
        for k in range(2):
            pltpu.make_async_copy(
                ready.at[pl.ds(0, 32), pl.ds(0, MIX)], out_m.at[j, k], m_recv.at[j, k]
            ).wait()
    f_mine.wait()
    for copy in f_sent:
        copy.wait()
    for same, copy in m_sent:

        @pl.when(jnp.logical_not(same))
        def _():
            copy.wait_send()

    for copy in list(fars.values()) + list(nears.values()):
        copy.wait_send()


def scatter_all(grads, collective_id):
    cols = grads.shape[1]
    half = cols // 2
    return remote_call(
        functools.partial(scatter_kernel, cols),
        collective_id,
        (grads.reshape(4, 4, 128, cols),),
        [jax.ShapeDtypeStruct((2, 2, 32, MIX), BF), jax.ShapeDtypeStruct((4, 32, FFN), BF)],
        [ANY],
        [ANY, ANY],
        [
            pltpu.VMEM((2, 4, 128, half), BF),
            pltpu.VMEM((2, 4, 3, 128, half), BF),
            pltpu.VMEM((2, 3, 128, half), BF),
            pltpu.VMEM((2, 3, 128, half), BF),
            pltpu.VMEM((128, cols), BF),
            pltpu.VMEM((2, 128, half), F32),
            DMA((2, 4)),
            DMA((2, 4, 3)),
            DMA((2, 4, 3)),
            DMA((2, 3)),
            DMA((2, 3)),
            DMA((4,)),
            DMA((2, 2)),
            DMA((3,)),
            DMA((3,)),
            DMA(()),
        ],
    )


def small_kernel(src, out, held, here_s, own_s, send, recv, pair_s, pair_r):
    x, y, z, c = here()
    rows = src.shape[0] // 2
    partner = (x, y, z, 1 - c)
    greet(plane_peers() + row_peers())

    def half(k):
        return pl.ds(pl.multiple_of(k * rows, 8), rows)

    copy = push(src.at[half(1 - c)], held.at[0, c], pair_s.at[0], pair_r.at[0], partner)
    mine = pltpu.make_async_copy(src.at[half(c)], held.at[0, c], own_s)
    mine.start()
    mine.wait()
    copy.wait()
    here_s[...] = held[0, 0] + held[0, 1]
    for stage, at in enumerate((x, y, z)):
        held[stage + 1, at] = here_s[...]
        sent = []
        for d in range(1, 4):
            peer = [x, y, z, c]
            peer[stage] = wrap(at + d)
            sent.append(
                push(
                    held.at[stage + 1, at],
                    held.at[stage + 1, at],
                    send.at[stage, d - 1],
                    recv.at[stage, d - 1],
                    tuple(peer),
                )
            )
        for copy in sent:
            copy.wait()
        value = held[stage + 1, 0]
        for k in range(1, 4):
            value = value + held[stage + 1, k]
        here_s[...] = value
    copy = push(here_s, out.at[half(c)], pair_s.at[1], pair_r.at[1], partner)
    out[half(c)] = here_s[...]
    copy.wait()


def small_sum(values, collective_id):
    flat = jnp.concatenate([v.reshape(-1) for v in values])
    size = flat.shape[0]
    rows = -(-size // 2048) * 16
    flat = jnp.pad(flat, (0, rows * 128 - size)).reshape(rows, 128)
    flat = remote_call(
        small_kernel,
        collective_id,
        (flat,),
        jax.ShapeDtypeStruct((rows, 128), F32),
        [VMEM],
        VMEM,
        [
            pltpu.VMEM((4, 4, rows // 2, 128), F32),
            pltpu.VMEM((rows // 2, 128), F32),
            DMA(()),
            DMA((3, 3)),
            DMA((3, 3)),
            DMA((2,)),
            DMA((2,)),
        ],
    ).reshape(-1)
    outs, at = [], 0
    for v in values:
        outs.append(flat[at : at + v.size].reshape(v.shape))
        at += v.size
    return outs


def rms(v, gain):
    return v * lax.rsqrt(jnp.mean(v * v, axis=-1, keepdims=True) + EPS) * gain


def rms_back(v, gain, e):
    r = lax.rsqrt(jnp.mean(v * v, axis=-1, keepdims=True) + EPS)
    grad = r * gain * e - v * (r**3) * jnp.mean(v * gain * e, axis=-1, keepdims=True)
    return grad, jnp.sum(e * v * r, axis=0)


def body(
    inputs,
    offsets,
    norm1_gain,
    query_weight,
    key_weight,
    value_weight,
    gate_weight,
    out_weight,
    low_down,
    low_up,
    forget_bias,
    head_gain,
    norm2_gain,
    ffn_gate,
    ffn_up,
    ffn_down,
    cotangent,
):
    head, core = lax.axis_index("z"), lax.axis_index("c")
    mixer = (query_weight, key_weight, value_weight, gate_weight, out_weight.T)
    wm = jnp.stack([w.reshape(32, 2, 2, HALF) for w in mixer], axis=3)
    wm = wm.transpose(1, 2, 0, 3, 4).reshape(2, 2, 32, MIX)
    wf = jnp.stack([w.reshape(32, 4, UNITS) for w in (ffn_gate, ffn_up, ffn_down)], axis=2)
    wf = jnp.pad(wf, ((0, 0), (0, 0), (0, 0), (0, UNITS_PAD - UNITS)))
    wf = wf.transpose(1, 0, 2, 3).reshape(4, 32, FFN)
    resid = inputs.astype(F32)
    first_own = rms(resid, norm1_gain).astype(BF)
    wide_m, wide_f, first, cot = gather_all(wm, wf, first_own, cotangent, 1)
    wide_m, wide_f = wide_m.reshape(2048, MIX), wide_f.reshape(2048, FFN)
    tokens = first
    first, cot = first.reshape(512, 2048), cot.reshape(512, 2048)
    w_qkvg, w_out = wide_m[:, : 4 * HALF], wide_m[:, 4 * HALF :]
    w_gate, w_up, w_down = (wide_f[:, n * UNITS_PAD : (n + 1) * UNITS_PAD] for n in range(3))

    qkv = dot(first, wide_m[:, : 3 * HALF]).astype(BF)
    gate_lin = dot(first, wide_m[:, 3 * HALF : 4 * HALF])
    qkv = swap(qkv.reshape(2, 4, 64, 3 * HALF), 2)
    mine = lax.dynamic_index_in_dim(tokens, core, 0, keepdims=False).reshape(256, 2048)
    up_cols = lax.dynamic_slice_in_dim(low_up.astype(F32), head * SLOTS, SLOTS, 1)
    bias = lax.dynamic_slice_in_dim(forget_bias, head * SLOTS, SLOTS, 0)
    lowrank = dot(mine, low_down)
    logits = (dot(lowrank, up_cols, precision=HIGH) + bias).astype(BF).astype(F32)
    lam = (jax.nn.log_sigmoid(logits) / 8.0).reshape(4, 64, SLOTS)
    write = -jnp.expm1(lam)
    slope = (jax.nn.sigmoid(-logits) / 8.0).reshape(4, 64, SLOTS)
    pair = lax.all_gather(offsets.reshape(2, 64), "z")
    offs = lax.dynamic_index_in_dim(pair, core, 1, keepdims=False).reshape(4, 64, 1)

    square = ((4, 64, 64), F32)
    ends, cum, near = chunk_call(
        ends_kernel, (qkv, lam, write, offs), [((4, SLOTS, 1152), F32), square, square]
    )
    states = scan_states(ends, False, 3)
    mixed, probs, mixing, far = chunk_call(
        out_kernel,
        (qkv, cum, write, offs, near, states),
        [((4, 64, DK), F32), square, square, square],
    )
    mixed = mixed.reshape(256, DK)
    headnorm = rms(mixed, head_gain).reshape(4, 64, 2, HALF).transpose(2, 0, 1, 3)
    headnorm = swap(headnorm, 4).reshape(512, HALF)
    branch = (headnorm * jax.nn.silu(gate_lin)).astype(BF)
    (mixer_out,) = sum_rows([nt(branch, w_out)], 5)
    resid1 = resid + mixer_out
    second_own = rms(resid1, norm2_gain).astype(BF)
    second = gather_rows(second_own, 6)

    act_gate, act_up = dot(second, w_gate), dot(second, w_up)
    sig = jax.nn.sigmoid(act_gate)
    silu = act_gate * sig
    hidden = (silu * act_up).astype(BF)
    grad_hidden = dot(cot, w_down)
    grad_gate = (grad_hidden * act_up * sig * (1 + act_gate * (1 - sig))).astype(BF)
    grad_up = (grad_hidden * silu).astype(BF)
    ffn_part = nt(hidden, w_down)
    second_part = nt(grad_gate, w_gate) + nt(grad_up, w_up)
    ffn_out, grad_second = sum_rows([ffn_part, second_part], 7)
    output = (resid1 + ffn_out).astype(BF)
    grad_norm, d_norm2 = rms_back(resid1, norm2_gain, grad_second)
    grad_resid1 = cotangent.astype(F32) + grad_norm
    grad_attn = gather_rows(grad_resid1.astype(BF), 8)

    grad_branch = dot(grad_attn, w_out)
    sig = jax.nn.sigmoid(gate_lin)
    grad_lin = (grad_branch * headnorm * sig * (1 + gate_lin * (1 - sig))).astype(BF)
    grad_headnorm = (grad_branch * gate_lin * sig).reshape(2, 4, 64, HALF)
    grad_headnorm = swap(grad_headnorm, 9).transpose(1, 2, 0, 3).reshape(256, DK)
    grad_mixed, d_head = rms_back(mixed, head_gain, grad_headnorm)
    grad_mixed = grad_mixed.astype(BF).reshape(4, 64, DK)

    dmix, dscore, dprob, dfar, back_ends = chunk_call(
        back_kernel,
        (qkv, grad_mixed, cum, write, offs, states, probs, far, ends),
        [square, square, square, square, ((4, SLOTS, 1152), F32)],
    )
    nexts = scan_states(back_ends, True, 10)
    dqkv, dlogit = chunk_call(
        last_kernel,
        (qkv, grad_mixed, lam, cum, write, slope, offs, states, near, probs, mixing, far, dmix, dscore, dprob, dfar, nexts),
        [((2, 4, 64, 3 * HALF), BF), square],
    )
    dqkv = swap(dqkv, 11).reshape(512, 3 * HALF)
    dlogit = dlogit.reshape(256, SLOTS)
    grad_low = dot(dlogit, up_cols.T, precision=HIGH)
    dproj = jnp.concatenate([dqkv, grad_lin], axis=1)
    first_part = nt(dproj, w_qkvg).reshape(2, 256, 2048)
    low_part = nt(grad_low, low_down.astype(F32), precision=HIGH)
    own = (jnp.arange(2) == core).astype(F32)[:, None, None]
    first_part = (first_part + own * low_part[None]).reshape(512, 2048)
    (grad_first,) = sum_rows([first_part], 12)
    grad_in, d_norm1 = rms_back(resid, norm1_gain, grad_first)
    d_inputs = grad_resid1 + grad_in

    grads = jnp.concatenate(
        [
            tn(first, dproj).astype(BF),
            tn(grad_attn, branch).astype(BF),
            tn(second, grad_gate).astype(BF),
            tn(second, grad_up).astype(BF),
            tn(cot, hidden).astype(BF),
        ],
        axis=1,
    )
    sums_m, sums_f = scatter_all(grads, 13)
    sums_m = sums_m.reshape(2, 2, 32, 5, HALF).transpose(3, 2, 0, 1, 4).reshape(5, 32, 1024)
    sums_m = sums_m.astype(F32)
    sums_f = sums_f.reshape(4, 32, 3, UNITS_PAD)[..., :UNITS].transpose(2, 1, 0, 3)
    sums_f = sums_f.reshape(3, 32, 4 * UNITS).astype(F32)

    d_up = jnp.zeros(low_up.shape, F32)
    d_up = lax.dynamic_update_slice_in_dim(d_up, tn(lowrank, dlogit, HIGH), head * SLOTS, 1)
    d_bias = jnp.zeros(forget_bias.shape, F32)
    d_bias = lax.dynamic_update_slice_in_dim(d_bias, jnp.sum(dlogit, axis=0), head * SLOTS, 0)
    d_down = tn(grad_low, mine.astype(F32), HIGH)
    small = small_sum([d_norm1, d_norm2, d_head, d_down, d_up, d_bias], 14)
    return (
        output,
        d_inputs,
        small[0],
        sums_m[0],
        sums_m[1],
        sums_m[2],
        sums_m[3],
        sums_m[4].T,
        small[3].T,
        small[4],
        small[5],
        small[2],
        small[1],
        sums_f[0],
        sums_f[1],
        sums_f[2],
    )


def solution(mesh):
    fine = Mesh(mesh.devices.reshape(4, 4, 4, 2), ("x", "y", "z", "c"))
    seq = ("x", "y", "z")
    rows = P(("x", "y", "z", "c"), None)
    wide = P(seq, "c")
    placed = (
        (rows, P(seq), P())
        + (wide,) * 4
        + (P("c", seq), P(), P(), P(), P(), P(), wide, wide, wide, rows)
    )
    return jax.shard_map(
        body,
        mesh=fine,
        in_specs=placed,
        out_specs=(rows, rows, P())
        + (wide,) * 4
        + (P("c", seq), P(), P(), P(), P(), P(), wide, wide, wide),
        check_vma=False,
    )
```

time: 3280 us -> 657 us (0.20); the launches traced: 3220 us -> 648 us
  waiting for transfers between devices: 1810 us -> 0 us
  blocking collectives: 764 us -> 5.53 us
  Pallas kernels: 0 us -> 507 us
  other arithmetic: 238 us -> 14.4 us
  matrix products: 229 us -> 61.7 us
  local copies, waits for them, and re-layouts: 146 us -> 56.8 us
    reduce_scatter x4 -> x0, waiting for transfers between devices: 759 us -> none  [the longest x1 402 us: body(): lax.psum_scatter(grad_up_cols, 'seq', scatter_dimension=0, tiled=True)]
    pallas_call x0 -> x18, Pallas kernels: none -> 507 us  [the longest x14 483 us: remote_call(): pl.pallas_call(kernel, out_shape=out_shape, in_specs=in_specs, out_specs=...]
    all_gather x12 -> x0, waiting for transfers between devices: 499 us -> none  [the longest x2 111 us: entering(): pieces = jax.tree.map(lambda part: lax.all_gather(part, axis), value)]
    psum x1 -> x0, blocking collectives: 464 us -> none  [body(): lax.psum((grad_norm1, grad_norm2, grad_head, grad_low_down, grad_low_up,...]
    unnamed x23 -> x0, waiting for transfers between devices: 407 us -> none
    all_gather x4 -> x1, blocking collectives: 300 us -> 5.53 us  [body(): pair = lax.all_gather(offsets.reshape(2, 64), 'z')]
    dot_general x90 -> x22, matrix products: 229 us -> 61.7 us  [dot(): lax.dot_general(left, right, (dims, ((), ())), precision=precision, prefe...]
    psum x3 -> x0, waiting for transfers between devices: 148 us -> none  [the longest x1 107 us: body(): lax.psum((grad_norm1, grad_norm2, grad_head, grad_low_down, grad_low_up,...]
  transfers between devices with their start and end apart: 21 -> 0, of which waited for: 13 -> 0; matrix products, arithmetic and copies ran while one was open for 14% -> 0% of each run, Pallas kernels for 0% -> 0%
where the time goes in v1:
time: 657 us; the launch traced here: 648 us
  Pallas kernels  507 us (77%)
  matrix products  61.7 us (9%)
  local copies, waits for them, and re-layouts  56.8 us (9%)
  other arithmetic  14.4 us (2%)
    pallas_call x14, Pallas kernels, remote_call(): pl.pallas_call(kernel, out_shape=out_shape, in_specs=in_specs, out_specs=...  483 us
    dot_general x22, matrix products, dot(): lax.dot_general(left, right, (dims, ((), ())), precision=precision, prefe...  61.7 us
    pallas_call x4, Pallas kernels, chunk_call(): pl.pallas_call(kernel, grid=(4,), out_shape=[jax.ShapeDtypeStruct(shape,...  23.7 us
    concatenate x1, local copies, waits for them, and re-layouts, body(): jnp.concatenate([tn(first, dproj).astype(BF), tn(grad_attn, branch).astyp...  18.6 us

profile of v1, /device:TPU:1, one launch (start us, length us, event | category | flops | bytes accessed | tf_op | source)
XLA Modules:
  0.0 647.6 jit_solution(4469285190076686430)
XLA Ops:
  13.4 118.2 %shard_map.288 = (bf16[4,4,128,1280]{3,2,1,0:T(8,128)(2,1)}, bf16[4,4,128,2304]{3,2,1,0:T(8,128)(2,1)}, bf16[2,4,64,2048]{3,2,1,0:T(8,128)(2,1)}, bf16[2,4,64,2048]{3,2,1,0:T(8,128)(2,1)}) custom-call(bf16[2,2,32,1280]{3,2,1,0:T(8,128)(2,1)} %reshape.276.wm, bf16[4,32,2304]{2,1,0:T(8,128)(2,1)} %reshape.277.wf, bf16[64,2048]{1,0:T(8,128)(2,1)} %fusion.41.rows_a, ...), custom_call_target="tpu_custom_call" | custom-call | tf_op jit(solution)/shard_map/pallas_call | solution.py:69
  131.7 5.2 fusion.26
  136.9 13.0 %shard_map.289.qkv = bf16[2,4,64,768]{3,2,1,0:T(8,128)(2,1)} custom-call(bf16[2,4,64,768]{3,2,1,0:T(8,128)(2,1)} %bitcast.152), custom_call_target="tpu_custom_call" | custom-call | tf_op jit(solution)/shard_map/pallas_call | solution.py:69
  153.0 5.5 all_gather.3
  158.7 3.8 shard_map.290
  163.5 33.0 %shard_map.291.states = f32[4,64,1024]{2,1,0:T(8,128)} custom-call(f32[4,64,1152]{2,1,0:T(8,128)} %copy-done.5), custom_call_target="tpu_custom_call" | custom-call | tf_op jit(solution)/shard_map/pallas_call | solution.py:69
  197.7 3.9 shard_map.292
  202.7 9.2 %shard_map.293 = f32[2,4,64,256]{3,2,1,0:T(8,128)} custom-call(f32[2,4,64,256]{3,2,1,0:T(8,128)} %fusion.50.src), custom_call_target="tpu_custom_call" | custom-call | tf_op jit(solution)/shard_map/pallas_call | solution.py:69
  214.8 3.4 convolution_convert_fusion.3
  218.2 20.8 %shard_map.294 = f32[64,2048]{1,0:T(8,128)} custom-call(bf16[2,4,64,2048]{3,2,1,0:T(8,128)(2,1)} %bitcast.132), custom_call_target="tpu_custom_call" | custom-call | tf_op jit(solution)/shard_map/pallas_call | solution.py:69
  241.1 18.0 %shard_map.295 = bf16[2,4,64,2048]{3,2,1,0:T(8,128)(2,1)} custom-call(bf16[64,2048]{1,0:T(8,128)(2,1)} %multiply_convert_fusion.3.src), custom_call_target="tpu_custom_call" | custom-call | tf_op jit(solution)/shard_map/pallas_call | solution.py:69
  259.2 4.5 fusion.19
  263.7 3.8 fusion.15
  269.8 3.2 convolution_convert_fusion.4
  274.9 3.2 add_convert_fusion
  278.1 31.8 %shard_map.296 = (f32[64,2048]{1,0:T(8,128)}, f32[64,2048]{1,0:T(8,128)}) custom-call(bf16[2,4,64,2048]{3,2,1,0:T(8,128)(2,1)} %bitcast.148, bf16[2,4,64,2048]{3,2,1,0:T(8,128)(2,1)} %bitcast.149), custom_call_target="tpu_custom_call" | custom-call | tf_op jit(solution)/shard_map/pallas_call | solution.py:69
  313.7 18.0 %shard_map.297 = bf16[2,4,64,2048]{3,2,1,0:T(8,128)(2,1)} custom-call(bf16[64,2048]{1,0:T(8,128)(2,1)} %get-tuple-element.66.src), custom_call_target="tpu_custom_call" | custom-call | tf_op jit(solution)/shard_map/pallas_call | solution.py:69
  331.7 3.5 fusion.58
  335.3 9.2 %shard_map.298 = f32[2,4,64,256]{3,2,1,0:T(8,128)} custom-call(f32[2,4,64,256]{3,2,1,0:T(8,128)} %bitcast.156), custom_call_target="tpu_custom_call" | custom-call | tf_op jit(solution)/shard_map/pallas_call | solution.py:69
  350.1 4.0 shard_map.299
  355.2 30.5 %shard_map.300.nexts = f32[4,64,1024]{2,1,0:T(8,128)} custom-call(f32[4,64,1152]{2,1,0:T(8,128)} %copy-done.8), custom_call_target="tpu_custom_call" | custom-call | tf_op jit(solution)/shard_map/pallas_call | solution.py:69
  386.9 12.1 %shard_map.301 = (bf16[2,4,64,768]{3,2,1,0:T(8,128)(2,1)S(1)}, f32[4,64,64]{2,1,0:T(8,128)S(1)}) custom-call(bf16[2,4,64,768]{3,2,1,0:T(8,128)(2,1)S(1)} %copy-done.2, bf16[4,64,512]{2,1,0:T(8,128)(2,1)S(1)} %subtract_convert_fusion.grad, f32[4,64,64]{2,1,0:T(8,128)S(1)} %bitcast.124, f32[4,64,64]{2,1,0:T(8,128)S(1)} %get-tuple-element.40.cum_ref, ...), custom_call_target="tpu_custom_call" | custom-call | tf_op jit(solution)/shard_map/pallas_call | solution.py:618
  401.3 13.2 %shard_map.302 = bf16[2,4,64,768]{3,2,1,0:T(8,128)(2,1)} custom-call(bf16[2,4,64,768]{3,2,1,0:T(8,128)(2,1)} %copy-done.9), custom_call_target="tpu_custom_call" | custom-call | tf_op jit(solution)/shard_map/pallas_call | solution.py:69
  414.5 6.1 fusion.3
  420.6 19.9 %shard_map.303 = f32[64,2048]{1,0:T(8,128)} custom-call(bf16[2,4,64,2048]{3,2,1,0:T(8,128)(2,1)} %bitcast.131), custom_call_target="tpu_custom_call" | custom-call | tf_op jit(solution)/shard_map/pallas_call | solution.py:69
  446.1 32.6 %shard_map.304 = f32[336,128]{1,0:T(8,128)} custom-call(f32[336,128]{1,0:T(8,128)} %pad_bitcast_fusion.src), custom_call_target="tpu_custom_call" | custom-call | tf_op jit(solution)/shard_map/pallas_call | solution.py:69
  480.0 6.1 convert_dynamic-update-slice_fusion
  488.1 3.6 fusion.4
  491.6 3.5 fusion.5
  495.1 3.6 fusion.6
  498.7 18.6 %copy.117 = bf16[2048,3584]{1,0:T(8,128)(2,1)} copy(bf16[2048,3584]{0,1:T(8,128)(2,1)} %fusion.6) | data formatting | bytes 29360128 | tf_op jit(solution)/shard_map/concatenate | solution.py:980
  517.3 115.8 %shard_map.305 = (bf16[2,2,32,1280]{3,2,1,0:T(8,128)(2,1)}, bf16[4,32,2304]{2,1,0:T(8,128)(2,1)}) custom-call(bf16[4,4,128,3584]{3,2,1,0:T(8,128)(2,1)} %bitcast.128), custom_call_target="tpu_custom_call" | custom-call | tf_op jit(solution)/shard_map/pallas_call | solution.py:69
  (211 shorter events, 64.7 us)
Async XLA Ops:
  0.6 150.8 %copy-start = (bf16[2048,16]{0,1:T(8,128)(2,1)S(1)}, bf16[2048,16]{0,1:T(8,128)(2,1)}, u32[]{:S(2)}) copy-start(bf16[2048,16]{0,1:T(8,128)(2,1)} %param.25) | copy-start | bytes 196612
  0.7 7.2 %copy-start.32 = (bf16[32,2816]{1,0:T(8,128)(2,1)S(1)}, bf16[32,2816]{1,0:T(8,128)(2,1)}, u32[]{:S(2)}) copy-start(bf16[32,2816]{1,0:T(8,128)(2,1)} %param.32) | copy-start | bytes 540676
  2.6 5.8 copy-start.33
  131.7 18.3 %copy-start.41 = (f32[256]{0:T(256)S(1)}, f32[256]{0:T(256)}, u32[]{:S(2)}) copy-start(f32[256]{0:T(256)} %param.27) | copy-start | bytes 3076
  136.9 14.9 %copy-start.38 = (bf16[16,256]{1,0:T(8,128)(2,1)S(1)}, bf16[16,256]{1,0:T(8,128)(2,1)}, u32[]{:S(2)}) copy-start(bf16[16,256]{1,0:T(8,128)(2,1)} %param.26) | copy-start | bytes 24580
  150.0 8.7 %copy-start.2 = (bf16[2,4,64,768]{3,2,1,0:T(8,128)(2,1)S(1)}, bf16[2,4,64,768]{3,2,1,0:T(8,128)(2,1)}, u32[]{:S(2)}) copy-start(bf16[2,4,64,768]{3,2,1,0:T(8,128)(2,1)} %shard_map.289.qkv) | copy-start | bytes 2359300
  163.5 38.1 %copy-start.37 = (f32[512]{0:T(512)S(1)}, f32[512]{0:T(512)}, u32[]{:S(2)}) copy-start(f32[512]{0:T(512)} %param.28) | copy-start | bytes 6148
  201.6 13.2 %copy-start.10 = (f32[4,64,64]{2,1,0:T(8,128)}, f32[4,64,64]{2,1,0:T(8,128)S(1)}, u32[]{:S(2)}) copy-start(f32[4,64,64]{2,1,0:T(8,128)S(1)} %get-tuple-element.50.far_ref.far) | copy-start | bytes 196612
  201.6 13.2 %copy-start.13 = (f32[4,64,64]{2,1,0:T(8,128)}, f32[4,64,64]{2,1,0:T(8,128)S(1)}, u32[]{:S(2)}) copy-start(f32[4,64,64]{2,1,0:T(8,128)S(1)} %get-tuple-element.49.mixing) | copy-start | bytes 196612
  201.7 10.3 %copy-start.27 = (bf16[2,4,64,2048]{3,2,1,0:T(8,128)(2,1)S(1)}, bf16[2,4,64,2048]{3,2,1,0:T(8,128)(2,1)}, u32[]{:S(2)}) copy-start(bf16[2,4,64,2048]{3,2,1,0:T(8,128)(2,1)} %get-tuple-element.38) | copy-start | bytes 6291460
  214.8 24.2 %copy-start.30 = (bf16[512,256]{1,0:T(8,128)(2,1)}, bf16[512,256]{1,0:T(8,128)(2,1)S(1)}, u32[]{:S(2)}) copy-start(bf16[512,256]{1,0:T(8,128)(2,1)S(1)} %get-tuple-element.94) | copy-start | bytes 786436
  218.2 22.1 %copy-start.35 = (f32[2048]{0:T(1024)S(1)}, f32[2048]{0:T(1024)}, u32[]{:S(2)}) copy-start(f32[2048]{0:T(1024)} %param.29) | copy-start | bytes 24580
  259.2 4.5 copy-start.20
  259.2 8.3 %slice-start = ((s8[9437184]{0:T(1024)(128)(4,1)}), s8[4194304]{0:T(1024)(128)(4,1)S(1)}, s32[]{:S(2)}) async-start(s8[9437184]{0:T(1024)(128)(4,1)} %bitcast.169), calls=%async_computation | async-start | bytes 8388608
  259.2 8.3 %slice-start.1 = ((s8[9437184]{0:T(1024)(128)(4,1)}), s8[4194304]{0:T(1024)(128)(4,1)S(1)}, s32[]{:S(2)}) async-start(s8[9437184]{0:T(1024)(128)(4,1)} %bitcast.169), calls=%async_computation.1 | async-start | bytes 8388608
  263.7 3.9 slice-start.2
  269.8 5.0 copy-start.43
  278.1 33.1 %copy-start.24 = (bf16[64,2048]{1,0:T(8,128)(2,1)S(1)}, bf16[64,2048]{1,0:T(8,128)(2,1)}, u32[]{:S(2)}) copy-start(bf16[64,2048]{1,0:T(8,128)(2,1)} %rows_b.1) | copy-start | bytes 786436
  311.2 20.6 %copy-start.28 = (f32[2,4,64,256]{3,2,1,0:T(8,128)S(1)}, f32[2,4,64,256]{3,2,1,0:T(8,128)}, u32[]{:S(2)}) copy-start(f32[2,4,64,256]{3,2,1,0:T(8,128)} %shard_map.293) | copy-start | bytes 1572868
  311.2 20.6 %copy-start.47 = (f32[512,256]{1,0:T(8,128)S(1)}, f32[512,256]{1,0:T(8,128)}, u32[]{:S(2)}) copy-start(f32[512,256]{1,0:T(8,128)} %get-tuple-element.95) | copy-start | bytes 1572868
  335.2 12.7 %copy-start.4 = (f32[4,64,1024]{2,1,0:T(8,128)S(1)}, f32[4,64,1024]{2,1,0:T(8,128)}, u32[]{:S(2)}) copy-start(f32[4,64,1024]{2,1,0:T(8,128)} %shard_map.291.states) | copy-start | bytes 3145732
  355.2 30.5 %copy-start.12 = (f32[4,64,64]{2,1,0:T(8,128)S(1)}, f32[4,64,64]{2,1,0:T(8,128)}, u32[]{:S(2)}) copy-start(f32[4,64,64]{2,1,0:T(8,128)} %copy-done.10) | copy-start | bytes 196612
  355.2 30.5 %copy-start.14 = (f32[4,64,64]{2,1,0:T(8,128)S(1)}, f32[4,64,64]{2,1,0:T(8,128)}, u32[]{:S(2)}) copy-start(f32[4,64,64]{2,1,0:T(8,128)} %copy-done.13) | copy-start | bytes 196612
  399.9 14.6 %copy-start.29 = (bf16[512,256]{1,0:T(8,128)(2,1)S(1)}, bf16[512,256]{1,0:T(8,128)(2,1)}, u32[]{:S(2)}) copy-start(bf16[512,256]{1,0:T(8,128)(2,1)} %get-tuple-element.81) | copy-start | bytes 786436
  420.6 19.9 %copy-start.18 = (bf16[64,2048]{1,0:T(8,128)(2,1)S(1)}, bf16[64,2048]{1,0:T(8,128)(2,1)}, u32[]{:S(2)}) copy-start(bf16[64,2048]{1,0:T(8,128)(2,1)} %param.17) | copy-start | bytes 786436
  420.6 21.2 %copy-start.23 = (f32[64,2048]{1,0:T(8,128)S(1)}, f32[64,2048]{1,0:T(8,128)}, u32[]{:S(2)}) copy-start(f32[64,2048]{1,0:T(8,128)} %get-tuple-element.67) | copy-start | bytes 1572868
  420.6 23.3 %copy-start.16 = (bf16[1,4,64,2048]{3,2,1,0:T(8,128)(2,1)S(1)}, bf16[1,4,64,2048]{3,2,1,0:T(8,128)(2,1)}, u32[]{:S(2)}) copy-start(bf16[1,4,64,2048]{3,2,1,0:T(8,128)(2,1)} %copy-done.15) | copy-start | bytes 3145732
  441.8 38.2 %copy-start.19 = (bf16[2,4,64,768]{3,2,1,0:T(8,128)(2,1)S(1)}, bf16[2,4,64,768]{3,2,1,0:T(8,128)(2,1)}, u32[]{:S(2)}) copy-start(bf16[2,4,64,768]{3,2,1,0:T(8,128)(2,1)} %shard_map.302) | copy-start | bytes 2359300
  480.0 6.1 copy-start.22
  480.0 6.1 copy-start.31
  634.4 4.9 copy-start.25
  634.4 7.4 %copy-start.26 = (bf16[4,32,2304]{2,1,0:T(8,128)(2,1)S(1)}, bf16[4,32,2304]{2,1,0:T(8,128)(2,1)}, u32[]{:S(2)}) copy-start(bf16[4,32,2304]{2,1,0:T(8,128)(2,1)} %get-tuple-element.59) | copy-start | bytes 1769476
  (21 other events, 50.6 us)

commit v2 on v0

v2 whole, which is shorter than its diff:
```python
import functools

import jax
import jax.numpy as jnp
from jax import lax
from jax.experimental import pallas as pl
from jax.experimental.pallas import tpu as pltpu
from jax.sharding import Mesh
from jax.sharding import PartitionSpec as P

DK = 512
SLOTS = 64
CHUNK = 64
HALF = 256
UNITS = 704
UNITS_PAD = 768
REACH = 8
EPS = 1e-06
SCALE = 0.125
BF = jnp.bfloat16
F32 = jnp.float32
HIGH = lax.Precision.HIGHEST
MESH = pl.DeviceIdType.MESH
ANY = pl.BlockSpec(memory_space=pl.ANY)
VMEM = pl.BlockSpec(memory_space=pltpu.VMEM)
DMA = pltpu.SemaphoreType.DMA
MIX = 5 * HALF
FFN = 3 * UNITS_PAD


def dot(left, right, dims=((1,), (0,)), precision=None):
    return lax.dot_general(
        left, right, (dims, ((), ())), precision=precision, preferred_element_type=F32
    )


def nt(left, right, precision=None):
    return dot(left, right, ((1,), (1,)), precision)


def tn(left, right, precision=None):
    return dot(left, right, ((0,), (0,)), precision)


def here():
    return tuple(lax.axis_index(a) for a in ("x", "y", "z", "c"))


def wrap(v, n=4):
    return lax.rem(v + n, n)


def greet(peers):
    barrier = pltpu.get_barrier_semaphore()
    for peer in peers:
        pl.semaphore_signal(barrier, inc=1, device_id=peer, device_id_type=MESH)
    pl.semaphore_wait(barrier, len(peers))


def push(src, dst, send, recv, peer):
    copy = pltpu.make_async_remote_copy(
        src_ref=src, dst_ref=dst, send_sem=send, recv_sem=recv, device_id=peer, device_id_type=MESH
    )
    copy.start()
    return copy


class Refs:
    pass


def remote_call(kernel, collective_id, operands, outs, scratch):
    names = list(operands) + list(outs) + list(scratch)

    def run(*refs):
        r = Refs()
        for name, ref in zip(names, refs):
            setattr(r, name, ref)
        kernel(r)

    results = pl.pallas_call(
        run,
        out_shape=[jax.ShapeDtypeStruct(shape, dtype) for shape, dtype, _ in outs.values()],
        in_specs=[spec for _, spec in operands.values()],
        out_specs=[spec for _, _, spec in outs.values()],
        scratch_shapes=list(scratch.values()),
        compiler_params=pltpu.CompilerParams(
            collective_id=collective_id, has_side_effects=True, vmem_limit_bytes=63 * 2**20
        ),
    )(*[array for array, _ in operands.values()])
    return dict(zip(outs, results))


def spread_block(w_ref, side, k, cols):
    x, y, z, c = here()
    part = pl.ds(side * (cols // 2), cols // 2)
    if side == 0:
        return w_ref.at[x, wrap(y - k), :, part]
    return w_ref.at[wrap(x - k), y, :, part]


def spread_near(w_ref, sems, cols):
    x, y, z, c = here()
    sent = {}
    for d in range(1, 4):
        for side in range(2):
            block = spread_block(w_ref, side, 0, cols)
            peer = (x, wrap(y + d), z, c) if side == 0 else (wrap(x + d), y, z, c)
            sent[side, d] = push(
                block, block, sems[0].at[side, d - 1], sems[1].at[side, d - 1], peer
            )
    return sent


def spread_far(w_ref, sems, cols, near, k):
    x, y, z, c = here()
    sent = []
    for side in range(2):
        if k > 0:
            near[side, k].wait_recv()
        block = spread_block(w_ref, side, k, cols)
        for d in range(1, 4):
            peer = (wrap(x + d), y, z, c) if side == 0 else (x, wrap(y + d), z, c)
            sent.append(
                push(
                    block, block, sems[2].at[side, k, d - 1], sems[3].at[side, k, d - 1], peer
                )
            )
    return sent


def rows_start(src, out, sems):
    x, y, z, c = here()
    hop_s, hop_r, pair_s, pair_r, own = sems
    mine = pltpu.make_async_copy(src, out.at[c, z], own)
    mine.start()
    hops = [
        push(src, out.at[c, z], hop_s.at[d - 1], hop_r.at[d - 1], (x, y, wrap(z + d), c))
        for d in range(1, 4)
    ]
    pairs = [push(src, out.at[c, z], pair_s.at[0], pair_r.at[0], (x, y, z, 1 - c))]
    return mine, hops, pairs


def rows_finish(started, out, sems):
    x, y, z, c = here()
    hop_s, hop_r, pair_s, pair_r, own = sems
    mine, hops, pairs = started
    for d in range(1, 4):
        hops[d - 1].wait_recv()
        block = out.at[c, wrap(z - d)]
        pairs.append(push(block, block, pair_s.at[d], pair_r.at[d], (x, y, z, 1 - c)))
    mine.wait()
    for copy in hops:
        copy.wait_send()
    for copy in pairs:
        copy.wait()


def group_peers():
    x, y, z, c = here()
    return [(x, y, wrap(z + d), k) for d in range(1, 4) for k in range(2)] + [(x, y, z, 1 - c)]


def row_peers():
    x, y, z, c = here()
    return [(x, y, wrap(z + d), c) for d in range(1, 4)] + [(x, y, z, 1 - c)]


def plane_peers():
    x, y, z, c = here()
    return [(wrap(x + d), y, z, c) for d in range(1, 4)] + [
        (x, wrap(y + d), z, c) for d in range(1, 4)
    ]


def all_peers():
    return group_peers() + plane_peers()


def spread_sems(name):
    kinds = ((2, 3), (2, 3), (2, 4, 3), (2, 4, 3))
    return {f"{name}{n}": DMA(shape) for n, shape in enumerate(kinds)}


def rows_sems(name):
    kinds = ((3,), (3,), (4,), (4,), ())
    return {f"{name}{n}": DMA(shape) for n, shape in enumerate(kinds)}


def sems_of(r, name, count):
    return [getattr(r, f"{name}{n}") for n in range(count)]


def deal_start(src, wide, send, recv):
    x, y, z, c = here()
    dst = wide.at[x, y, pl.ds(pl.multiple_of(z * 32, 32), 32), :]
    sent = []
    for j in range(2):
        for k in range(2):
            same = jnp.logical_and(2 * c + j == z, c == k)
            copy = pltpu.make_async_remote_copy(
                src_ref=src.at[j, k],
                dst_ref=dst,
                send_sem=send.at[j, k],
                recv_sem=recv.at[z],
                device_id=(x, y, 2 * c + j, k),
                device_id_type=MESH,
            )

            @pl.when(same)
            def _():
                pltpu.make_async_copy(src.at[j, k], dst, recv.at[z]).start()

            @pl.when(jnp.logical_not(same))
            def _():
                copy.start()

            sent.append((same, copy))
    return sent


def deal_wait(src, wide, recv):
    x, y, z, c = here()
    for s in range(4):
        dst = wide.at[x, y, pl.ds(s * 32, 32), :]
        pltpu.make_async_copy(src.at[0, 0], dst, recv.at[s]).wait()


def deal_done(sent):
    for same, copy in sent:

        @pl.when(jnp.logical_not(same))
        def _():
            copy.wait_send()


def shuffle_start(block, dst, send, recv, own):
    x, y, z, c = here()
    mine = pltpu.make_async_copy(block(z), dst, own)
    mine.start()
    sent = [
        push(block(wrap(z + d)), dst, send.at[d - 1], recv.at[d - 1], (x, y, wrap(z + d), c))
        for d in range(1, 4)
    ]
    return mine, sent


def shuffle_wait(started):
    started[0].wait()
    for copy in started[1]:
        copy.wait_recv()


def shuffle_done(started):
    for copy in started[1]:
        copy.wait_send()


def shuffle_sems(name):
    return {f"{name}0": DMA((3,)), f"{name}1": DMA((3,)), f"{name}2": DMA(())}


class RowSum:
    def __init__(self, r, name, parts, own):
        self.parts, self.own = parts, own
        self.theirs, self.landed = sems_of(r, name + "b", 2)
        self.sems = sems_of(r, name + "s", 4)

    def pairs(self):
        x, y, z, c = here()
        self.pair = [
            push(
                self.parts.at[1 - c, wrap(z + 1 + k)],
                self.theirs.at[k],
                self.sems[0].at[k],
                self.sems[1].at[k],
                (x, y, z, 1 - c),
            )
            for k in range(4)
        ]

    def hops(self):
        x, y, z, c = here()
        self.hop = []
        for k in range(3):
            to = wrap(z + 1 + k)
            self.pair[k].wait_recv()
            both = self.own(to).astype(F32) + self.theirs[k].astype(F32)
            self.theirs[k] = both.astype(BF)
            self.hop.append(
                push(
                    self.theirs.at[k],
                    self.landed.at[k],
                    self.sems[2].at[k],
                    self.sems[3].at[k],
                    (x, y, to, c),
                )
            )

    def result(self):
        x, y, z, c = here()
        self.pair[3].wait_recv()
        value = self.own(z).astype(F32) + self.theirs[3].astype(F32)
        for k in range(3):
            self.hop[k].wait_recv()
            value = value + self.landed[k].astype(F32)
        return value

    def done(self):
        for copy in self.pair + self.hop:
            copy.wait_send()


def sum_scratch(name):
    out = {f"{name}b{n}": pltpu.VMEM((k, 64, 2048), BF) for n, k in enumerate((4, 3))}
    out.update({f"{name}s{n}": DMA((k,)) for n, k in enumerate((4, 4, 3, 3))})
    return out


class Scan:
    def __init__(self, r, back):
        self.back, self.every = back, r.every
        self.total, self.sending, self.landed, self.entry = r.total, r.scan_out, r.scan_in, r.entry
        self.sems = sems_of(r, "scan", 6)
        self.order = [(n, k) for n in range(4) for k in range(2)]
        if back:
            self.order = self.order[::-1]

    def member(self, d):
        x, y, z, c = here()
        at = lax.rem(x * 4 + y + (-d if self.back else d) + 32, 16)
        return (at // 4, lax.rem(at, 4), z, c)

    def senders(self):
        return [self.member(-d) for d in range(1, REACH + 1)]

    def factor(self, k, n, width):
        return jnp.concatenate([self.every[k, n, :, 1024:1152]] * (width // 128), axis=1)

    def pair(self):
        x, y, z, c = here()
        self.swap = push(
            self.every.at[c], self.every.at[c], self.sems[0], self.sems[1], (x, y, z, 1 - c)
        )

    def send(self):
        x, y, z, c = here()
        self.swap.wait_recv()
        half = pl.ds(pl.multiple_of(c * DK, DK), DK)
        n, k = self.order[0]
        state = self.every[k, n, :, half]
        decay = self.every[k, n, :, 1024:1152]
        for n, k in self.order[1:]:
            state = self.factor(k, n, DK) * state + self.every[k, n, :, half]
            decay = self.every[k, n, :, 1024:1152] * decay
        self.sending[:, 0:512] = state.astype(BF)
        high = decay.astype(BF)
        self.sending[:, 512:640] = high
        self.sending[:, 640:768] = (decay - high.astype(F32)).astype(BF)
        self.far = [
            push(
                self.sending,
                self.landed.at[d - 1],
                self.sems[2].at[d - 1],
                self.sems[3].at[d - 1],
                self.member(d),
            )
            for d in range(1, REACH + 1)
        ]

    def fold(self, out):
        x, y, z, c = here()
        group = x * 4 + y
        state = jnp.zeros((SLOTS, DK), F32)
        for d in range(REACH, 0, -1):
            self.far[d - 1].wait_recv()
            valid = (group + d < 16) if self.back else (group >= d)
            block = self.landed.at[d - 1]
            keep = block[:, 512:640].astype(F32) + block[:, 640:768].astype(F32)
            fresh = jnp.concatenate([keep] * 4, axis=1) * state + block[:, 0:512].astype(F32)
            state = jnp.where(valid, fresh, 0.0)
        self.total[...] = state
        self.entry[c] = state
        self.last = push(
            self.total, self.entry.at[c], self.sems[4], self.sems[5], (x, y, z, 1 - c)
        )
        self.last.wait_recv()
        for s in range(2):
            state = self.entry[s]
            cols = pl.ds(s * DK, DK)
            for n, k in self.order:

                @pl.when(c == k)
                def _():
                    out[n, :, cols] = state

                state = self.factor(k, n, DK) * state + self.every[k, n, :, cols]

    def done(self):
        for copy in self.far + [self.swap, self.last]:
            copy.wait_send()


def scan_scratch():
    out = dict(
        every=pltpu.VMEM((2, 4, SLOTS, 1152), F32),
        total=pltpu.VMEM((SLOTS, DK), F32),
        scan_out=pltpu.VMEM((SLOTS, 768), BF),
        scan_in=pltpu.VMEM((REACH, SLOTS, 768), BF),
        entry=pltpu.VMEM((2, SLOTS, DK), F32),
    )
    kinds = ((), (), (REACH,), (REACH,), (), ())
    out.update({f"scan{n}": DMA(shape) for n, shape in enumerate(kinds)})
    return out


def places():
    row = lax.broadcasted_iota(jnp.int32, (CHUNK, CHUNK), 0)
    col = lax.broadcasted_iota(jnp.int32, (CHUNK, CHUNK), 1)
    return row, col


def tri(lower):
    row, col = places()
    return ((row >= col) if lower else (row <= col)).astype(F32)


def seen_mask(offs):
    row, col = places()
    return jnp.logical_and(row >= col, offs >= (row - col).astype(F32))


def carried(cum, offs):
    return jnp.exp(cum) * (offs > places()[0].astype(F32)).astype(F32)


def reaching(cum, offs):
    final = offs[CHUNK - 1 : CHUNK]
    tail = (places()[0].astype(F32) >= CHUNK - 1 - final).astype(F32)
    return jnp.exp(cum[CHUNK - 1 : CHUNK] - cum) * tail


def features(ref, n, which):
    cols = pl.ds(which * HALF, HALF)
    return jnp.concatenate([ref[0, n, :, cols], ref[1, n, :, cols]], axis=1)


def tiles(value):
    return [value[8 * b : 8 * b + 8] for b in range(CHUNK // 8)]


def one_row(blocks, i):
    return blocks[i // 8][i % 8 : i % 8 + 1]


def spans(cum, i):
    last = one_row(cum, i)
    return [(b, jnp.exp(jnp.minimum(cum[b] - last, 0.0))) for b in range(i // 8, CHUNK // 8)]


def weigh(cum, write, columns):
    cum, write, cols = tiles(cum), tiles(write), tiles(columns)
    total = [jnp.zeros((8, SLOTS), F32) for _ in range(CHUNK // 8)]
    for i in range(CHUNK):
        scale = one_row(write, i)
        for b, span in spans(cum, i):
            total[b] = total[b] + cols[b][:, i : i + 1] * (span * scale)
    return jnp.concatenate(total, axis=0)


def weigh_slots(cum, write, values):
    cum, write, vals = tiles(cum), tiles(write), tiles(values)
    lane = lax.broadcasted_iota(jnp.int32, (8, CHUNK), 1)
    total = [jnp.zeros((8, CHUNK), F32) for _ in range(CHUNK // 8)]
    for i in range(CHUNK):
        scale = one_row(write, i)
        for b, span in spans(cum, i):
            got = jnp.sum(vals[b] * (span * scale), axis=1, keepdims=True)
            total[b] = jnp.where(lane == i, got, total[b])
    return jnp.concatenate(total, axis=0)


def chunk_ends(key, value, lam, write, offs):
    cum = dot(tri(True), lam, precision=HIGH)
    ending = (reaching(cum, offs) * write).astype(BF)
    keep = (offs[CHUNK - 1 : CHUNK, 0:1] > CHUNK - 1).astype(F32)
    keep = keep * jnp.exp(tn(lam, jnp.ones((CHUNK, 128), F32), HIGH))
    return cum, jnp.concatenate([tn(ending, key), tn(ending, value), keep], axis=1)


def chunk_near(query, key, cum, write, offs):
    return weigh(cum, write, jnp.where(seen_mask(offs), nt(query, key) * SCALE, 0.0))


def chunk_out(query, value, cum, write, offs, near, state):
    carry = carried(cum, offs)
    far = nt(query, state[:, 0:512].astype(BF)) * SCALE
    scores = near + carry * far
    scores = jnp.exp(scores - jnp.max(scores, axis=1, keepdims=True))
    probs = scores / jnp.sum(scores, axis=1, keepdims=True)
    mixing = jnp.where(seen_mask(offs), weigh_slots(cum, write, probs), 0.0)
    mixed = dot(mixing.astype(BF), value) + dot(
        (probs * carry).astype(BF), state[:, 512:1024].astype(BF)
    )
    return far, probs, mixing, mixed


def chunk_back(query, value, g, cum, write, offs, probs, state):
    carry = carried(cum, offs)
    dmix = jnp.where(seen_mask(offs), nt(g, value), 0.0)
    dfar = nt(g, state[:, 512:1024].astype(BF))
    dnear = weigh(cum, write, dmix)
    dprobs = dnear + carry * dfar
    dscore = probs * (dprobs - jnp.sum(probs * dprobs, axis=1, keepdims=True))
    ends_k = tn((SCALE * dscore * carry).astype(BF), query)
    ends_v = tn((probs * carry).astype(BF), g)
    return dmix, dfar, dnear, dscore, ends_k, ends_v


def chunk_pairs(cum, write, affinity, dmix, dscore, probs):
    cums, writes = tiles(cum), tiles(write)
    aff, dmx, dsc, prb = tiles(affinity), tiles(dmix), tiles(dscore), tiles(probs)
    lane = lax.broadcasted_iota(jnp.int32, (8, CHUNK), 1)
    daff = [jnp.zeros((8, CHUNK), F32) for _ in range(CHUNK // 8)]
    fresh = []
    for i in range(CHUNK):
        scale = one_row(writes, i)
        both = jnp.zeros((8, SLOTS), F32)
        for b, span in spans(cums, i):
            got = jnp.sum(dsc[b] * (span * scale), axis=1, keepdims=True)
            daff[b] = jnp.where(lane == i, got, daff[b])
            both = both + (dsc[b] * aff[b][:, i : i + 1] + prb[b] * dmx[b][:, i : i + 1]) * span
        fresh.append(jnp.sum(both, axis=0, keepdims=True))
    return jnp.concatenate(daff, axis=0), jnp.concatenate(fresh, axis=0)


def chunk_last(
    query, key, value, g, lam, write, slope, offs, cum, near, far, probs, mixing, state, dmix, dfar, dnear, dscore, after
):
    carry, seen, reach = carried(cum, offs), seen_mask(offs), reaching(cum, offs)
    affinity = jnp.where(seen, nt(query, key) * SCALE, 0.0)
    daff, fresh = chunk_pairs(cum, write, affinity, dmix, dscore, probs)
    daff = jnp.where(seen, daff * SCALE, 0.0).astype(BF)
    ending = (reach * write).astype(BF)
    nk, nv = after[:, 0:512].astype(BF), after[:, 512:1024].astype(BF)
    dq = dot(daff, key) + dot((SCALE * dscore * carry).astype(BF), state[:, 0:512].astype(BF))
    dk = tn(daff, query) + dot(ending, nk)
    dv = tn(mixing.astype(BF), g) + dot(ending, nv)
    dend = (nt(key, nk) + nt(value, nv)) * reach
    dkeep = nt(jnp.ones((8, 1024), F32), after * state, HIGH)[0:1]
    keep = (offs[CHUNK - 1 : CHUNK] > CHUNK - 1).astype(F32) * jnp.exp(cum[CHUNK - 1 : CHUNK])
    scaled = write * dend
    dcum = dscore * near + probs * dnear + carry * (dscore * far + probs * dfar)
    dcum = dcum - write * fresh - scaled
    at_end = jnp.sum(scaled, axis=0, keepdims=True) + dkeep * keep
    dcum = dcum + jnp.where(places()[0] == CHUNK - 1, at_end, 0.0)
    dlam = dot(tri(False), dcum, precision=HIGH) - jnp.exp(lam) * (fresh + dend)
    return dq, dk, dv, dlam * slope


def forward_kernel(r):
    x, y, z, c = here()
    partner = (x, y, z, 1 - c)
    scan = Scan(r, False)
    greet(all_peers() + scan.senders())
    q_deal = deal_start(r.wq, r.wide_q, r.q_send, r.q_recv)
    a_sems, b_sems, s_sems = (sems_of(r, n, 5) for n in ("rows_a_", "rows_b_", "rows_s_"))
    a_rows = rows_start(r.rows_a, r.first, a_sems)
    gates = shuffle_start(lambda k: r.packed.at[k], r.gates.at[z], *sems_of(r, "gate", 3))
    g_deal = deal_start(r.wg, r.wide_g, r.g_send, r.g_recv)
    f_deal = shuffle_start(
        lambda k: r.wf.at[k],
        r.wide_f.at[x, y, pl.ds(pl.multiple_of(z * 32, 32), 32), :],
        *sems_of(r, "deal", 3),
    )
    b_rows = rows_start(r.rows_b, r.cot, b_sems)
    q_sems, g_sems, f_sems = (sems_of(r, n, 4) for n in ("q_spread", "g_spread", "f_spread"))
    deal_wait(r.wq, r.wide_q, r.q_recv)
    q_near = spread_near(r.wide_q, q_sems, 3 * HALF)
    q_far = spread_far(r.wide_q, q_sems, 3 * HALF, q_near, 0)
    for k in range(1, 4):
        q_far += spread_far(r.wide_q, q_sems, 3 * HALF, q_near, k)
    deal_wait(r.wg, r.wide_g, r.g_recv)
    g_near = spread_near(r.wide_g, g_sems, 2 * HALF)
    rows_finish(a_rows, r.first, a_sems)
    shuffle_wait(gates)
    for copy in q_far:
        copy.wait_recv()
    g_far = []
    for k in range(4):
        g_far += spread_far(r.wide_g, g_sems, 2 * HALF, g_near, k)
    shuffle_wait(f_deal)
    f_near = spread_near(r.wide_f, f_sems, FFN)

    @pl.loop(0, 3)
    def _(n):
        cols = pl.ds(pl.multiple_of(n * HALF, HALF), HALF)
        rows = r.first[...].reshape(512, 2048)
        got = dot(rows, r.wide_q[:, :, :, cols].reshape(2048, HALF))
        r.proj[:, :, :, cols] = got.astype(BF).reshape(2, 4, 64, HALF)

    swap = push(r.proj.at[1 - c], r.qkv.at[c], r.swap_s.at[0], r.swap_r.at[0], partner)
    r.qkv[c] = r.proj[c]
    swap.wait()

    @pl.loop(0, 4)
    def _(n):
        lam, write, offs = r.gates[n, 0], r.gates[n, 1], r.gates[n, 3]
        cum, ends = chunk_ends(features(r.qkv, n, 1), features(r.qkv, n, 2), lam, write, offs)
        r.cum[n] = cum
        r.every[c, n] = ends
        r.decays[n] = ends[:, 1024:1152]

    scan.pair()
    scan.send()

    @pl.loop(0, 4)
    def _(n):
        query, key = features(r.qkv, n, 0), features(r.qkv, n, 1)
        r.near[n] = chunk_near(query, key, r.cum[n], r.gates[n, 1], r.gates[n, 3])

    for copy in g_far:
        copy.wait_recv()
    r.gate_lin[...] = dot(
        r.first[...].reshape(512, 2048), r.wide_g[:, :, :, 0:HALF].reshape(2048, HALF)
    ).reshape(2, 4, 64, HALF)
    scan.fold(r.states)
    f_far = []
    for k in range(4):
        f_far += spread_far(r.wide_f, f_sems, FFN, f_near, k)

    @pl.loop(0, 4)
    def _(n):
        query, value = features(r.qkv, n, 0), features(r.qkv, n, 2)
        far, probs, mixing, mixed = chunk_out(
            query, value, r.cum[n], r.gates[n, 1], r.gates[n, 3], r.near[n], r.states[n]
        )
        r.far[n], r.probs[n], r.mixing[n], r.mixed[n] = far, probs, mixing, mixed
        normed = rms(mixed, r.head_gain[...])
        for s in range(2):
            r.normed[s, n] = normed[:, s * HALF : (s + 1) * HALF]

    swap2 = push(r.normed.at[1 - c], r.headnorm.at[c], r.swap_s.at[1], r.swap_r.at[1], partner)
    r.headnorm[c] = r.normed[c]
    rows_finish(b_rows, r.cot, b_sems)
    swap2.wait()
    sums = RowSum(r, "mix", r.parts, lambda k: r.parts[c, k])
    for core in (1 - c, c):
        lin = r.gate_lin[core].reshape(256, HALF)
        branch = (r.headnorm[core].reshape(256, HALF) * (lin * jax.nn.sigmoid(lin))).astype(BF)
        r.branch[core] = branch.reshape(4, 64, HALF)

        @pl.loop(0, 4)
        def _(n):
            got = nt(branch, r.wide_g[n, :, :, HALF : 2 * HALF].reshape(512, HALF))
            cols = pl.ds(pl.multiple_of(n * 512, 512), 512)
            r.parts[core, :, :, cols] = got.astype(BF).reshape(4, 64, 512)

        if core is not c:
            sums.pairs()
    sums.hops()
    resid1 = r.resid[...] + sums.result()
    r.resid1[...] = resid1
    r.second_own[...] = rms(resid1, r.norm2_gain[...]).astype(BF)
    s_rows = rows_start(r.second_own, r.second, s_sems)
    rows_finish(s_rows, r.second, s_sems)
    for copy in f_far:
        copy.wait()
    for sent in (q_deal, g_deal):
        deal_done(sent)
    for sent in (gates, f_deal):
        shuffle_done(sent)
    for near in (q_near, g_near, f_near):
        for copy in near.values():
            copy.wait_send()
    for copy in q_far + g_far:
        copy.wait_send()
    scan.done()
    sums.done()


def forward(wq, wg, wf, rows_a, rows_b, packed, resid, head_gain, norm2_gain):
    square = ((4, 64, 64), F32, VMEM)
    rows = (2, 4, 64, 2048)
    scratch = dict(
        proj=pltpu.VMEM((2, 4, 64, 3 * HALF), BF),
        normed=pltpu.VMEM((2, 4, 64, HALF), F32),
        parts=pltpu.VMEM(rows, BF),
        second_own=pltpu.VMEM((64, 2048), BF),
        q_send=DMA((2, 2)),
        q_recv=DMA((4,)),
        g_send=DMA((2, 2)),
        g_recv=DMA((4,)),
        swap_s=DMA((2,)),
        swap_r=DMA((2,)),
    )
    for name in ("rows_a_", "rows_b_", "rows_s_"):
        scratch.update(rows_sems(name))
    for name in ("q_spread", "g_spread", "f_spread"):
        scratch.update(spread_sems(name))
    for name in ("gate", "deal"):
        scratch.update(shuffle_sems(name))
    scratch.update(scan_scratch())
    scratch.update(sum_scratch("mix"))
    return remote_call(
        forward_kernel,
        1,
        dict(
            wq=(wq, ANY),
            wg=(wg, ANY),
            wf=(wf, ANY),
            rows_a=(rows_a, ANY),
            rows_b=(rows_b, ANY),
            packed=(packed, ANY),
            resid=(resid, VMEM),
            head_gain=(head_gain, VMEM),
            norm2_gain=(norm2_gain, VMEM),
        ),
        dict(
            wide_q=((4, 4, 128, 3 * HALF), BF, VMEM),
            wide_g=((4, 4, 128, 2 * HALF), BF, VMEM),
            wide_f=((4, 4, 128, FFN), BF, ANY),
            first=(rows, BF, VMEM),
            cot=(rows, BF, ANY),
            second=(rows, BF, VMEM),
            gates=((4, 4, 64, 64), F32, VMEM),
            qkv=((2, 4, 64, 3 * HALF), BF, VMEM),
            cum=square,
            near=square,
            far=square,
            probs=square,
            mixing=square,
            decays=((4, SLOTS, 128), F32, VMEM),
            states=((4, SLOTS, 1024), F32, VMEM),
            mixed=((4, 64, DK), F32, VMEM),
            gate_lin=((2, 4, 64, HALF), F32, VMEM),
            headnorm=((2, 4, 64, HALF), F32, VMEM),
            branch=((2, 4, 64, HALF), BF, VMEM),
            resid1=((64, 2048), F32, VMEM),
        ),
        scratch,
    )


class WeightSum:
    def __init__(self, r, name, grads, cols, loaded):
        self.grads, self.cols, self.half, self.loaded = grads, cols, cols // 2, loaded
        self.far, self.landed, self.ready = sems_of(r, name + "b", 3)
        self.own = getattr(r, name + "own") if loaded else None
        self.sems = sems_of(r, name + "s", 4)
        self.own_sem = getattr(r, name + "own_s") if loaded else None
        self.fars, self.nears, self.owns = {}, {}, {}

    def part(self, side):
        return pl.ds(side * self.half, self.half)

    def block(self, side, k, d):
        x, y, z, c = here()
        if side == 0:
            return self.grads.at[wrap(x + d), wrap(y + k), :, self.part(0)]
        return self.grads.at[wrap(x + k), wrap(y + d), :, self.part(1)]

    def peer(self, side, d):
        x, y, z, c = here()
        return (wrap(x + d), y, z, c) if side == 0 else (x, wrap(y + d), z, c)

    def mine(self, side, k):
        return self.own.at[side, k] if self.loaded else self.block(side, k, 0)

    def load(self):
        if self.loaded:
            for k in (1, 2, 3, 0):
                for side in range(2):
                    self.owns[side, k] = pltpu.make_async_copy(
                        self.block(side, k, 0), self.own.at[side, k], self.own_sem.at[side, k]
                    )
                    self.owns[side, k].start()

    def send(self, k):
        for d in range(1, 4):
            for side in range(2):
                self.fars[side, k, d] = push(
                    self.block(side, k, d),
                    self.far.at[side, k, d - 1],
                    self.sems[0].at[side, k, d - 1],
                    self.sems[1].at[side, k, d - 1],
                    self.peer(side, d),
                )

    def arrive(self, side, k):
        if self.loaded:
            self.owns[side, k].wait()
        for d in range(1, 4):
            self.fars[side, k, d].wait_recv()

    def total(self, side, k, rows):
        value = self.mine(side, k)[rows, :].astype(F32)
        for d in range(3):
            value = value + self.far[side, k, d, rows, :].astype(F32)
        return value

    def turn(self, k):
        for side in range(2):
            self.arrive(side, k)

            @pl.loop(0, 8)
            def _(t):
                rows = pl.ds(pl.multiple_of(t * 16, 16), 16)
                self.mine(side, k)[rows, :] = self.total(side, k, rows).astype(BF)

            self.nears[side, k] = push(
                self.mine(side, k),
                self.landed.at[side, k - 1],
                self.sems[2].at[side, k - 1],
                self.sems[3].at[side, k - 1],
                self.peer(1 - side, k),
            )

    def finish(self):
        for side in range(2):
            self.arrive(side, 0)
            for k in range(1, 4):
                self.nears[side, k].wait_recv()

            @pl.loop(0, 8)
            def _(t):
                rows = pl.ds(pl.multiple_of(t * 16, 16), 16)
                value = self.total(side, 0, rows)
                for k in range(3):
                    value = value + self.landed[side, k, rows, :].astype(F32)
                self.ready[rows, self.part(side)] = value.astype(BF)

    def done(self):
        for copy in list(self.fars.values()) + list(self.nears.values()):
            copy.wait_send()


def weight_scratch(name, cols, loaded):
    half = cols // 2
    out = {
        f"{name}b0": pltpu.VMEM((2, 4, 3, 128, half), BF),
        f"{name}b1": pltpu.VMEM((2, 3, 128, half), BF),
        f"{name}b2": pltpu.VMEM((128, cols), BF),
        f"{name}s0": DMA((2, 4, 3)),
        f"{name}s1": DMA((2, 4, 3)),
        f"{name}s2": DMA((2, 3)),
        f"{name}s3": DMA((2, 3)),
    }
    if loaded:
        out[f"{name}own"] = pltpu.VMEM((2, 4, 128, half), BF)
        out[f"{name}own_s"] = DMA((2, 4))
    return out


def return_start(ready, out, send, recv):
    x, y, z, c = here()
    dst, arrived = out.at[lax.rem(z, 2), c], recv.at[lax.rem(z, 2), c]
    sent = []
    for k in range(4):
        src = ready.at[pl.ds(k * 32, 32), :]
        same = jnp.logical_and(k == z, c == z // 2)
        copy = pltpu.make_async_remote_copy(
            src_ref=src,
            dst_ref=dst,
            send_sem=send.at[k],
            recv_sem=arrived,
            device_id=(x, y, k, z // 2),
            device_id_type=MESH,
        )

        @pl.when(same)
        def _():
            pltpu.make_async_copy(src, dst, arrived).start()

        @pl.when(jnp.logical_not(same))
        def _():
            copy.start()

        sent.append((same, copy))
    return sent


def return_wait(ready, out, recv):
    for j in range(2):
        for k in range(2):
            pltpu.make_async_copy(ready.at[pl.ds(0, 32), :], out.at[j, k], recv.at[j, k]).wait()


class SmallSum:
    def __init__(self, r, name, src, out):
        self.src, self.out = src, out
        self.held, self.now = sems_of(r, name + "b", 2)
        self.sems = sems_of(r, name + "s", 4)
        self.sends = []

    def half(self, k):
        width = self.src.shape[1] // 2
        return pl.ds(pl.multiple_of(k * width, 128), width)

    def pair(self):
        x, y, z, c = here()
        self.copy = push(
            self.src.at[:, self.half(1 - c)],
            self.held.at[0, c],
            self.sems[0].at[0],
            self.sems[1].at[0],
            (x, y, z, 1 - c),
        )
        self.held[0, c] = self.src[:, self.half(c)]

    def send(self, stage):
        x, y, z, c = here()
        if stage == 0:
            self.copy.wait()
            self.now[...] = self.held[0, 0] + self.held[0, 1]
        else:
            self.collect(stage)
        at = (z, y, x)[stage]
        self.held[stage + 1, at] = self.now[...]
        self.sent = []
        for d in range(1, 4):
            peer = [x, y, z, c]
            peer[2 - stage] = wrap(at + d)
            self.sent.append(
                push(
                    self.held.at[stage + 1, at],
                    self.held.at[stage + 1, at],
                    self.sems[2].at[stage, d - 1],
                    self.sems[3].at[stage, d - 1],
                    tuple(peer),
                )
            )

    def collect(self, stage):
        for copy in self.sent:
            copy.wait()
        value = self.held[stage, 0]
        for k in range(1, 4):
            value = value + self.held[stage, k]
        self.now[...] = value

    def close(self):
        x, y, z, c = here()
        self.collect(3)
        self.out[:, self.half(c)] = self.now[...]
        self.copy = push(
            self.now,
            self.out.at[:, self.half(c)],
            self.sems[0].at[1],
            self.sems[1].at[1],
            (x, y, z, 1 - c),
        )

    def done(self):
        self.copy.wait()


def small_scratch(name, rows, cols):
    return {
        f"{name}b0": pltpu.VMEM((4, 4, rows, cols // 2), F32),
        f"{name}b1": pltpu.VMEM((rows, cols // 2), F32),
        f"{name}s0": DMA((2,)),
        f"{name}s1": DMA((2,)),
        f"{name}s2": DMA((3, 3)),
        f"{name}s3": DMA((3, 3)),
    }


def backward_kernel(r):
    x, y, z, c = here()
    partner = (x, y, z, 1 - c)
    scan = Scan(r, True)
    greet(all_peers() + scan.senders())
    second = RowSum(r, "sec", r.second_part, lambda k: r.second_mine[k])
    ffn = RowSum(r, "ffn", r.ffn_part, lambda k: r.ffn_mine[k])
    one = WeightSum(r, "one", r.grads_one, 6 * HALF, True)
    two = WeightSum(r, "two", r.grads_two, 3 * HALF, True)
    tail = WeightSum(r, "tail", r.grads_tail, 2 * HALF, False)
    last = WeightSum(r, "last", r.grads_last, 3 * HALF, False)
    second.pairs()
    mine = [
        pltpu.make_async_copy(part.at[c], dst, r.mine_s.at[n])
        for n, (part, dst) in enumerate(
            ((r.second_part, r.second_mine), (r.ffn_part, r.ffn_mine))
        )
    ]
    for copy in mine:
        copy.start()
    one.load()
    for k in (1, 2, 3, 0):
        one.send(k)
    for copy in mine:
        copy.wait()
    second.hops()
    two.load()
    for k in (1, 2, 3, 0):
        two.send(k)
    ffn.pairs()
    e = second.result()
    v = r.resid1[...]
    grad, d_norm2 = rms_back(v, r.norm2_gain[...], e)
    r.small[...] = jnp.zeros_like(r.small)
    r.small[17:18, 0:2048] = d_norm2
    grad_resid1 = r.cot_own[...].astype(F32) + grad
    r.attn_own[...] = grad_resid1.astype(BF)
    r.grad_resid1[...] = grad_resid1
    a_sems = sems_of(r, "rows_a_", 5)
    a_rows = rows_start(r.attn_own, r.attn, a_sems)
    ffn.hops()
    rows_finish(a_rows, r.attn, a_sems)

    attn = r.attn[...].reshape(512, 2048)
    grad_branch = dot(attn, r.wide_g[:, :, :, HALF : 2 * HALF].reshape(2048, HALF))
    lin = r.gate_lin[...].reshape(512, HALF)
    sig = jax.nn.sigmoid(lin)
    normed = r.headnorm[...].reshape(512, HALF)
    r.grad_lin[...] = (
        (grad_branch * normed * sig * (1 + lin * (1 - sig))).astype(BF).reshape(2, 4, 64, HALF)
    )
    r.grad_out[...] = (grad_branch * lin * sig).reshape(2, 4, 64, HALF)
    swap = push(r.grad_out.at[1 - c], r.grad_norm.at[c], r.swap_s.at[0], r.swap_r.at[0], partner)
    r.grad_norm[c] = r.grad_out[c]
    swap.wait()

    def all_rows(ref):
        return ref[...].reshape(512, ref.shape[-1])

    def weight_rows(ref, n):
        return ref[:, :, :, pl.ds(pl.multiple_of(n * 512, 512), 512)].reshape(512, 512)

    r.d_head[...] = jnp.zeros_like(r.d_head)

    @pl.loop(0, 4)
    def _(n):
        mixed = r.mixed[n]
        e = jnp.concatenate([r.grad_norm[0, n], r.grad_norm[1, n]], axis=1)
        grad, d_head = rms_back(mixed, r.head_gain[...], e)
        r.d_head[0:1] += d_head
        g = grad.astype(BF)
        r.grad_mixed[n] = g
        dmix, dfar, dnear, dscore, ends_k, ends_v = chunk_back(
            features(r.qkv, n, 0),
            features(r.qkv, n, 2),
            g,
            r.cum[n],
            r.gates[n, 1],
            r.gates[n, 3],
            r.probs[n],
            r.states[n],
        )
        r.dmix[n], r.dfar[n], r.dnear[n], r.dscore[n] = dmix, dfar, dnear, dscore
        r.every[c, n] = jnp.concatenate([ends_k, ends_v, r.decays[n]], axis=1)

    scan.pair()
    r.small[18:19, 0:512] = r.d_head[0:1]
    scan.send()

    @pl.loop(0, 4)
    def _(n):
        r.grads_tail[n, :, :, 0:HALF] = (
            tn(weight_rows(r.first, n), all_rows(r.grad_lin)).astype(BF).reshape(4, 128, HALF)
        )
        r.grads_tail[n, :, :, HALF : 2 * HALF] = (
            tn(weight_rows(r.attn, n), all_rows(r.branch)).astype(BF).reshape(4, 128, HALF)
        )

    scan.fold(r.nexts)
    for k in (1, 2, 3, 0):
        tail.send(k)

    @pl.loop(0, 4)
    def _(n):
        dq, dk, dv, dlogit = chunk_last(
            features(r.qkv, n, 0),
            features(r.qkv, n, 1),
            features(r.qkv, n, 2),
            r.grad_mixed[n],
            r.gates[n, 0],
            r.gates[n, 1],
            r.gates[n, 2],
            r.gates[n, 3],
            r.cum[n],
            r.near[n],
            r.far[n],
            r.probs[n],
            r.mixing[n],
            r.states[n],
            r.dmix[n],
            r.dfar[n],
            r.dnear[n],
            r.dscore[n],
            r.nexts[n],
        )
        for m, part in enumerate((dq, dk, dv)):
            for s in range(2):
                r.dproj[s, n, :, pl.ds(m * HALF, HALF)] = part[
                    :, s * HALF : (s + 1) * HALF
                ].astype(BF)
        r.dlogit[n] = dlogit

    swap2 = push(r.dproj.at[1 - c], r.dqkv.at[c], r.swap_s.at[1], r.swap_r.at[1], partner)
    r.dqkv[c] = r.dproj[c]
    logits = shuffle_start(lambda k: r.dlogit.at[k], r.dl.at[z], *sems_of(r, "gate", 3))
    swap2.wait()

    first_part = r.attn
    first = RowSum(r, "fst", first_part, lambda k: first_part[c, k])
    for core in (1 - c, c):

        @pl.loop(0, 4)
        def _(n):
            got = nt(
                r.dqkv[core].reshape(256, 3 * HALF), r.wide_q[n].reshape(512, 3 * HALF)
            ) + nt(
                r.grad_lin[core].reshape(256, HALF),
                r.wide_g[n, :, :, 0:HALF].reshape(512, HALF),
            )
            cols = pl.ds(pl.multiple_of(n * 512, 512), 512)
            first_part[core, :, :, cols] = got.astype(BF).reshape(4, 64, 512)

        if core is not c:
            first.pairs()

    first.hops()

    @pl.loop(0, 4)
    def _(n):
        r.grads_last[n] = (
            tn(weight_rows(r.first, n), all_rows(r.dqkv)).astype(BF).reshape(4, 128, 3 * HALF)
        )

    for k in (1, 2, 3, 0):
        last.send(k)
    for k in range(1, 4):
        one.turn(k)
    for k in range(1, 4):
        two.turn(k)
    for k in range(1, 4):
        tail.turn(k)

    shuffle_wait(logits)
    low = jnp.zeros((64, 16), F32)
    bias = []
    for h in range(4):
        dl = r.dl[h]
        low = low + nt(dl, r.up[h], HIGH)
        r.small[0:16, 2048 + h * 64 : 2112 + h * 64] = tn(r.lowrank[...], dl, HIGH)
        bias.append(jnp.sum(dl, axis=0, keepdims=True))
    r.small[18:19, 512:768] = jnp.concatenate(bias, axis=1)
    r.small[0:16, 0:2048] = tn(low, r.first_own[...].astype(F32), HIGH)
    small = SmallSum(r, "sml", r.small, r.small_out)
    small.pair()
    small.send(0)
    grad_first = first.result() + dot(low, r.down[...], precision=HIGH)
    grad, d_norm1 = rms_back(r.resid[...], r.norm1_gain[...], grad_first)
    r.d_inputs[...] = r.grad_resid1[...] + grad
    r.tiny[...] = jnp.zeros_like(r.tiny)
    r.tiny[0:1, :] = d_norm1
    tiny = SmallSum(r, "tny", r.tiny, r.tiny_out)
    tiny.pair()
    tiny.send(0)
    one.finish()
    one_back = shuffle_start(
        lambda k: one.ready.at[pl.ds(pl.multiple_of(k * 32, 32), 32), :],
        r.out_one.at[z],
        *sems_of(r, "back_one", 3),
    )
    two.finish()
    two_back = shuffle_start(
        lambda k: two.ready.at[pl.ds(pl.multiple_of(k * 32, 32), 32), :],
        r.out_two.at[z],
        *sems_of(r, "back_two", 3),
    )
    small.send(1)
    tiny.send(1)
    tail.finish()
    tail_back = return_start(tail.ready, r.out_tail, r.tail_send, r.tail_recv)
    r.output[...] = (r.resid1[...] + ffn.result()).astype(BF)
    for k in range(1, 4):
        last.turn(k)
    small.send(2)
    tiny.send(2)
    last.finish()
    last_back = return_start(last.ready, r.out_last, r.last_send, r.last_recv)
    small.close()
    tiny.close()
    for sent in (one_back, two_back):
        shuffle_wait(sent)
        shuffle_done(sent)
    shuffle_done(logits)
    return_wait(tail.ready, r.out_tail, r.tail_recv)
    return_wait(last.ready, r.out_last, r.last_recv)
    deal_done(tail_back)
    deal_done(last_back)
    small.done()
    tiny.done()
    for part in (second, ffn, first, one, two, tail, last, scan):
        part.done()


def backward(operands):
    rows = (2, 4, 64, 2048)
    small = pltpu.VMEM((4, 64, 64), F32)
    scratch = dict(
        small=pltpu.VMEM((24, 2304), F32),
        tiny=pltpu.VMEM((8, 2048), F32),
        attn_own=pltpu.VMEM((64, 2048), BF),
        grad_resid1=pltpu.VMEM((64, 2048), F32),
        attn=pltpu.VMEM(rows, BF),
        grad_lin=pltpu.VMEM((2, 4, 64, HALF), BF),
        grad_out=pltpu.VMEM((2, 4, 64, HALF), F32),
        grad_norm=pltpu.VMEM((2, 4, 64, HALF), F32),
        grad_mixed=pltpu.VMEM((4, 64, DK), BF),
        d_head=pltpu.VMEM((8, DK), F32),
        dmix=small,
        dfar=small,
        dnear=small,
        dscore=small,
        dlogit=small,
        dl=small,
        nexts=pltpu.VMEM((4, SLOTS, 1024), F32),
        dproj=pltpu.VMEM((2, 4, 64, 3 * HALF), BF),
        dqkv=pltpu.VMEM((2, 4, 64, 3 * HALF), BF),
        second_mine=pltpu.VMEM((4, 64, 2048), BF),
        ffn_mine=pltpu.VMEM((4, 64, 2048), BF),
        mine_s=DMA((2,)),
        grads_tail=pltpu.VMEM((4, 4, 128, 2 * HALF), BF),
        grads_last=pltpu.VMEM((4, 4, 128, 3 * HALF), BF),
        swap_s=DMA((2,)),
        swap_r=DMA((2,)),
        tail_send=DMA((4,)),
        tail_recv=DMA((2, 2)),
        last_send=DMA((4,)),
        last_recv=DMA((2, 2)),
    )
    for name, cols, loaded in (
        ("one", 6 * HALF, True),
        ("two", 3 * HALF, True),
        ("tail", 2 * HALF, False),
        ("last", 3 * HALF, False),
    ):
        scratch.update(weight_scratch(name, cols, loaded))
    for name in ("sec", "ffn", "fst"):
        scratch.update(sum_scratch(name))
    for name in ("gate", "back_one", "back_two"):
        scratch.update(shuffle_sems(name))
    scratch.update(rows_sems("rows_a_"))
    scratch.update(scan_scratch())
    scratch.update(small_scratch("sml", 24, 2304))
    scratch.update(small_scratch("tny", 8, 2048))
    in_hbm = ("grads_one", "grads_two", "second_part", "ffn_part")
    return remote_call(
        backward_kernel,
        2,
        {name: (value, ANY if name in in_hbm else VMEM) for name, value in operands.items()},
        dict(
            output=((64, 2048), BF, VMEM),
            d_inputs=((64, 2048), F32, VMEM),
            out_last=((2, 2, 32, 3 * HALF), BF, VMEM),
            out_tail=((2, 2, 32, 2 * HALF), BF, VMEM),
            out_one=((4, 32, 6 * HALF), BF, VMEM),
            out_two=((4, 32, 3 * HALF), BF, VMEM),
            small_out=((24, 2304), F32, VMEM),
            tiny_out=((8, 2048), F32, VMEM),
        ),
        scratch,
    )


def rms(v, gain):
    return v * lax.rsqrt(jnp.mean(v * v, axis=-1, keepdims=True) + EPS) * gain


def rms_back(v, gain, e):
    r = lax.rsqrt(jnp.mean(v * v, axis=-1, keepdims=True) + EPS)
    grad = r * gain * e - v * (r * r * r) * jnp.mean(v * gain * e, axis=-1, keepdims=True)
    return grad, jnp.sum(e * v * r, axis=0, keepdims=True)


def body(
    inputs,
    offsets,
    norm1_gain,
    query_weight,
    key_weight,
    value_weight,
    gate_weight,
    out_weight,
    low_down,
    low_up,
    forget_bias,
    head_gain,
    norm2_gain,
    ffn_gate,
    ffn_up,
    ffn_down,
    cotangent,
):
    core = lax.axis_index("c")

    def dealt(weights):
        out = jnp.stack([w.reshape(32, 2, 2, HALF) for w in weights], axis=3)
        return out.transpose(1, 2, 0, 3, 4).reshape(2, 2, 32, len(weights) * HALF)

    wq = dealt((query_weight, key_weight, value_weight))
    wg = dealt((gate_weight, out_weight.T))
    wf = jnp.stack([w.reshape(32, 4, UNITS) for w in (ffn_gate, ffn_up, ffn_down)], axis=2)
    wf = jnp.pad(wf, ((0, 0), (0, 0), (0, 0), (0, UNITS_PAD - UNITS)))
    wf = wf.transpose(1, 0, 2, 3).reshape(4, 32, FFN)
    resid = inputs.astype(F32)
    gain1, gain2, gain_head = norm1_gain[None], norm2_gain[None], head_gain[None]
    first_own = rms(resid, gain1).astype(BF)

    lowrank = dot(first_own, low_down)
    up = low_up.astype(F32)
    logits = (dot(lowrank, up, precision=HIGH) + forget_bias).astype(BF).astype(F32)
    lam = jax.nn.log_sigmoid(logits) / 8.0
    offs = lax.dynamic_slice_in_dim(offsets, core * 64, 64, 0).astype(F32)
    offs = jnp.broadcast_to(offs[:, None], (64, 256))
    packed = jnp.stack([lam, -jnp.expm1(lam), jax.nn.sigmoid(-logits) / 8.0, offs])
    packed = packed.reshape(4, 64, 4, SLOTS).transpose(2, 0, 1, 3)

    f = forward(wq, wg, wf, first_own, cotangent, packed, resid, gain_head, gain2)

    second, cot = f["second"].reshape(512, 2048), f["cot"].reshape(512, 2048)
    wide_f = f["wide_f"].reshape(2048, FFN)
    w_gate, w_up, w_down = (wide_f[:, n * UNITS_PAD : (n + 1) * UNITS_PAD] for n in range(3))
    act_gate, act_up = dot(second, w_gate), dot(second, w_up)
    sig = jax.nn.sigmoid(act_gate)
    silu = act_gate * sig
    hidden = (silu * act_up).astype(BF)
    grad_hidden = dot(cot, w_down)
    grad_gate = (grad_hidden * act_up * sig * (1 + act_gate * (1 - sig))).astype(BF)
    grad_up = (grad_hidden * silu).astype(BF)
    ffn_part = nt(hidden, w_down).astype(BF).reshape(2, 4, 64, 2048)
    grad_acts = jnp.concatenate([grad_gate, grad_up], axis=1)
    second_part = nt(grad_acts, wide_f[:, : 2 * UNITS_PAD]).astype(BF).reshape(2, 4, 64, 2048)
    grads_one = tn(second, grad_acts).astype(BF).reshape(4, 4, 128, 2 * UNITS_PAD)
    grads_two = tn(cot, hidden).astype(BF).reshape(4, 4, 128, UNITS_PAD)

    done = ("wide_f", "cot", "second")
    operands = {name: value for name, value in f.items() if name not in done}
    operands.update(
        grads_one=grads_one,
        grads_two=grads_two,
        second_part=second_part,
        ffn_part=ffn_part,
        cot_own=cotangent,
        resid=resid,
        first_own=first_own,
        lowrank=lowrank,
        up=up.reshape(16, 4, SLOTS).transpose(1, 0, 2),
        down=low_down.astype(F32).T,
        norm1_gain=gain1,
        norm2_gain=gain2,
        head_gain=gain_head,
    )
    b = backward(operands)

    def owned(value, count):
        value = value.reshape(2, 2, 32, count, HALF).transpose(3, 2, 0, 1, 4)
        return value.reshape(count, 32, 1024).astype(F32)

    def units(value, count):
        value = value.reshape(4, 32, count, UNITS_PAD)[..., :UNITS].transpose(2, 1, 0, 3)
        return value.reshape(count, 32, 4 * UNITS).astype(F32)

    last, tail = owned(b["out_last"], 3), owned(b["out_tail"], 2)
    one, two = units(b["out_one"], 2), units(b["out_two"], 1)
    small, tiny = b["small_out"], b["tiny_out"]
    return (
        b["output"],
        b["d_inputs"],
        tiny[0],
        last[0],
        last[1],
        last[2],
        tail[0],
        tail[1].T,
        small[0:16, 0:2048].T,
        small[0:16, 2048:2304],
        small[18, 512:768],
        small[18, 0:512],
        small[17, 0:2048],
        one[0],
        one[1],
        two[0],
    )


def solution(mesh):
    fine = Mesh(mesh.devices.reshape(4, 4, 4, 2), ("x", "y", "z", "c"))
    seq = ("x", "y", "z")
    rows = P(("x", "y", "z", "c"), None)
    wide = P(seq, "c")
    placed = (
        (rows, P(seq), P())
        + (wide,) * 4
        + (P("c", seq), P(), P(), P(), P(), P(), wide, wide, wide, rows)
    )
    return jax.shard_map(
        body,
        mesh=fine,
        in_specs=placed,
        out_specs=(rows, rows, P())
        + (wide,) * 4
        + (P("c", seq), P(), P(), P(), P(), P(), wide, wide, wide),
        check_vma=False,
    )
```

time: 3280 us -> 382 us (0.12); the launches traced: 3220 us -> 375 us
  waiting for transfers between devices: 1810 us -> 0 us
  blocking collectives: 764 us -> 0 us
  Pallas kernels: 0 us -> 311 us
  other arithmetic: 238 us -> 7.87 us
  matrix products: 229 us -> 29.5 us
  local copies, waits for them, and re-layouts: 146 us -> 24.7 us
    reduce_scatter x4 -> x0, waiting for transfers between devices: 759 us -> none  [the longest x1 402 us: body(): lax.psum_scatter(grad_up_cols, 'seq', scatter_dimension=0, tiled=True)]
    all_gather x12 -> x0, waiting for transfers between devices: 499 us -> none  [the longest x2 111 us: entering(): pieces = jax.tree.map(lambda part: lax.all_gather(part, axis), value)]
    psum x1 -> x0, blocking collectives: 464 us -> none  [body(): lax.psum((grad_norm1, grad_norm2, grad_head, grad_low_down, grad_low_up,...]
    unnamed x23 -> x0, waiting for transfers between devices: 407 us -> none
    pallas_call x0 -> x2, Pallas kernels: none -> 311 us  [remote_call(): pl.pallas_call(run, out_shape=[jax.ShapeDtypeStruct(shape, dtype) for sha...]
    all_gather x4 -> x0, blocking collectives: 300 us -> none  [the longest x1 148 us: carried_in(): lax.all_gather(part.astype(kind), axis)]
    dot_general x90 -> x9, matrix products: 229 us -> 29.5 us  [dot(): lax.dot_general(left, right, (dims, ((), ())), precision=precision, prefe...]
    psum x3 -> x0, waiting for transfers between devices: 148 us -> none  [the longest x1 107 us: body(): lax.psum((grad_norm1, grad_norm2, grad_head, grad_low_down, grad_low_up,...]
  transfers between devices with their start and end apart: 21 -> 0, of which waited for: 13 -> 0; matrix products, arithmetic and copies ran while one was open for 14% -> 0% of each run, Pallas kernels for 0% -> 0%
where the time goes in v2:
time: 382 us; the launch traced here: 375 us
  Pallas kernels  311 us (81%)
  matrix products  29.5 us (8%)
  local copies, waits for them, and re-layouts  24.7 us (6%)
  other arithmetic  7.87 us (2%)
    pallas_call x2, Pallas kernels, remote_call(): pl.pallas_call(run, out_shape=[jax.ShapeDtypeStruct(shape, dtype) for sha...  311 us
    dot_general x9, matrix products, dot(): lax.dot_general(left, right, (dims, ((), ())), precision=precision, prefe...  29.5 us

profile of v2, /device:TPU:1, one launch (start us, length us, event | category | flops | bytes accessed | tf_op | source)
XLA Modules:
  0.0 374.9 jit_solution(10472283452216725587)
XLA Ops:
  0.7 0.8 dynamic-slice_convert_fusion
  1.5 1.1 multiply_reduce_fusion
  2.6 1.1 multiply_convert_fusion.3.refs_3_.refs_23_
  3.8 1.1 fusion.28
  4.9 1.0 fusion.22
  6.3 0.8 maximum_bitcast_fusion.refs_5_
  7.2 0.9 convert_element_type.79.refs_6_.refs_22_
  9.8 1.5 fusion.20
  11.3 1.4 reshape.125.refs_2_
  13.7 0.9 reshape.123.refs_0_
  15.2 0.7 reshape.124.refs_1_
  15.9 155.5 %shard_map.288 = (bf16[4,4,128,768]{3,2,1,0:T(8,128)(2,1)}, bf16[4,4,128,512]{3,2,1,0:T(8,128)(2,1)}, bf16[4,4,128,2304]{3,2,1,0:T(8,128)(2,1)}, bf16[2,4,64,204...) custom-call(bf16[2,2,32,768]{3,2,1,0:T(8,128)(2,1)} %reshape.123.ref, ...), custom_call_target="tpu_custom_call" | custom-call | tf_op jit(solution)/shard_map/pallas_call | solution.py:81
  171.4 4.5 %fusion.2 = f32[512,768]{1,0:T(8,128)S(1)} fusion(bf16[512,2048]{1,0:T(8,128)(2,1)} %bitcast.77, bf16[2048,2304]{1,0:T(8,128)(2,1)} %bitcast.72), kind=kOutput, calls=%fused_computation.4 | convolution fusion | flops 1610612736 | bytes 6815744 | tf_op jit(solution)/shard_map/dot_general | solution.py:32
  175.9 0.8 copy-done.18
  176.7 3.5 fusion.10
  180.2 2.2 multiply_convert_fusion
  182.4 3.1 convolution_convert_fusion.2
  185.6 4.7 %fusion.6 = bf16[512,2048]{1,0:T(8,128)(2,1)} fusion(bf16[2048,2304]{1,0:T(8,128)(2,1)S(1)} %bitcast.76, bf16[512,768]{1,0:T(8,128)(2,1)S(1)} %get-tuple-element.74, bf16[512,768]{1,0:T(8,128)(2,1)S(1)} %get-tuple-element.73), kind=kOutput, calls=%fused_computation.8 | convolution fusion | flops 3225419776 | bytes 9961472 | tf_op jit(solution)/shard_map/dot_general | solution.py:32
  190.2 3.6 convolution_convert_fusion.1
  193.8 5.8 %convolution_convert_fusion = bf16[2048,1536]{1,0:T(8,128)(2,1)} fusion(bf16[512,2048]{1,0:T(8,128)(2,1)S(1)} %bitcast.79, bf16[512,768]{1,0:T(8,128)(2,1)S(1)} %get-tuple-element.74, bf16[512,768]{1,0:T(8,128)(2,1)S(1)} %get-tuple-element.73), kind=kOutput, calls=%fused_computation | convolution fusion | flops 3227516928 | bytes 9961472 | tf_op jit(solution)/shard_map/dot_general | solution.py:32
  201.7 155.9 %shard_map.289 = (bf16[64,2048]{1,0:T(8,128)(2,1)}, f32[64,2048]{1,0:T(8,128)}, bf16[2,2,32,768]{3,2,1,0:T(8,128)(2,1)}, bf16[2,2,32,512]{3,2,1,0:T(8,128)(2,1)}...) custom-call(bf16[4,4,128,768]{3,2,1,0:T(8,128)(2,1)} %get-tuple-element.44, ...), custom_call_target="tpu_custom_call" | custom-call | tf_op jit(solution)/shard_map/pallas_call | solution.py:81
  357.5 1.1 reshape.134
  359.8 1.0 squeeze.43
  361.1 1.0 squeeze.44
  362.7 0.8 squeeze.35
  363.6 0.8 squeeze.36
  364.4 0.8 squeeze.37
  365.5 1.0 reshape.136
  367.0 0.8 squeeze.39
  367.9 0.8 squeeze.38
  369.9 1.4 slice.68
  373.8 0.8 copy.93
  (92 shorter events, 12.5 us)
Async XLA Ops:
  0.6 6.5 %copy-start.1 = (bf16[64,2048]{1,0:T(8,128)(2,1)S(1)}, bf16[64,2048]{1,0:T(8,128)(2,1)}, u32[]{:S(2)}) copy-start(bf16[64,2048]{1,0:T(8,128)(2,1)} %param.17) | copy-start | bytes 786436
  3.7 4.6 %copy-start = (bf16[64,2048]{1,0:T(8,128)(2,1)}, bf16[64,2048]{1,0:T(8,128)(2,1)S(1)}, u32[]{:S(2)}) copy-start(bf16[64,2048]{1,0:T(8,128)(2,1)S(1)} %multiply_convert_fusion.3.refs_3_.refs_23_) | copy-start | bytes 786436
  3.8 4.3 %copy-start.7 = (bf16[32,2816]{1,0:T(8,128)(2,1)S(1)}, bf16[32,2816]{1,0:T(8,128)(2,1)}, u32[]{:S(2)}) copy-start(bf16[32,2816]{1,0:T(8,128)(2,1)} %param.30) | copy-start | bytes 540676
  5.9 2.7 copy-start.8
  6.2 3.0 copy-start.9
  9.2 3.5 copy-start.12
  9.5 3.4 copy-start.13
  9.8 3.2 copy-start.14
  11.3 3.3 copy-start.15
  11.3 3.4 copy-start.16
  171.4 5.3 %copy-start.18 = (bf16[4,4,128,2304]{3,2,1,0:T(8,128)(2,1)S(1)}, bf16[4,4,128,2304]{3,2,1,0:T(8,128)(2,1)}, u32[]{:S(2)}) copy-start(bf16[4,4,128,2304]{3,2,1,0:T(8,128)(2,1)} %get-tuple-element.63) | copy-start | bytes 28311556
  176.7 3.5 copy-start.19
  185.6 4.7 %copy-start.20 = (bf16[2,4,64,2048]{3,2,1,0:T(8,128)(2,1)S(1)}, bf16[2,4,64,2048]{3,2,1,0:T(8,128)(2,1)}, u32[]{:S(2)}) copy-start(bf16[2,4,64,2048]{3,2,1,0:T(8,128)(2,1)} %get-tuple-element.62) | copy-start | bytes 6291460
  193.8 6.5 %copy-start.4 = (bf16[2048,16]{0,1:T(8,128)(2,1)S(1)}, bf16[2048,16]{0,1:T(8,128)(2,1)}, u32[]{:S(2)}) copy-start(bf16[2048,16]{0,1:T(8,128)(2,1)} %param.25) | copy-start | bytes 196612
  193.8 7.2 %copy-start.17 = (bf16[16,256]{1,0:T(8,128)(2,1)S(1)}, bf16[16,256]{1,0:T(8,128)(2,1)}, u32[]{:S(2)}) copy-start(bf16[16,256]{1,0:T(8,128)(2,1)} %param.26) | copy-start | bytes 24580
  358.9 3.1 copy-start.6
  361.1 4.1 %copy-start.5 = (bf16[4,32,768]{2,1,0:T(8,128)(2,1)S(1)}, bf16[4,32,768]{2,1,0:T(8,128)(2,1)}, u32[]{:S(2)}) copy-start(bf16[4,32,768]{2,1,0:T(8,128)(2,1)} %get-tuple-element.71) | copy-start | bytes 589828
  362.3 4.2 %copy-start.10 = (bf16[2,2,32,512]{3,2,1,0:T(8,128)(2,1)S(1)}, bf16[2,2,32,512]{3,2,1,0:T(8,128)(2,1)}, u32[]{:S(2)}) copy-start(bf16[2,2,32,512]{3,2,1,0:T(8,128)(2,1)} %get-tuple-element.68) | copy-start | bytes 393220
  365.2 3.4 copy-start.11
  365.2 7.9 %copy-start.3 = (bf16[64,2048]{1,0:T(8,128)(2,1)S(1)}, bf16[64,2048]{1,0:T(8,128)(2,1)}, u32[]{:S(2)}) copy-start(bf16[64,2048]{1,0:T(8,128)(2,1)} %get-tuple-element.101) | copy-start | bytes 786436
  365.2 8.6 %copy-start.2 = (f32[64,2048]{1,0:T(8,128)S(1)}, f32[64,2048]{1,0:T(8,128)}, u32[]{:S(2)}) copy-start(f32[64,2048]{1,0:T(8,128)} %get-tuple-element.102) | copy-start | bytes 1572868

commit v3 on v2

--- a/solution.py
+++ b/solution.py
@@ -14,7 +14,6 @@
 HALF = 256
 UNITS = 704
 UNITS_PAD = 768
-REACH = 8
 EPS = 1e-06
 SCALE = 0.125
 BF = jnp.bfloat16
@@ -54,7 +53,10 @@
     barrier = pltpu.get_barrier_semaphore()
     for peer in peers:
         pl.semaphore_signal(barrier, inc=1, device_id=peer, device_id_type=MESH)
-    pl.semaphore_wait(barrier, len(peers))
+
+
+def greeted(peers):
+    pl.semaphore_wait(pltpu.get_barrier_semaphore(), len(peers))
 
 
 def push(src, dst, send, recv, peer):
@@ -321,19 +323,26 @@
 class Scan:
     def __init__(self, r, back):
         self.back, self.every = back, r.every
-        self.total, self.sending, self.landed, self.entry = r.total, r.scan_out, r.scan_in, r.entry
-        self.sems = sems_of(r, "scan", 6)
+        self.total, self.rows, self.cols, self.entry = r.total, r.scan_y, r.scan_x, r.entry
+        self.lead_b, self.lead_a = r.lead_b, r.lead_a
+        self.sems = sems_of(r, "scan", 8)
         self.order = [(n, k) for n in range(4) for k in range(2)]
+        self.line = list(range(4))
         if back:
-            self.order = self.order[::-1]
-
-    def member(self, d):
-        x, y, z, c = here()
-        at = lax.rem(x * 4 + y + (-d if self.back else d) + 32, 16)
-        return (at // 4, lax.rem(at, 4), z, c)
-
-    def senders(self):
-        return [self.member(-d) for d in range(1, REACH + 1)]
+            self.order, self.line = self.order[::-1], self.line[::-1]
+
+    def before(self, other, mine):
+        return (other > mine) if self.back else (other < mine)
+
+    def pack(self, block, state, decay):
+        block[:, 0:512] = state.astype(BF)
+        high = decay.astype(BF)
+        block[:, 512:640] = high
+        block[:, 640:768] = (decay - high.astype(F32)).astype(BF)
+
+    def unpack(self, block):
+        keep = block[:, 512:640].astype(F32) + block[:, 640:768].astype(F32)
+        return block[:, 0:512].astype(F32), keep
 
     def factor(self, k, n, width):
         return jnp.concatenate([self.every[k, n, :, 1024:1152]] * (width // 128), axis=1)
@@ -354,32 +363,54 @@
         for n, k in self.order[1:]:
             state = self.factor(k, n, DK) * state + self.every[k, n, :, half]
             decay = self.every[k, n, :, 1024:1152] * decay
-        self.sending[:, 0:512] = state.astype(BF)
-        high = decay.astype(BF)
-        self.sending[:, 512:640] = high
-        self.sending[:, 640:768] = (decay - high.astype(F32)).astype(BF)
+        self.pack(self.rows.at[y], state, decay)
         self.far = [
             push(
-                self.sending,
-                self.landed.at[d - 1],
+                self.rows.at[y],
+                self.rows.at[y],
                 self.sems[2].at[d - 1],
                 self.sems[3].at[d - 1],
-                self.member(d),
+                (x, wrap(y + d), z, c),
             )
-            for d in range(1, REACH + 1)
+            for d in range(1, 4)
+        ]
+
+    def middle(self):
+        x, y, z, c = here()
+        for copy in self.far:
+            copy.wait_recv()
+        state, decay = jnp.zeros((SLOTS, DK), F32), jnp.ones((SLOTS, 128), F32)
+        lead_b, lead_a = state, decay
+        for k in self.line:
+            term, keep = self.unpack(self.rows.at[k])
+            wide = jnp.concatenate([keep] * 4, axis=1)
+            valid = self.before(k, y)
+            lead_b = jnp.where(valid, wide * lead_b + term, lead_b)
+            lead_a = jnp.where(valid, keep * lead_a, lead_a)
+            state, decay = wide * state + term, keep * decay
+        self.lead_b[...], self.lead_a[...] = lead_b, lead_a
+        self.pack(self.cols.at[x], state, decay)
+        self.far += [
+            push(
+                self.cols.at[x],
+                self.cols.at[x],
+                self.sems[6].at[d - 1],
+                self.sems[7].at[d - 1],
+                (wrap(x + d), y, z, c),
+            )
+            for d in range(1, 4)
         ]
 
     def fold(self, out):
         x, y, z, c = here()
-        group = x * 4 + y
+        for copy in self.far[3:]:
+            copy.wait_recv()
         state = jnp.zeros((SLOTS, DK), F32)
-        for d in range(REACH, 0, -1):
-            self.far[d - 1].wait_recv()
-            valid = (group + d < 16) if self.back else (group >= d)
-            block = self.landed.at[d - 1]
-            keep = block[:, 512:640].astype(F32) + block[:, 640:768].astype(F32)
-            fresh = jnp.concatenate([keep] * 4, axis=1) * state + block[:, 0:512].astype(F32)
-            state = jnp.where(valid, fresh, 0.0)
+        for k in self.line:
+            term, keep = self.unpack(self.cols.at[k])
+            fresh = jnp.concatenate([keep] * 4, axis=1) * state + term
+            state = jnp.where(self.before(k, x), fresh, state)
+        state = jnp.concatenate([self.lead_a[...]] * 4, axis=1) * state + self.lead_b[...]
         self.total[...] = state
         self.entry[c] = state
         self.last = push(
@@ -406,11 +437,13 @@
     out = dict(
         every=pltpu.VMEM((2, 4, SLOTS, 1152), F32),
         total=pltpu.VMEM((SLOTS, DK), F32),
-        scan_out=pltpu.VMEM((SLOTS, 768), BF),
-        scan_in=pltpu.VMEM((REACH, SLOTS, 768), BF),
+        scan_y=pltpu.VMEM((4, SLOTS, 768), BF),
+        scan_x=pltpu.VMEM((4, SLOTS, 768), BF),
+        lead_b=pltpu.VMEM((SLOTS, DK), F32),
+        lead_a=pltpu.VMEM((SLOTS, 128), F32),
         entry=pltpu.VMEM((2, SLOTS, DK), F32),
     )
-    kinds = ((), (), (REACH,), (REACH,), (), ())
+    kinds = ((), (), (3,), (3,), (), (), (3,), (3,))
     out.update({f"scan{n}": DMA(shape) for n, shape in enumerate(kinds)})
     return out
 
@@ -559,14 +592,68 @@
     return dq, dk, dv, dlam * slope
 
 
+def log1p_small(u):
+    series = u * (1 - u * (1 / 2 - u * (1 / 3 - u / 4)))
+    return jnp.where(u < 0.01, series, jnp.log(1 + u))
+
+
+def one_less_exp(v):
+    series = -v * (1 + v * (1 / 2 + v * (1 / 6 + v / 24)))
+    return jnp.where(v > -0.03, series, 1 - jnp.exp(v))
+
+
+def forget_gate(logits):
+    small = jnp.exp(-jnp.abs(logits))
+    lam = (jnp.minimum(logits, 0.0) - log1p_small(small)) / 8
+    slope = jnp.where(logits >= 0, small, 1.0) / (1 + small) / 8
+    return lam, one_less_exp(lam), slope
+
+
+def prepare(r):
+    x, y, z, c = here()
+    first = rms(r.inputs[...].astype(F32), r.norm1_gain[...]).astype(BF)
+    r.first_own[...] = first
+    eye = (
+        lax.broadcasted_iota(jnp.int32, (32, 32), 0) == lax.broadcasted_iota(jnp.int32, (32, 32), 1)
+    ).astype(BF)
+    out_t = nt(eye, r.out_weight[...]).astype(BF)
+    for j in range(2):
+        for k in range(2):
+            cols = slice((2 * j + k) * HALF, (2 * j + k + 1) * HALF)
+            for n, w in enumerate((r.query_weight, r.key_weight, r.value_weight)):
+                r.wq[j, k, :, n * HALF : (n + 1) * HALF] = w[:, cols]
+            r.wg[j, k, :, 0:HALF] = r.gate_weight[:, cols]
+            r.wg[j, k, :, HALF : 2 * HALF] = out_t[:, cols]
+    lowrank = dot(first, r.low_down[...])
+    r.lowrank[...] = lowrank
+    logits = dot(lowrank, r.low_up[...].astype(F32), precision=HIGH) + r.forget_bias[...]
+    lam, write, slope = forget_gate(logits.astype(BF).astype(F32))
+    row = lax.broadcasted_iota(jnp.int32, (64, 128), 0)
+    col = lax.broadcasted_iota(jnp.int32, (64, 128), 1)
+    offs = jnp.where(col == row + 64 * c, r.offsets[...].astype(F32), 0.0)
+    offs = jnp.broadcast_to(jnp.sum(offs, axis=1, keepdims=True), (64, SLOTS))
+    for h in range(4):
+        cols = slice(h * SLOTS, (h + 1) * SLOTS)
+        for n, value in enumerate((lam, write, slope)):
+            r.packed[h, n] = value[:, cols]
+        r.packed[h, 3] = offs
+    for k in range(4):
+        for n, w in enumerate((r.ffn_gate, r.ffn_up, r.ffn_down)):
+            piece = w[:, k * UNITS : (k + 1) * UNITS]
+            pad = jnp.zeros((32, UNITS_PAD - UNITS), BF)
+            r.wf[k, :, n * UNITS_PAD : (n + 1) * UNITS_PAD] = jnp.concatenate([piece, pad], axis=1)
+
+
 def forward_kernel(r):
     x, y, z, c = here()
     partner = (x, y, z, 1 - c)
     scan = Scan(r, False)
-    greet(all_peers() + scan.senders())
+    greet(all_peers())
+    prepare(r)
+    greeted(all_peers())
     q_deal = deal_start(r.wq, r.wide_q, r.q_send, r.q_recv)
     a_sems, b_sems, s_sems = (sems_of(r, n, 5) for n in ("rows_a_", "rows_b_", "rows_s_"))
-    a_rows = rows_start(r.rows_a, r.first, a_sems)
+    a_rows = rows_start(r.first_own, r.first, a_sems)
     gates = shuffle_start(lambda k: r.packed.at[k], r.gates.at[z], *sems_of(r, "gate", 3))
     g_deal = deal_start(r.wg, r.wide_g, r.g_send, r.g_recv)
     f_deal = shuffle_start(
@@ -574,7 +661,6 @@
         r.wide_f.at[x, y, pl.ds(pl.multiple_of(z * 32, 32), 32), :],
         *sems_of(r, "deal", 3),
     )
-    b_rows = rows_start(r.rows_b, r.cot, b_sems)
     q_sems, g_sems, f_sems = (sems_of(r, n, 4) for n in ("q_spread", "g_spread", "f_spread"))
     deal_wait(r.wq, r.wide_q, r.q_recv)
     q_near = spread_near(r.wide_q, q_sems, 3 * HALF)
@@ -614,20 +700,22 @@
 
     scan.pair()
     scan.send()
+    b_rows = rows_start(r.rows_b, r.cot, b_sems)
 
     @pl.loop(0, 4)
     def _(n):
         query, key = features(r.qkv, n, 0), features(r.qkv, n, 1)
         r.near[n] = chunk_near(query, key, r.cum[n], r.gates[n, 1], r.gates[n, 3])
 
+    scan.middle()
+    f_far = spread_far(r.wide_f, f_sems, FFN, f_near, 0)
     for copy in g_far:
         copy.wait_recv()
     r.gate_lin[...] = dot(
         r.first[...].reshape(512, 2048), r.wide_g[:, :, :, 0:HALF].reshape(2048, HALF)
     ).reshape(2, 4, 64, HALF)
     scan.fold(r.states)
-    f_far = []
-    for k in range(4):
+    for k in range(1, 4):
         f_far += spread_far(r.wide_f, f_sems, FFN, f_near, k)
 
     @pl.loop(0, 4)
@@ -660,7 +748,7 @@
         if core is not c:
             sums.pairs()
     sums.hops()
-    resid1 = r.resid[...] + sums.result()
+    resid1 = r.inputs[...].astype(F32) + sums.result()
     r.resid1[...] = resid1
     r.second_own[...] = rms(resid1, r.norm2_gain[...]).astype(BF)
     s_rows = rows_start(r.second_own, r.second, s_sems)
@@ -680,7 +768,7 @@
     sums.done()
 
 
-def forward(wq, wg, wf, rows_a, rows_b, packed, resid, head_gain, norm2_gain):
+def forward(operands):
     square = ((4, 64, 64), F32, VMEM)
     rows = (2, 4, 64, 2048)
     scratch = dict(
@@ -688,6 +776,10 @@
         normed=pltpu.VMEM((2, 4, 64, HALF), F32),
         parts=pltpu.VMEM(rows, BF),
         second_own=pltpu.VMEM((64, 2048), BF),
+        wq=pltpu.VMEM((2, 2, 32, 3 * HALF), BF),
+        wg=pltpu.VMEM((2, 2, 32, 2 * HALF), BF),
+        wf=pltpu.VMEM((4, 32, FFN), BF),
+        packed=pltpu.VMEM((4, 4, 64, SLOTS), F32),
         q_send=DMA((2, 2)),
         q_recv=DMA((4,)),
         g_send=DMA((2, 2)),
@@ -706,21 +798,13 @@
     return remote_call(
         forward_kernel,
         1,
-        dict(
-            wq=(wq, ANY),
-            wg=(wg, ANY),
-            wf=(wf, ANY),
-            rows_a=(rows_a, ANY),
-            rows_b=(rows_b, ANY),
-            packed=(packed, ANY),
-            resid=(resid, VMEM),
-            head_gain=(head_gain, VMEM),
-            norm2_gain=(norm2_gain, VMEM),
-        ),
+        {name: (value, ANY if name == "rows_b" else VMEM) for name, value in operands.items()},
         dict(
             wide_q=((4, 4, 128, 3 * HALF), BF, VMEM),
             wide_g=((4, 4, 128, 2 * HALF), BF, VMEM),
             wide_f=((4, 4, 128, FFN), BF, ANY),
+            first_own=((64, 2048), BF, VMEM),
+            lowrank=((64, 16), F32, VMEM),
             first=(rows, BF, VMEM),
             cot=(rows, BF, ANY),
             second=(rows, BF, VMEM),
@@ -971,7 +1055,8 @@
     x, y, z, c = here()
     partner = (x, y, z, 1 - c)
     scan = Scan(r, True)
-    greet(all_peers() + scan.senders())
+    greet(all_peers())
+    greeted(all_peers())
     second = RowSum(r, "sec", r.second_part, lambda k: r.second_mine[k])
     ffn = RowSum(r, "ffn", r.ffn_part, lambda k: r.ffn_mine[k])
     one = WeightSum(r, "one", r.grads_one, 6 * HALF, True)
@@ -996,7 +1081,6 @@
     two.load()
     for k in (1, 2, 3, 0):
         two.send(k)
-    ffn.pairs()
     e = second.result()
     v = r.resid1[...]
     grad, d_norm2 = rms_back(v, r.norm2_gain[...], e)
@@ -1007,8 +1091,8 @@
     r.grad_resid1[...] = grad_resid1
     a_sems = sems_of(r, "rows_a_", 5)
     a_rows = rows_start(r.attn_own, r.attn, a_sems)
-    ffn.hops()
     rows_finish(a_rows, r.attn, a_sems)
+    ffn.pairs()
 
     attn = r.attn[...].reshape(512, 2048)
     grad_branch = dot(attn, r.wide_g[:, :, :, HALF : 2 * HALF].reshape(2048, HALF))
@@ -1022,6 +1106,7 @@
     swap = push(r.grad_out.at[1 - c], r.grad_norm.at[c], r.swap_s.at[0], r.swap_r.at[0], partner)
     r.grad_norm[c] = r.grad_out[c]
     swap.wait()
+    ffn.hops()
 
     def all_rows(ref):
         return ref[...].reshape(512, ref.shape[-1])
@@ -1065,6 +1150,9 @@
             tn(weight_rows(r.attn, n), all_rows(r.branch)).astype(BF).reshape(4, 128, HALF)
         )
 
+    scan.middle()
+    for k in range(1, 4):
+        one.turn(k)
     scan.fold(r.nexts)
     for k in (1, 2, 3, 0):
         tail.send(k)
@@ -1102,8 +1190,18 @@
     swap2 = push(r.dproj.at[1 - c], r.dqkv.at[c], r.swap_s.at[1], r.swap_r.at[1], partner)
     r.dqkv[c] = r.dproj[c]
     logits = shuffle_start(lambda k: r.dlogit.at[k], r.dl.at[z], *sems_of(r, "gate", 3))
+    for k in range(1, 4):
+        two.turn(k)
     swap2.wait()
 
+    @pl.loop(0, 4)
+    def _(n):
+        r.grads_last[n] = (
+            tn(weight_rows(r.first, n), all_rows(r.dqkv)).astype(BF).reshape(4, 128, 3 * HALF)
+        )
+
+    for k in (1, 2, 3, 0):
+        last.send(k)
     first_part = r.attn
     first = RowSum(r, "fst", first_part, lambda k: first_part[c, k])
     for core in (1 - c, c):
@@ -1124,18 +1222,6 @@
 
     first.hops()
 
-    @pl.loop(0, 4)
-    def _(n):
-        r.grads_last[n] = (
-            tn(weight_rows(r.first, n), all_rows(r.dqkv)).astype(BF).reshape(4, 128, 3 * HALF)
-        )
-
-    for k in (1, 2, 3, 0):
-        last.send(k)
-    for k in range(1, 4):
-        one.turn(k)
-    for k in range(1, 4):
-        two.turn(k)
     for k in range(1, 4):
         tail.turn(k)
 
@@ -1153,7 +1239,7 @@
     small.pair()
     small.send(0)
     grad_first = first.result() + dot(low, r.down[...], precision=HIGH)
-    grad, d_norm1 = rms_back(r.resid[...], r.norm1_gain[...], grad_first)
+    grad, d_norm1 = rms_back(r.inputs[...].astype(F32), r.norm1_gain[...], grad_first)
     r.d_inputs[...] = r.grad_resid1[...] + grad
     r.tiny[...] = jnp.zeros_like(r.tiny)
     r.tiny[0:1, :] = d_norm1
@@ -1268,6 +1354,51 @@
     )
 
 
+def results_kernel(
+    out, d_in, last, tail, one, two, small, tiny, output, d_inputs, norm1, q, k, v, g, o, down, up, bias, head, norm2, fg, fu, fd
+):
+    output[...] = out[...]
+    d_inputs[...] = d_in[...]
+    for j in range(2):
+        for n in range(2):
+            at = slice((2 * j + n) * HALF, (2 * j + n + 1) * HALF)
+            for m, ref in enumerate((q, k, v)):
+                ref[:, at] = last[j, n, :, m * HALF : (m + 1) * HALF].astype(F32)
+            g[:, at] = tail[j, n, :, 0:HALF].astype(F32)
+            row = lax.broadcasted_iota(jnp.int32, (HALF, HALF), 0)
+            col = lax.broadcasted_iota(jnp.int32, (HALF, HALF), 1)
+            o[at, :] = nt((row == col).astype(BF), tail[j, n, :, HALF : 2 * HALF])
+    for n in range(4):
+        at = slice(n * UNITS, (n + 1) * UNITS)
+        fg[:, at] = one[n, :, 0:UNITS].astype(F32)
+        fu[:, at] = one[n, :, UNITS_PAD : UNITS_PAD + UNITS].astype(F32)
+        fd[:, at] = two[n, :, 0:UNITS].astype(F32)
+    norm1[...] = tiny[0:1, :]
+    norm2[...] = small[17:18, 0:2048]
+    head[...] = small[18:19, 0:512]
+    bias[...] = small[18:19, 512:768]
+    up[...] = small[0:16, 2048:2304]
+    down[...] = small[0:16, 0:2048]
+
+
+def results(b):
+    shapes = [((64, 2048), BF), ((64, 2048), F32), ((1, 2048), F32)]
+    shapes += [((32, 1024), F32)] * 4 + [((1024, 32), F32), ((16, 2048), F32), ((16, 256), F32)]
+    shapes += [((1, 256), F32), ((1, 512), F32), ((1, 2048), F32)] + [((32, 4 * UNITS), F32)] * 3
+    names = ("output", "d_inputs", "out_last", "out_tail", "out_one", "out_two")
+    names += ("small_out", "tiny_out")
+    call = pl.pallas_call(
+        results_kernel,
+        out_shape=[jax.ShapeDtypeStruct(shape, dtype) for shape, dtype in shapes],
+        compiler_params=pltpu.CompilerParams(vmem_limit_bytes=32 * 2**20),
+    )
+    out = list(call(*[b[name] for name in names]))
+    out[8] = out[8].T
+    for n in (2, 10, 11, 12):
+        out[n] = out[n][0]
+    return tuple(out)
+
+
 def rms(v, gain):
     return v * lax.rsqrt(jnp.mean(v * v, axis=-1, keepdims=True) + EPS) * gain
 
@@ -1297,31 +1428,28 @@
     ffn_down,
     cotangent,
 ):
-    core = lax.axis_index("c")
-
-    def dealt(weights):
-        out = jnp.stack([w.reshape(32, 2, 2, HALF) for w in weights], axis=3)
-        return out.transpose(1, 2, 0, 3, 4).reshape(2, 2, 32, len(weights) * HALF)
-
-    wq = dealt((query_weight, key_weight, value_weight))
-    wg = dealt((gate_weight, out_weight.T))
-    wf = jnp.stack([w.reshape(32, 4, UNITS) for w in (ffn_gate, ffn_up, ffn_down)], axis=2)
-    wf = jnp.pad(wf, ((0, 0), (0, 0), (0, 0), (0, UNITS_PAD - UNITS)))
-    wf = wf.transpose(1, 0, 2, 3).reshape(4, 32, FFN)
-    resid = inputs.astype(F32)
     gain1, gain2, gain_head = norm1_gain[None], norm2_gain[None], head_gain[None]
-    first_own = rms(resid, gain1).astype(BF)
-
-    lowrank = dot(first_own, low_down)
-    up = low_up.astype(F32)
-    logits = (dot(lowrank, up, precision=HIGH) + forget_bias).astype(BF).astype(F32)
-    lam = jax.nn.log_sigmoid(logits) / 8.0
-    offs = lax.dynamic_slice_in_dim(offsets, core * 64, 64, 0).astype(F32)
-    offs = jnp.broadcast_to(offs[:, None], (64, 256))
-    packed = jnp.stack([lam, -jnp.expm1(lam), jax.nn.sigmoid(-logits) / 8.0, offs])
-    packed = packed.reshape(4, 64, 4, SLOTS).transpose(2, 0, 1, 3)
-
-    f = forward(wq, wg, wf, first_own, cotangent, packed, resid, gain_head, gain2)
+    f = forward(
+        dict(
+            query_weight=query_weight,
+            key_weight=key_weight,
+            value_weight=value_weight,
+            gate_weight=gate_weight,
+            out_weight=out_weight,
+            ffn_gate=ffn_gate,
+            ffn_up=ffn_up,
+            ffn_down=ffn_down,
+            inputs=inputs,
+            rows_b=cotangent,
+            offsets=offsets[None],
+            low_down=low_down,
+            low_up=low_up,
+            forget_bias=forget_bias[None],
+            norm1_gain=gain1,
+            norm2_gain=gain2,
+            head_gain=gain_head,
+        )
+    )
 
     second, cot = f["second"].reshape(512, 2048), f["cot"].reshape(512, 2048)
     wide_f = f["wide_f"].reshape(2048, FFN)
@@ -1347,10 +1475,8 @@
         second_part=second_part,
         ffn_part=ffn_part,
         cot_own=cotangent,
-        resid=resid,
-        first_own=first_own,
-        lowrank=lowrank,
-        up=up.reshape(16, 4, SLOTS).transpose(1, 0, 2),
+        inputs=inputs,
+        up=low_up.astype(F32).reshape(16, 4, SLOTS).transpose(1, 0, 2),
         down=low_down.astype(F32).T,
         norm1_gain=gain1,
         norm2_gain=gain2,
@@ -1358,35 +1484,7 @@
     )
     b = backward(operands)
 
-    def owned(value, count):
-        value = value.reshape(2, 2, 32, count, HALF).transpose(3, 2, 0, 1, 4)
-        return value.reshape(count, 32, 1024).astype(F32)
-
-    def units(value, count):
-        value = value.reshape(4, 32, count, UNITS_PAD)[..., :UNITS].transpose(2, 1, 0, 3)
-        return value.reshape(count, 32, 4 * UNITS).astype(F32)
-
-    last, tail = owned(b["out_last"], 3), owned(b["out_tail"], 2)
-    one, two = units(b["out_one"], 2), units(b["out_two"], 1)
-    small, tiny = b["small_out"], b["tiny_out"]
-    return (
-        b["output"],
-        b["d_inputs"],
-        tiny[0],
-        last[0],
-        last[1],
-        last[2],
-        tail[0],
-        tail[1].T,
-        small[0:16, 0:2048].T,
-        small[0:16, 2048:2304],
-        small[18, 512:768],
-        small[18, 0:512],
-        small[17, 0:2048],
-        one[0],
-        one[1],
-        two[0],
-    )
+    return results(b)
 
 
 def solution(mesh):

time: 382 us -> 319 us (0.84); the launches traced: 375 us -> 318 us
  Pallas kernels: 311 us -> 276 us
  local copies, waits for them, and re-layouts: 24.7 us -> 13.4 us
  other arithmetic: 7.87 us -> 0.67 us
    pallas_call x2, Pallas kernels: 311 us -> 275 us  [remote_call(): pl.pallas_call(run, out_shape=[jax.ShapeDtypeStruct(shape, dtype) for sha...]
    unnamed x44 -> x29, local copies, waits for them, and re-layouts: 2.39 us -> 12.7 us
    slice x15 -> x0, local copies, waits for them, and re-layouts: 5.94 us -> none  [the longest x1 1.44 us: body(): tiny[0]]
    squeeze x7 -> x0, local copies, waits for them, and re-layouts: 5.78 us -> none  [the longest x1 0.99 us: body(): one[0]]
    reshape x4 -> x0, local copies, waits for them, and re-layouts: 4.16 us -> none  [the longest x2 1.64 us: dealt(): return out.transpose(1, 2, 0, 3, 4).reshape(2, 2, 32, len(weights) * HALF)]
    dot_general x9 -> x7, matrix products: 29.5 us -> 27.1 us  [dot(): lax.dot_general(left, right, (dims, ((), ())), precision=precision, prefe...]
where the time goes in v3:
time: 319 us; the launch traced here: 318 us
  Pallas kernels  276 us (87%)
  matrix products  27.1 us (8%)
  local copies, waits for them, and re-layouts  13.4 us (4%)
    pallas_call x2, Pallas kernels, remote_call(): pl.pallas_call(run, out_shape=[jax.ShapeDtypeStruct(shape, dtype) for sha...  275 us
    dot_general x7, matrix products, dot(): lax.dot_general(left, right, (dims, ((), ())), precision=precision, prefe...  27.1 us
    unnamed x29, local copies, waits for them, and re-layouts  12.7 us

profile of v3, /device:TPU:1, one launch (start us, length us, event | category | flops | bytes accessed | tf_op | source)
XLA Modules:
  0.0 318.2 jit_solution(12769651865459672981)
XLA Ops:
  0.6 1.8 copy.37.refs_11_
  2.5 1.7 copy.36.refs_4_
  4.2 134.6 %shard_map.288 = (bf16[4,4,128,768]{3,2,1,0:T(8,128)(2,1)}, bf16[4,4,128,512]{3,2,1,0:T(8,128)(2,1)}, bf16[4,4,128,2304]{3,2,1,0:T(8,128)(2,1)}, bf16[64,2048]{1...) custom-call(bf16[32,1024]{1,0:T(8,128)(2,1)} %refs_0_.1, ...), custom_call_target="tpu_custom_call" | custom-call | tf_op jit(solution)/shard_map/pallas_call | solution.py:83
  138.7 0.0 copy-start.10
  138.8 4.5 %fusion.2 = f32[512,768]{1,0:T(8,128)S(1)} fusion(bf16[512,2048]{1,0:T(8,128)(2,1)} %bitcast.47, bf16[2048,2304]{1,0:T(8,128)(2,1)} %bitcast.42), kind=kOutput, calls=%fused_computation.4 | convolution fusion | flops 1610612736 | bytes 6815744 | tf_op jit(solution)/shard_map/dot_general | solution.py:31
  143.2 0.8 copy-done.10
  144.0 0.0 copy-start.11
  144.0 3.5 %fusion.10 = f32[512,768]{1,0:T(8,128)S(1)} fusion(bf16[512,2048]{1,0:T(8,128)(2,1)} %bitcast.50, bf16[2048,2304]{1,0:T(8,128)(2,1)S(1)} %bitcast.43), kind=kOutput, calls=%fused_computation.11 | convolution fusion | flops 1610612736 | bytes 6815744 | tf_op jit(solution)/shard_map/dot_general | solution.py:31
  147.5 0.0 copy-done.11
  147.5 2.2 multiply_convert_fusion
  149.7 3.2 convolution_convert_fusion.2
  152.9 4.6 %fusion.6 = bf16[512,2048]{1,0:T(8,128)(2,1)} fusion(bf16[2048,2304]{1,0:T(8,128)(2,1)S(1)} %bitcast.46, bf16[512,768]{1,0:T(8,128)(2,1)S(1)} %get-tuple-element.142, bf16[512,768]{1,0:T(8,128)(2,1)S(1)} %get-tuple-element.141), kind=kOutput, calls=%fused_computation.8 | convolution fusion | flops 3225419776 | bytes 9961472 | tf_op jit(solution)/shard_map/dot_general | solution.py:31
  157.5 0.0 copy-done.12
  157.5 3.6 %convolution_convert_fusion.1 = bf16[2048,768]{1,0:T(8,128)(2,1)} fusion(bf16[512,2048]{1,0:T(8,128)(2,1)S(1)} %bitcast.51, bf16[512,768]{1,0:T(8,128)(2,1)S(1)} %get-tuple-element.140), kind=kOutput, calls=%fused_computation.3 | convolution fusion | flops 1612185600 | bytes 6029312 | tf_op jit(solution)/shard_map/dot_general | solution.py:31
  161.1 5.6 %convolution_convert_fusion = bf16[2048,1536]{1,0:T(8,128)(2,1)} fusion(bf16[512,2048]{1,0:T(8,128)(2,1)S(1)} %bitcast.49, bf16[512,768]{1,0:T(8,128)(2,1)S(1)} %get-tuple-element.142, bf16[512,768]{1,0:T(8,128)(2,1)S(1)} %get-tuple-element.141), kind=kOutput, calls=%fused_computation | convolution fusion | flops 3227516928 | bytes 9961472 | tf_op jit(solution)/shard_map/dot_general | solution.py:31
  166.7 0.0 copy-done.8
  166.7 0.7 convert_bitcast_fusion.refs_26_
  167.4 0.0 copy-done.9
  167.4 0.1 reshape.65
  167.5 0.6 copy.41
  168.1 140.0 %shard_map.289 = (bf16[64,2048]{1,0:T(8,128)(2,1)}, f32[64,2048]{1,0:T(8,128)}, bf16[2,2,32,768]{3,2,1,0:T(8,128)(2,1)}, bf16[2,2,32,512]{3,2,1,0:T(8,128)(2,1)}...) custom-call(bf16[4,4,128,768]{3,2,1,0:T(8,128)(2,1)} %get-tuple-element.62, ...), custom_call_target="tpu_custom_call" | custom-call | tf_op jit(solution)/shard_map/pallas_call | solution.py:83
  308.1 0.0 copy-start
  308.1 1.0 copy-done
  309.1 1.0 copy-done.1
  310.1 0.9 copy-done.2
  311.1 0.9 copy-done.3
  312.0 0.9 copy-done.4
  312.9 0.9 copy-done.5
  313.9 0.9 copy-done.6
  314.8 0.8 copy-done.7
  315.6 1.7 shard_map.290
  317.3 0.8 copy.39
  (10 shorter events, 0.0 us)
Async XLA Ops:
  138.7 5.3 %copy-start.10 = (bf16[4,4,128,2304]{3,2,1,0:T(8,128)(2,1)S(1)}, bf16[4,4,128,2304]{3,2,1,0:T(8,128)(2,1)}, u32[]{:S(2)}) copy-start(bf16[4,4,128,2304]{3,2,1,0:T(8,128)(2,1)} %get-tuple-element.83) | copy-start | bytes 28311556
  144.0 3.5 %copy-start.11 = (bf16[2,4,64,2048]{3,2,1,0:T(8,128)(2,1)S(1)}, bf16[2,4,64,2048]{3,2,1,0:T(8,128)(2,1)}, u32[]{:S(2)}) copy-start(bf16[2,4,64,2048]{3,2,1,0:T(8,128)(2,1)} %get-tuple-element.81) | copy-start | bytes 6291460
  152.9 4.6 %copy-start.12 = (bf16[2,4,64,2048]{3,2,1,0:T(8,128)(2,1)S(1)}, bf16[2,4,64,2048]{3,2,1,0:T(8,128)(2,1)}, u32[]{:S(2)}) copy-start(bf16[2,4,64,2048]{3,2,1,0:T(8,128)(2,1)} %get-tuple-element.82) | copy-start | bytes 6291460
  161.1 5.6 %copy-start.8 = (bf16[2048,16]{0,1:T(8,128)(2,1)S(1)}, bf16[2048,16]{0,1:T(8,128)(2,1)}, u32[]{:S(2)}) copy-start(bf16[2048,16]{0,1:T(8,128)(2,1)} %param.25) | copy-start | bytes 196612
  161.1 6.3 %copy-start.9 = (bf16[16,256]{1,0:T(8,128)(2,1)S(1)}, bf16[16,256]{1,0:T(8,128)(2,1)}, u32[]{:S(2)}) copy-start(bf16[16,256]{1,0:T(8,128)(2,1)} %refs_12_.1) | copy-start | bytes 24580
  308.1 1.0 copy-start
  309.1 1.0 copy-start.1
  310.1 0.9 copy-start.2
  311.1 0.9 copy-start.3
  312.0 0.9 copy-start.4
  312.9 0.9 copy-start.5
  313.9 0.9 copy-start.6
  314.8 0.8 copy-start.7

commit v4 on v3

--- a/solution.py
+++ b/solution.py
@@ -23,7 +23,6 @@
 ANY = pl.BlockSpec(memory_space=pl.ANY)
 VMEM = pl.BlockSpec(memory_space=pltpu.VMEM)
 DMA = pltpu.SemaphoreType.DMA
-MIX = 5 * HALF
 FFN = 3 * UNITS_PAD
 
 
@@ -68,16 +67,55 @@
 
 
 class Refs:
-    pass
-
-
-def remote_call(kernel, collective_id, operands, outs, scratch):
+    def start(self):
+        self.loads = {}
+        for n, name in enumerate(self.loaded):
+            copy = pltpu.make_async_copy(
+                getattr(self, "in_" + name), getattr(self, name), self.load_sem.at[n]
+            )
+            copy.start()
+            self.loads[name] = copy
+        self.saves = []
+
+    def need(self, *names):
+        for name in names:
+            copy = self.loads.pop(name, None)
+            if copy is not None:
+                copy.wait()
+
+    def save(self, *names):
+        for name in names:
+            copy = pltpu.make_async_copy(
+                getattr(self, name),
+                getattr(self, "out_" + name),
+                self.save_sem.at[len(self.saves)],
+            )
+            copy.start()
+            self.saves.append(copy)
+
+    def finish(self):
+        for copy in self.saves:
+            copy.wait()
+
+
+def remote_call(kernel, collective_id, operands, outs, scratch, loaded=(), saved=()):
+    loaded, saved = dict(loaded), dict(saved)
+    operands = dict(operands)
+    operands.update({"in_" + name: (value, ANY) for name, value in loaded.items()})
+    outs = dict(outs)
+    outs.update({"out_" + name: (shape, dtype, ANY) for name, (shape, dtype) in saved.items()})
+    scratch = dict(scratch)
+    scratch.update({name: pltpu.VMEM(v.shape, v.dtype) for name, v in loaded.items()})
+    scratch.update({name: pltpu.VMEM(shape, dtype) for name, (shape, dtype) in saved.items()})
+    scratch["load_sem"] = DMA((max(len(loaded), 1),))
+    scratch["save_sem"] = DMA((max(len(saved), 1),))
     names = list(operands) + list(outs) + list(scratch)
 
     def run(*refs):
         r = Refs()
         for name, ref in zip(names, refs):
             setattr(r, name, ref)
+        r.loaded = list(loaded)
         kernel(r)
 
     results = pl.pallas_call(
@@ -90,45 +128,63 @@
             collective_id=collective_id, has_side_effects=True, vmem_limit_bytes=63 * 2**20
         ),
     )(*[array for array, _ in operands.values()])
-    return dict(zip(outs, results))
-
-
-def spread_block(w_ref, side, k, cols):
-    x, y, z, c = here()
-    part = pl.ds(side * (cols // 2), cols // 2)
-    if side == 0:
-        return w_ref.at[x, wrap(y - k), :, part]
-    return w_ref.at[wrap(x - k), y, :, part]
-
-
-def spread_near(w_ref, sems, cols):
-    x, y, z, c = here()
-    sent = {}
-    for d in range(1, 4):
-        for side in range(2):
-            block = spread_block(w_ref, side, 0, cols)
-            peer = (x, wrap(y + d), z, c) if side == 0 else (wrap(x + d), y, z, c)
-            sent[side, d] = push(
-                block, block, sems[0].at[side, d - 1], sems[1].at[side, d - 1], peer
-            )
-    return sent
-
-
-def spread_far(w_ref, sems, cols, near, k):
-    x, y, z, c = here()
-    sent = []
-    for side in range(2):
-        if k > 0:
-            near[side, k].wait_recv()
-        block = spread_block(w_ref, side, k, cols)
+    return {name.removeprefix("out_"): value for name, value in zip(outs, results)}
+
+
+class Spread:
+    def __init__(self, r, name, ref, start, width):
+        self.ref, self.start, self.half = ref, start, width // 2
+        self.sems = sems_of(r, name, 4)
+        self.nears, self.fars = {}, []
+
+    def block(self, side, k):
+        x, y, z, c = here()
+        part = pl.ds(self.start + side * self.half, self.half)
+        if side == 0:
+            return self.ref.at[x, wrap(y - k), :, part]
+        return self.ref.at[wrap(x - k), y, :, part]
+
+    def near(self):
+        x, y, z, c = here()
         for d in range(1, 4):
-            peer = (wrap(x + d), y, z, c) if side == 0 else (x, wrap(y + d), z, c)
-            sent.append(
-                push(
-                    block, block, sems[2].at[side, k, d - 1], sems[3].at[side, k, d - 1], peer
+            for side in range(2):
+                block = self.block(side, 0)
+                peer = (x, wrap(y + d), z, c) if side == 0 else (wrap(x + d), y, z, c)
+                self.nears[side, d] = push(
+                    block, block, self.sems[0].at[side, d - 1], self.sems[1].at[side, d - 1], peer
                 )
-            )
-    return sent
+
+    def far(self, *steps):
+        x, y, z, c = here()
+        for k in steps:
+            for side in range(2):
+                if k > 0:
+                    self.nears[side, k].wait_recv()
+                block = self.block(side, k)
+                for d in range(1, 4):
+                    peer = (wrap(x + d), y, z, c) if side == 0 else (x, wrap(y + d), z, c)
+                    self.fars.append(
+                        push(
+                            block,
+                            block,
+                            self.sems[2].at[side, k, d - 1],
+                            self.sems[3].at[side, k, d - 1],
+                            peer,
+                        )
+                    )
+
+    def arrive(self):
+        for copy in self.fars:
+            copy.wait_recv()
+
+    def done(self):
+        for copy in list(self.nears.values()) + self.fars:
+            copy.wait_send()
+
+
+def spread_sems(name):
+    kinds = ((2, 3), (2, 3), (2, 4, 3), (2, 4, 3))
+    return {f"{name}{n}": DMA(shape) for n, shape in enumerate(kinds)}
 
 
 def rows_start(src, out, sems):
@@ -178,11 +234,6 @@
 
 def all_peers():
     return group_peers() + plane_peers()
-
-
-def spread_sems(name):
-    kinds = ((2, 3), (2, 3), (2, 4, 3), (2, 4, 3))
-    return {f"{name}{n}": DMA(shape) for n, shape in enumerate(kinds)}
 
 
 def rows_sems(name):
@@ -266,7 +317,7 @@
 class RowSum:
     def __init__(self, r, name, parts, own):
         self.parts, self.own = parts, own
-        self.theirs, self.landed = sems_of(r, name + "b", 2)
+        self.theirs, self.landed = r.theirs, r.landed
         self.sems = sems_of(r, name + "s", 4)
 
     def pairs(self):
@@ -314,9 +365,10 @@
             copy.wait_send()
 
 
-def sum_scratch(name):
-    out = {f"{name}b{n}": pltpu.VMEM((k, 64, 2048), BF) for n, k in enumerate((4, 3))}
-    out.update({f"{name}s{n}": DMA((k,)) for n, k in enumerate((4, 4, 3, 3))})
+def sum_scratch(*names):
+    out = dict(theirs=pltpu.VMEM((4, 64, 2048), BF), landed=pltpu.VMEM((3, 64, 2048), BF))
+    for name in names:
+        out.update({f"{name}s{n}": DMA((k,)) for n, k in enumerate((4, 4, 3, 3))})
     return out
 
 
@@ -551,7 +603,8 @@
     return dmix, dfar, dnear, dscore, ends_k, ends_v
 
 
-def chunk_pairs(cum, write, affinity, dmix, dscore, probs):
+def chunk_pairs(query, key, cum, write, offs, dmix, dscore, probs):
+    affinity = jnp.where(seen_mask(offs), nt(query, key) * SCALE, 0.0)
     cums, writes = tiles(cum), tiles(write)
     aff, dmx, dsc, prb = tiles(affinity), tiles(dmix), tiles(dscore), tiles(probs)
     lane = lax.broadcasted_iota(jnp.int32, (8, CHUNK), 1)
@@ -569,11 +622,9 @@
 
 
 def chunk_last(
-    query, key, value, g, lam, write, slope, offs, cum, near, far, probs, mixing, state, dmix, dfar, dnear, dscore, after
+    query, key, value, g, lam, write, slope, offs, cum, near, far, probs, mixing, state, dfar, dnear, dscore, daff, fresh, after
 ):
     carry, seen, reach = carried(cum, offs), seen_mask(offs), reaching(cum, offs)
-    affinity = jnp.where(seen, nt(query, key) * SCALE, 0.0)
-    daff, fresh = chunk_pairs(cum, write, affinity, dmix, dscore, probs)
     daff = jnp.where(seen, daff * SCALE, 0.0).astype(BF)
     ending = (reach * write).astype(BF)
     nk, nv = after[:, 0:512].astype(BF), after[:, 512:1024].astype(BF)
@@ -613,18 +664,14 @@
     x, y, z, c = here()
     first = rms(r.inputs[...].astype(F32), r.norm1_gain[...]).astype(BF)
     r.first_own[...] = first
-    eye = (
-        lax.broadcasted_iota(jnp.int32, (32, 32), 0) == lax.broadcasted_iota(jnp.int32, (32, 32), 1)
-    ).astype(BF)
-    out_t = nt(eye, r.out_weight[...]).astype(BF)
     for j in range(2):
         for k in range(2):
             cols = slice((2 * j + k) * HALF, (2 * j + k + 1) * HALF)
-            for n, w in enumerate((r.query_weight, r.key_weight, r.value_weight)):
-                r.wq[j, k, :, n * HALF : (n + 1) * HALF] = w[:, cols]
-            r.wg[j, k, :, 0:HALF] = r.gate_weight[:, cols]
-            r.wg[j, k, :, HALF : 2 * HALF] = out_t[:, cols]
-    lowrank = dot(first, r.low_down[...])
+            for n, w in enumerate((r.key_weight, r.value_weight)):
+                r.wk[j, k, :, n * HALF : (n + 1) * HALF] = w[:, cols]
+            for n, w in enumerate((r.query_weight, r.gate_weight, r.out_weight)):
+                r.wm[j, k, :, n * HALF : (n + 1) * HALF] = w[:, cols]
+    lowrank = nt(first, r.low_down[...])
     r.lowrank[...] = lowrank
     logits = dot(lowrank, r.low_up[...].astype(F32), precision=HIGH) + r.forget_bias[...]
     lam, write, slope = forget_gate(logits.astype(BF).astype(F32))
@@ -634,9 +681,8 @@
     offs = jnp.broadcast_to(jnp.sum(offs, axis=1, keepdims=True), (64, SLOTS))
     for h in range(4):
         cols = slice(h * SLOTS, (h + 1) * SLOTS)
-        for n, value in enumerate((lam, write, slope)):
-            r.packed[h, n] = value[:, cols]
-        r.packed[h, 3] = offs
+        r.packed[h, 0] = jnp.concatenate([lam[:, cols], write[:, cols]], axis=1)
+        r.packed[h, 1] = jnp.concatenate([slope[:, cols], offs], axis=1)
     for k in range(4):
         for n, w in enumerate((r.ffn_gate, r.ffn_up, r.ffn_down)):
             piece = w[:, k * UNITS : (k + 1) * UNITS]
@@ -644,94 +690,142 @@
             r.wf[k, :, n * UNITS_PAD : (n + 1) * UNITS_PAD] = jnp.concatenate([piece, pad], axis=1)
 
 
+def gate_of(r, n, kind):
+    return r.gate[n, kind]
+
+
+def tile(n, width=HALF, start=0):
+    return pl.ds(pl.multiple_of(start + n * width, width), width)
+
+
+def all_rows(ref, *at):
+    value = ref[at] if at else ref[...]
+    return value.reshape(512, value.shape[-1])
+
+
+def columns(ref, cols):
+    return ref[:, :, :, cols].reshape(2048, -1)
+
+
 def forward_kernel(r):
     x, y, z, c = here()
     partner = (x, y, z, 1 - c)
     scan = Scan(r, False)
+    r.start()
     greet(all_peers())
     prepare(r)
     greeted(all_peers())
-    q_deal = deal_start(r.wq, r.wide_q, r.q_send, r.q_recv)
+    kv = Spread(r, "kv_spread", r.wide_k, 0, 2 * HALF)
+    mix = Spread(r, "m_spread", r.wide_m, 0, 3 * HALF)
+    down = Spread(r, "d_spread", r.wide_f, 2 * UNITS_PAD, UNITS_PAD)
+    acts = Spread(r, "f_spread", r.wide_f, 0, 2 * UNITS_PAD)
     a_sems, b_sems, s_sems = (sems_of(r, n, 5) for n in ("rows_a_", "rows_b_", "rows_s_"))
+    k_deal = deal_start(r.wk, r.wide_k, r.k_send, r.k_recv)
+    deal_wait(r.wk, r.wide_k, r.k_recv)
+    kv.near()
+    kv.far(0)
     a_rows = rows_start(r.first_own, r.first, a_sems)
     gates = shuffle_start(lambda k: r.packed.at[k], r.gates.at[z], *sems_of(r, "gate", 3))
-    g_deal = deal_start(r.wg, r.wide_g, r.g_send, r.g_recv)
+    m_deal = deal_start(r.wm, r.wide_m, r.m_send, r.m_recv)
     f_deal = shuffle_start(
         lambda k: r.wf.at[k],
         r.wide_f.at[x, y, pl.ds(pl.multiple_of(z * 32, 32), 32), :],
         *sems_of(r, "deal", 3),
     )
-    q_sems, g_sems, f_sems = (sems_of(r, n, 4) for n in ("q_spread", "g_spread", "f_spread"))
-    deal_wait(r.wq, r.wide_q, r.q_recv)
-    q_near = spread_near(r.wide_q, q_sems, 3 * HALF)
-    q_far = spread_far(r.wide_q, q_sems, 3 * HALF, q_near, 0)
-    for k in range(1, 4):
-        q_far += spread_far(r.wide_q, q_sems, 3 * HALF, q_near, k)
-    deal_wait(r.wg, r.wide_g, r.g_recv)
-    g_near = spread_near(r.wide_g, g_sems, 2 * HALF)
+    kv.far(1, 2, 3)
+    deal_wait(r.wm, r.wide_m, r.m_recv)
+    mix.near()
     rows_finish(a_rows, r.first, a_sems)
     shuffle_wait(gates)
-    for copy in q_far:
-        copy.wait_recv()
-    g_far = []
-    for k in range(4):
-        g_far += spread_far(r.wide_g, g_sems, 2 * HALF, g_near, k)
+    for n in range(4):
+        for kind in range(4):
+            r.gate[n, kind] = r.gates[n, kind // 2, :, (kind % 2) * SLOTS : (kind % 2 + 1) * SLOTS]
+    kv.arrive()
+    mix.far(0, 1, 2, 3)
+    r.save("wide_k", "first", "gate")
+
+    @pl.loop(0, 2)
+    def _(n):
+        got = dot(all_rows(r.first), columns(r.wide_k, tile(n)))
+        r.proj[:, :, :, tile(n, start=HALF)] = got.astype(BF).reshape(2, 4, 64, HALF)
+
+    key_value = pl.ds(HALF, 2 * HALF)
+    swap = push(
+        r.proj.at[1 - c, :, :, key_value],
+        r.qkv.at[c, :, :, key_value],
+        r.swap_s.at[0],
+        r.swap_r.at[0],
+        partner,
+    )
+    r.qkv[c, :, :, key_value] = r.proj[c, :, :, key_value]
     shuffle_wait(f_deal)
-    f_near = spread_near(r.wide_f, f_sems, FFN)
-
-    @pl.loop(0, 3)
-    def _(n):
-        cols = pl.ds(pl.multiple_of(n * HALF, HALF), HALF)
-        rows = r.first[...].reshape(512, 2048)
-        got = dot(rows, r.wide_q[:, :, :, cols].reshape(2048, HALF))
-        r.proj[:, :, :, cols] = got.astype(BF).reshape(2, 4, 64, HALF)
-
-    swap = push(r.proj.at[1 - c], r.qkv.at[c], r.swap_s.at[0], r.swap_r.at[0], partner)
-    r.qkv[c] = r.proj[c]
     swap.wait()
 
     @pl.loop(0, 4)
     def _(n):
-        lam, write, offs = r.gates[n, 0], r.gates[n, 1], r.gates[n, 3]
-        cum, ends = chunk_ends(features(r.qkv, n, 1), features(r.qkv, n, 2), lam, write, offs)
+        cum, ends = chunk_ends(
+            features(r.qkv, n, 1), features(r.qkv, n, 2), gate_of(r, n, 0), gate_of(r, n, 1), gate_of(r, n, 3)
+        )
         r.cum[n] = cum
         r.every[c, n] = ends
         r.decays[n] = ends[:, 1024:1152]
 
     scan.pair()
     scan.send()
+    down.near()
+    acts.near()
     b_rows = rows_start(r.rows_b, r.cot, b_sems)
+    mix.arrive()
+    r.save("wide_m")
+    got = dot(all_rows(r.first), columns(r.wide_m, pl.ds(0, HALF)))
+    query = pl.ds(0, HALF)
+    r.proj[:, :, :, query] = got.astype(BF).reshape(2, 4, 64, HALF)
+    swap_q = push(
+        r.proj.at[1 - c, :, :, query],
+        r.qkv.at[c, :, :, query],
+        r.swap_s.at[1],
+        r.swap_r.at[1],
+        partner,
+    )
+    r.qkv[c, :, :, query] = r.proj[c, :, :, query]
+    scan.middle()
+    down.far(0)
+    got = dot(all_rows(r.first), columns(r.wide_m, pl.ds(HALF, HALF)))
+    r.gate_lin[...] = got.reshape(2, 4, 64, HALF)
+    swap_q.wait()
+    r.save("qkv")
 
     @pl.loop(0, 4)
     def _(n):
-        query, key = features(r.qkv, n, 0), features(r.qkv, n, 1)
-        r.near[n] = chunk_near(query, key, r.cum[n], r.gates[n, 1], r.gates[n, 3])
-
-    scan.middle()
-    f_far = spread_far(r.wide_f, f_sems, FFN, f_near, 0)
-    for copy in g_far:
-        copy.wait_recv()
-    r.gate_lin[...] = dot(
-        r.first[...].reshape(512, 2048), r.wide_g[:, :, :, 0:HALF].reshape(2048, HALF)
-    ).reshape(2, 4, 64, HALF)
+        r.near[n] = chunk_near(
+            features(r.qkv, n, 0), features(r.qkv, n, 1), r.cum[n], gate_of(r, n, 1), gate_of(r, n, 3)
+        )
+
     scan.fold(r.states)
-    for k in range(1, 4):
-        f_far += spread_far(r.wide_f, f_sems, FFN, f_near, k)
+    down.far(1, 2, 3)
+    acts.far(0, 1, 2, 3)
 
     @pl.loop(0, 4)
     def _(n):
-        query, value = features(r.qkv, n, 0), features(r.qkv, n, 2)
         far, probs, mixing, mixed = chunk_out(
-            query, value, r.cum[n], r.gates[n, 1], r.gates[n, 3], r.near[n], r.states[n]
+            features(r.qkv, n, 0),
+            features(r.qkv, n, 2),
+            r.cum[n],
+            gate_of(r, n, 1),
+            gate_of(r, n, 3),
+            r.near[n],
+            r.states[n],
         )
         r.far[n], r.probs[n], r.mixing[n], r.mixed[n] = far, probs, mixing, mixed
         normed = rms(mixed, r.head_gain[...])
         for s in range(2):
             r.normed[s, n] = normed[:, s * HALF : (s + 1) * HALF]
 
-    swap2 = push(r.normed.at[1 - c], r.headnorm.at[c], r.swap_s.at[1], r.swap_r.at[1], partner)
+    swap2 = push(r.normed.at[1 - c], r.headnorm.at[c], r.swap_s.at[2], r.swap_r.at[2], partner)
     r.headnorm[c] = r.normed[c]
+    r.save("cum", "decays", "states", "near", "far", "probs", "mixing", "mixed", "gate_lin")
     rows_finish(b_rows, r.cot, b_sems)
+    r.save("cot")
     swap2.wait()
     sums = RowSum(r, "mix", r.parts, lambda k: r.parts[c, k])
     for core in (1 - c, c):
@@ -741,55 +835,93 @@
 
         @pl.loop(0, 4)
         def _(n):
-            got = nt(branch, r.wide_g[n, :, :, HALF : 2 * HALF].reshape(512, HALF))
-            cols = pl.ds(pl.multiple_of(n * 512, 512), 512)
-            r.parts[core, :, :, cols] = got.astype(BF).reshape(4, 64, 512)
+            got = nt(branch, r.wide_m[n, :, :, 2 * HALF : 3 * HALF].reshape(512, HALF))
+            r.parts[core, :, :, tile(n, 512)] = got.astype(BF).reshape(4, 64, 512)
 
         if core is not c:
             sums.pairs()
+    r.save("headnorm", "branch")
     sums.hops()
     resid1 = r.inputs[...].astype(F32) + sums.result()
     r.resid1[...] = resid1
     r.second_own[...] = rms(resid1, r.norm2_gain[...]).astype(BF)
     s_rows = rows_start(r.second_own, r.second, s_sems)
+    down.arrive()
+
+    @pl.loop(0, 3)
+    def _(n):
+        r.grad_hidden[:, tile(n)] = dot(
+            all_rows(r.cot), columns(r.wide_f, tile(n, start=2 * UNITS_PAD))
+        )
+
     rows_finish(s_rows, r.second, s_sems)
-    for copy in f_far:
-        copy.wait()
-    for sent in (q_deal, g_deal):
+    r.save("second")
+    acts.arrive()
+
+    @pl.loop(0, 3)
+    def _(n):
+        second = all_rows(r.second)
+        gate = dot(second, columns(r.wide_f, tile(n)))
+        up = dot(second, columns(r.wide_f, tile(n, start=UNITS_PAD)))
+        grad = r.grad_hidden[:, tile(n)]
+        sig = jax.nn.sigmoid(gate)
+        silu = gate * sig
+        parts = (grad * up * sig * (1 + gate * (1 - sig)), grad * silu, silu * up)
+        for m, part in enumerate(parts):
+            r.acts[m, :, :, :, tile(n)] = part.astype(BF).reshape(2, 4, 64, HALF)
+
+    r.save("acts")
+
+    @pl.loop(0, 4)
+    def _(n):
+        got = nt(all_rows(r.acts, 0), r.wide_f[n, :, :, 0:UNITS_PAD].reshape(512, UNITS_PAD))
+        got = got + nt(
+            all_rows(r.acts, 1), r.wide_f[n, :, :, UNITS_PAD : 2 * UNITS_PAD].reshape(512, UNITS_PAD)
+        )
+        r.second_part[:, :, :, tile(n, 512)] = got.astype(BF).reshape(2, 4, 64, 512)
+
+    r.save("second_part")
+
+    @pl.loop(0, 4)
+    def _(n):
+        got = nt(all_rows(r.acts, 2), r.wide_f[n, :, :, 2 * UNITS_PAD :].reshape(512, UNITS_PAD))
+        r.ffn_part[:, :, :, tile(n, 512)] = got.astype(BF).reshape(2, 4, 64, 512)
+
+    r.save("ffn_part")
+    for sent in (k_deal, m_deal):
         deal_done(sent)
     for sent in (gates, f_deal):
         shuffle_done(sent)
-    for near in (q_near, g_near, f_near):
-        for copy in near.values():
-            copy.wait_send()
-    for copy in q_far + g_far:
-        copy.wait_send()
-    scan.done()
-    sums.done()
+    for part in (kv, mix, down, acts, scan, sums):
+        part.done()
+    r.finish()
 
 
 def forward(operands):
-    square = ((4, 64, 64), F32, VMEM)
+    square = ((4, 64, 64), F32)
     rows = (2, 4, 64, 2048)
     scratch = dict(
         proj=pltpu.VMEM((2, 4, 64, 3 * HALF), BF),
         normed=pltpu.VMEM((2, 4, 64, HALF), F32),
         parts=pltpu.VMEM(rows, BF),
         second_own=pltpu.VMEM((64, 2048), BF),
-        wq=pltpu.VMEM((2, 2, 32, 3 * HALF), BF),
-        wg=pltpu.VMEM((2, 2, 32, 2 * HALF), BF),
+        grad_hidden=pltpu.VMEM((512, UNITS_PAD), F32),
+        wide_f=pltpu.VMEM((4, 4, 128, FFN), BF),
+        wk=pltpu.VMEM((2, 2, 32, 2 * HALF), BF),
+        wm=pltpu.VMEM((2, 2, 32, 3 * HALF), BF),
         wf=pltpu.VMEM((4, 32, FFN), BF),
-        packed=pltpu.VMEM((4, 4, 64, SLOTS), F32),
-        q_send=DMA((2, 2)),
-        q_recv=DMA((4,)),
-        g_send=DMA((2, 2)),
-        g_recv=DMA((4,)),
-        swap_s=DMA((2,)),
-        swap_r=DMA((2,)),
+        packed=pltpu.VMEM((4, 2, 64, 2 * SLOTS), F32),
+        gates=pltpu.VMEM((4, 2, 64, 2 * SLOTS), F32),
+        k_send=DMA((2, 2)),
+        k_recv=DMA((4,)),
+        m_send=DMA((2, 2)),
+        m_recv=DMA((4,)),
+        swap_s=DMA((3,)),
+        swap_r=DMA((3,)),
     )
     for name in ("rows_a_", "rows_b_", "rows_s_"):
         scratch.update(rows_sems(name))
-    for name in ("q_spread", "g_spread", "f_spread"):
+    for name in ("kv_spread", "m_spread", "d_spread", "f_spread"):
         scratch.update(spread_sems(name))
     for name in ("gate", "deal"):
         scratch.update(shuffle_sems(name))
@@ -800,30 +932,34 @@
         1,
         {name: (value, ANY if name == "rows_b" else VMEM) for name, value in operands.items()},
         dict(
-            wide_q=((4, 4, 128, 3 * HALF), BF, VMEM),
-            wide_g=((4, 4, 128, 2 * HALF), BF, VMEM),
-            wide_f=((4, 4, 128, FFN), BF, ANY),
             first_own=((64, 2048), BF, VMEM),
             lowrank=((64, 16), F32, VMEM),
-            first=(rows, BF, VMEM),
-            cot=(rows, BF, ANY),
-            second=(rows, BF, VMEM),
-            gates=((4, 4, 64, 64), F32, VMEM),
-            qkv=((2, 4, 64, 3 * HALF), BF, VMEM),
+            resid1=((64, 2048), F32, VMEM),
+        ),
+        scratch,
+        saved=dict(
+            wide_k=((4, 4, 128, 2 * HALF), BF),
+            wide_m=((4, 4, 128, 3 * HALF), BF),
+            first=(rows, BF),
+            cot=(rows, BF),
+            second=(rows, BF),
+            gate=((4, 4, 64, SLOTS), F32),
+            qkv=((2, 4, 64, 3 * HALF), BF),
             cum=square,
             near=square,
             far=square,
             probs=square,
             mixing=square,
-            decays=((4, SLOTS, 128), F32, VMEM),
-            states=((4, SLOTS, 1024), F32, VMEM),
-            mixed=((4, 64, DK), F32, VMEM),
-            gate_lin=((2, 4, 64, HALF), F32, VMEM),
-            headnorm=((2, 4, 64, HALF), F32, VMEM),
-            branch=((2, 4, 64, HALF), BF, VMEM),
-            resid1=((64, 2048), F32, VMEM),
+            decays=((4, SLOTS, 128), F32),
+            states=((4, SLOTS, 1024), F32),
+            mixed=((4, 64, DK), F32),
+            gate_lin=((2, 4, 64, HALF), F32),
+            headnorm=((2, 4, 64, HALF), F32),
+            branch=((2, 4, 64, HALF), BF),
+            acts=((3, 2, 4, 64, UNITS_PAD), BF),
+            second_part=(rows, BF),
+            ffn_part=(rows, BF),
         ),
-        scratch,
     )
 
 
@@ -852,25 +988,31 @@
     def mine(self, side, k):
         return self.own.at[side, k] if self.loaded else self.block(side, k, 0)
 
-    def load(self):
+    def load(self, side, k):
         if self.loaded:
-            for k in (1, 2, 3, 0):
-                for side in range(2):
-                    self.owns[side, k] = pltpu.make_async_copy(
-                        self.block(side, k, 0), self.own.at[side, k], self.own_sem.at[side, k]
-                    )
-                    self.owns[side, k].start()
-
-    def send(self, k):
-        for d in range(1, 4):
-            for side in range(2):
-                self.fars[side, k, d] = push(
-                    self.block(side, k, d),
-                    self.far.at[side, k, d - 1],
-                    self.sems[0].at[side, k, d - 1],
-                    self.sems[1].at[side, k, d - 1],
-                    self.peer(side, d),
-                )
+            self.owns[side, k] = pltpu.make_async_copy(
+                self.block(side, k, 0), self.own.at[side, k], self.own_sem.at[side, k]
+            )
+            self.owns[side, k].start()
+
+    def push_one(self, side, k, d):
+        self.fars[side, k, d] = push(
+            self.block(side, k, d),
+            self.far.at[side, k, d - 1],
+            self.sems[0].at[side, k, d - 1],
+            self.sems[1].at[side, k, d - 1],
+            self.peer(side, d),
+        )
+
+    def send(self, e):
+        for k in (1, 2, 3, 0):
+            if e > 0:
+                self.push_one(0, k, e)
+            else:
+                self.load(0, k)
+            if k > 0:
+                self.push_one(1, e, k)
+        self.load(1, e)
 
     def arrive(self, side, k):
         if self.loaded:
@@ -1056,34 +1198,41 @@
     partner = (x, y, z, 1 - c)
     scan = Scan(r, True)
     greet(all_peers())
+    mine = pltpu.make_async_copy(r.second_part.at[c], r.mine, r.mine_s.at[0])
+    mine.start()
+    r.start()
     greeted(all_peers())
-    second = RowSum(r, "sec", r.second_part, lambda k: r.second_mine[k])
-    ffn = RowSum(r, "ffn", r.ffn_part, lambda k: r.ffn_mine[k])
-    one = WeightSum(r, "one", r.grads_one, 6 * HALF, True)
-    two = WeightSum(r, "two", r.grads_two, 3 * HALF, True)
+    second = RowSum(r, "sec", r.second_part, lambda k: r.mine[k])
+    ffn = RowSum(r, "ffn", r.ffn_part, lambda k: r.mine[k])
+    units = WeightSum(r, "units", r.out_grads, FFN, True)
     tail = WeightSum(r, "tail", r.grads_tail, 2 * HALF, False)
     last = WeightSum(r, "last", r.grads_last, 3 * HALF, False)
     second.pairs()
-    mine = [
-        pltpu.make_async_copy(part.at[c], dst, r.mine_s.at[n])
-        for n, (part, dst) in enumerate(
-            ((r.second_part, r.second_mine), (r.ffn_part, r.ffn_mine))
-        )
-    ]
-    for copy in mine:
-        copy.start()
-    one.load()
-    for k in (1, 2, 3, 0):
-        one.send(k)
-    for copy in mine:
-        copy.wait()
+    mine.wait()
     second.hops()
-    two.load()
-    for k in (1, 2, 3, 0):
-        two.send(k)
+
+    r.need("acts", "second", "cot")
+    for e in (1, 2, 3, 0):
+        at = wrap(x + e)
+        steps = [
+            pltpu.make_async_copy(
+                r.grads_last.at[n], r.out_grads.at[at, :, :, pl.ds(n * UNITS_PAD, UNITS_PAD)], r.stage_s.at[n]
+            )
+            for n in range(3)
+        ]
+        for n, left in enumerate((r.second, r.second, r.cot)):
+            got = tn(left[:, :, :, tile(at, 512)].reshape(512, 512), all_rows(r.acts, n))
+            r.grads_last[n] = got.astype(BF).reshape(4, 128, UNITS_PAD)
+            steps[n].start()
+        for copy in steps:
+            copy.wait()
+        units.send(e)
+    r.need("resid1", "cot_own")
     e = second.result()
-    v = r.resid1[...]
-    grad, d_norm2 = rms_back(v, r.norm2_gain[...], e)
+    second.done()
+    mine = pltpu.make_async_copy(r.ffn_part.at[c], r.mine, r.mine_s.at[1])
+    mine.start()
+    grad, d_norm2 = rms_back(r.resid1[...], r.norm2_gain[...], e)
     r.small[...] = jnp.zeros_like(r.small)
     r.small[17:18, 0:2048] = d_norm2
     grad_resid1 = r.cot_own[...].astype(F32) + grad
@@ -1094,33 +1243,26 @@
     rows_finish(a_rows, r.attn, a_sems)
     ffn.pairs()
 
-    attn = r.attn[...].reshape(512, 2048)
-    grad_branch = dot(attn, r.wide_g[:, :, :, HALF : 2 * HALF].reshape(2048, HALF))
-    lin = r.gate_lin[...].reshape(512, HALF)
+    r.need("wide_m", "gate_lin", "headnorm")
+    grad_branch = dot(all_rows(r.attn), columns(r.wide_m, pl.ds(2 * HALF, HALF)))
+    lin, normed = all_rows(r.gate_lin), all_rows(r.headnorm)
     sig = jax.nn.sigmoid(lin)
-    normed = r.headnorm[...].reshape(512, HALF)
-    r.grad_lin[...] = (
-        (grad_branch * normed * sig * (1 + lin * (1 - sig))).astype(BF).reshape(2, 4, 64, HALF)
-    )
+    grad_lin = (grad_branch * normed * sig * (1 + lin * (1 - sig))).astype(BF)
+    r.grad_lin[...] = grad_lin.reshape(2, 4, 64, HALF)
     r.grad_out[...] = (grad_branch * lin * sig).reshape(2, 4, 64, HALF)
     swap = push(r.grad_out.at[1 - c], r.grad_norm.at[c], r.swap_s.at[0], r.swap_r.at[0], partner)
     r.grad_norm[c] = r.grad_out[c]
+    r.need("mixed", "qkv", "cum", "gate", "probs", "states", "decays")
     swap.wait()
+    mine.wait()
     ffn.hops()
-
-    def all_rows(ref):
-        return ref[...].reshape(512, ref.shape[-1])
-
-    def weight_rows(ref, n):
-        return ref[:, :, :, pl.ds(pl.multiple_of(n * 512, 512), 512)].reshape(512, 512)
 
     r.d_head[...] = jnp.zeros_like(r.d_head)
 
     @pl.loop(0, 4)
     def _(n):
-        mixed = r.mixed[n]
         e = jnp.concatenate([r.grad_norm[0, n], r.grad_norm[1, n]], axis=1)
-        grad, d_head = rms_back(mixed, r.head_gain[...], e)
+        grad, d_head = rms_back(r.mixed[n], r.head_gain[...], e)
         r.d_head[0:1] += d_head
         g = grad.astype(BF)
         r.grad_mixed[n] = g
@@ -1129,8 +1271,8 @@
             features(r.qkv, n, 2),
             g,
             r.cum[n],
-            r.gates[n, 1],
-            r.gates[n, 3],
+            gate_of(r, n, 1),
+            gate_of(r, n, 3),
             r.probs[n],
             r.states[n],
         )
@@ -1143,19 +1285,35 @@
 
     @pl.loop(0, 4)
     def _(n):
-        r.grads_tail[n, :, :, 0:HALF] = (
-            tn(weight_rows(r.first, n), all_rows(r.grad_lin)).astype(BF).reshape(4, 128, HALF)
-        )
-        r.grads_tail[n, :, :, HALF : 2 * HALF] = (
-            tn(weight_rows(r.attn, n), all_rows(r.branch)).astype(BF).reshape(4, 128, HALF)
+        r.daff[n], r.fresh[n] = chunk_pairs(
+            features(r.qkv, n, 0),
+            features(r.qkv, n, 1),
+            r.cum[n],
+            gate_of(r, n, 1),
+            gate_of(r, n, 3),
+            r.dmix[n],
+            r.dscore[n],
+            r.probs[n],
         )
 
     scan.middle()
     for k in range(1, 4):
-        one.turn(k)
+        units.turn(k)
+    r.need("first", "branch")
+
+    @pl.loop(0, 4)
+    def _(n):
+        got = tn(r.first[:, :, :, tile(n, 512)].reshape(512, 512), all_rows(r.grad_lin))
+        r.grads_tail[n, :, :, 0:HALF] = got.astype(BF).reshape(4, 128, HALF)
+        got = tn(r.attn[:, :, :, tile(n, 512)].reshape(512, 512), all_rows(r.branch))
+        r.grads_tail[n, :, :, HALF : 2 * HALF] = got.astype(BF).reshape(4, 128, HALF)
+
+    r.need("near", "far", "mixing")
     scan.fold(r.nexts)
-    for k in (1, 2, 3, 0):
-        tail.send(k)
+    for e in (1, 2, 3, 0):
+        tail.send(e)
+    r.output[...] = (r.resid1[...] + ffn.result()).astype(BF)
+    ffn.done()
 
     @pl.loop(0, 4)
     def _(n):
@@ -1164,20 +1322,21 @@
             features(r.qkv, n, 1),
             features(r.qkv, n, 2),
             r.grad_mixed[n],
-            r.gates[n, 0],
-            r.gates[n, 1],
-            r.gates[n, 2],
-            r.gates[n, 3],
+            gate_of(r, n, 0),
+            gate_of(r, n, 1),
+            gate_of(r, n, 2),
+            gate_of(r, n, 3),
             r.cum[n],
             r.near[n],
             r.far[n],
             r.probs[n],
             r.mixing[n],
             r.states[n],
-            r.dmix[n],
             r.dfar[n],
             r.dnear[n],
             r.dscore[n],
+            r.daff[n],
+            r.fresh[n],
             r.nexts[n],
         )
         for m, part in enumerate((dq, dk, dv)):
@@ -1190,47 +1349,40 @@
     swap2 = push(r.dproj.at[1 - c], r.dqkv.at[c], r.swap_s.at[1], r.swap_r.at[1], partner)
     r.dqkv[c] = r.dproj[c]
     logits = shuffle_start(lambda k: r.dlogit.at[k], r.dl.at[z], *sems_of(r, "gate", 3))
-    for k in range(1, 4):
-        two.turn(k)
     swap2.wait()
 
-    @pl.loop(0, 4)
-    def _(n):
-        r.grads_last[n] = (
-            tn(weight_rows(r.first, n), all_rows(r.dqkv)).astype(BF).reshape(4, 128, 3 * HALF)
-        )
-
-    for k in (1, 2, 3, 0):
-        last.send(k)
+    for e in (1, 2, 3, 0):
+        at = wrap(x + e)
+        got = tn(r.first[:, :, :, tile(at, 512)].reshape(512, 512), all_rows(r.dqkv))
+        r.grads_last[at] = got.astype(BF).reshape(4, 128, 3 * HALF)
+        last.send(e)
+    r.need("wide_k")
     first_part = r.attn
     first = RowSum(r, "fst", first_part, lambda k: first_part[c, k])
     for core in (1 - c, c):
 
         @pl.loop(0, 4)
         def _(n):
-            got = nt(
-                r.dqkv[core].reshape(256, 3 * HALF), r.wide_q[n].reshape(512, 3 * HALF)
-            ) + nt(
-                r.grad_lin[core].reshape(256, HALF),
-                r.wide_g[n, :, :, 0:HALF].reshape(512, HALF),
-            )
-            cols = pl.ds(pl.multiple_of(n * 512, 512), 512)
-            first_part[core, :, :, cols] = got.astype(BF).reshape(4, 64, 512)
+            dqkv = r.dqkv[core].reshape(256, 3 * HALF)
+            got = nt(dqkv[:, HALF:], r.wide_k[n].reshape(512, 2 * HALF))
+            left = jnp.concatenate([dqkv[:, 0:HALF], r.grad_lin[core].reshape(256, HALF)], axis=1)
+            got = got + nt(left, r.wide_m[n, :, :, 0 : 2 * HALF].reshape(512, 2 * HALF))
+            first_part[core, :, :, tile(n, 512)] = got.astype(BF).reshape(4, 64, 512)
 
         if core is not c:
             first.pairs()
 
+    shuffle_wait(logits)
     first.hops()
-
     for k in range(1, 4):
         tail.turn(k)
 
-    shuffle_wait(logits)
+    r.need("lowrank", "up", "down", "first_own", "inputs")
     low = jnp.zeros((64, 16), F32)
     bias = []
     for h in range(4):
         dl = r.dl[h]
-        low = low + nt(dl, r.up[h], HIGH)
+        low = low + nt(dl, r.up[:, h * SLOTS : (h + 1) * SLOTS].astype(F32), HIGH)
         r.small[0:16, 2048 + h * 64 : 2112 + h * 64] = tn(r.lowrank[...], dl, HIGH)
         bias.append(jnp.sum(dl, axis=0, keepdims=True))
     r.small[18:19, 512:768] = jnp.concatenate(bias, axis=1)
@@ -1238,7 +1390,13 @@
     small = SmallSum(r, "sml", r.small, r.small_out)
     small.pair()
     small.send(0)
-    grad_first = first.result() + dot(low, r.down[...], precision=HIGH)
+    units.finish()
+    units_back = shuffle_start(
+        lambda k: units.ready.at[pl.ds(pl.multiple_of(k * 32, 32), 32), :],
+        r.units_out.at[z],
+        *sems_of(r, "back", 3),
+    )
+    grad_first = first.result() + dot(low, r.down[...].astype(F32), precision=HIGH)
     grad, d_norm1 = rms_back(r.inputs[...].astype(F32), r.norm1_gain[...], grad_first)
     r.d_inputs[...] = r.grad_resid1[...] + grad
     r.tiny[...] = jnp.zeros_like(r.tiny)
@@ -1246,42 +1404,28 @@
     tiny = SmallSum(r, "tny", r.tiny, r.tiny_out)
     tiny.pair()
     tiny.send(0)
-    one.finish()
-    one_back = shuffle_start(
-        lambda k: one.ready.at[pl.ds(pl.multiple_of(k * 32, 32), 32), :],
-        r.out_one.at[z],
-        *sems_of(r, "back_one", 3),
-    )
-    two.finish()
-    two_back = shuffle_start(
-        lambda k: two.ready.at[pl.ds(pl.multiple_of(k * 32, 32), 32), :],
-        r.out_two.at[z],
-        *sems_of(r, "back_two", 3),
-    )
     small.send(1)
+    for k in range(1, 4):
+        last.turn(k)
     tiny.send(1)
     tail.finish()
-    tail_back = return_start(tail.ready, r.out_tail, r.tail_send, r.tail_recv)
-    r.output[...] = (r.resid1[...] + ffn.result()).astype(BF)
-    for k in range(1, 4):
-        last.turn(k)
+    tail_back = return_start(tail.ready, r.tail_out, r.tail_send, r.tail_recv)
     small.send(2)
+    last.finish()
+    last_back = return_start(last.ready, r.last_out, r.last_send, r.last_recv)
     tiny.send(2)
-    last.finish()
-    last_back = return_start(last.ready, r.out_last, r.last_send, r.last_recv)
     small.close()
     tiny.close()
-    for sent in (one_back, two_back):
-        shuffle_wait(sent)
-        shuffle_done(sent)
+    shuffle_wait(units_back)
+    shuffle_done(units_back)
     shuffle_done(logits)
-    return_wait(tail.ready, r.out_tail, r.tail_recv)
-    return_wait(last.ready, r.out_last, r.last_recv)
+    return_wait(tail.ready, r.tail_out, r.tail_recv)
+    return_wait(last.ready, r.last_out, r.last_recv)
     deal_done(tail_back)
     deal_done(last_back)
     small.done()
     tiny.done()
-    for part in (second, ffn, first, one, two, tail, last, scan):
+    for part in (first, units, tail, last, scan):
         part.done()
 
 
@@ -1303,14 +1447,16 @@
         dfar=small,
         dnear=small,
         dscore=small,
+        daff=small,
+        fresh=small,
         dlogit=small,
         dl=small,
         nexts=pltpu.VMEM((4, SLOTS, 1024), F32),
         dproj=pltpu.VMEM((2, 4, 64, 3 * HALF), BF),
         dqkv=pltpu.VMEM((2, 4, 64, 3 * HALF), BF),
-        second_mine=pltpu.VMEM((4, 64, 2048), BF),
-        ffn_mine=pltpu.VMEM((4, 64, 2048), BF),
+        mine=pltpu.VMEM((4, 64, 2048), BF),
         mine_s=DMA((2,)),
+        stage_s=DMA((3,)),
         grads_tail=pltpu.VMEM((4, 4, 128, 2 * HALF), BF),
         grads_last=pltpu.VMEM((4, 4, 128, 3 * HALF), BF),
         swap_s=DMA((2,)),
@@ -1321,42 +1467,54 @@
         last_recv=DMA((2, 2)),
     )
     for name, cols, loaded in (
-        ("one", 6 * HALF, True),
-        ("two", 3 * HALF, True),
+        ("units", FFN, True),
         ("tail", 2 * HALF, False),
         ("last", 3 * HALF, False),
     ):
         scratch.update(weight_scratch(name, cols, loaded))
-    for name in ("sec", "ffn", "fst"):
-        scratch.update(sum_scratch(name))
-    for name in ("gate", "back_one", "back_two"):
+    scratch.update(sum_scratch("sec", "ffn", "fst"))
+    for name in ("gate", "back"):
         scratch.update(shuffle_sems(name))
     scratch.update(rows_sems("rows_a_"))
     scratch.update(scan_scratch())
     scratch.update(small_scratch("sml", 24, 2304))
     scratch.update(small_scratch("tny", 8, 2048))
-    in_hbm = ("grads_one", "grads_two", "second_part", "ffn_part")
+    in_hbm = ("second_part", "ffn_part")
+    in_vmem = ("norm1_gain", "norm2_gain", "head_gain")
+    order = ("acts", "second", "cot", "resid1", "cot_own", "wide_m", "gate_lin", "headnorm")
+    order += tuple(name for name in operands if name not in order + in_hbm + in_vmem)
+    direct = {name: (operands[name], ANY) for name in in_hbm}
+    direct.update({name: (operands[name], VMEM) for name in in_vmem})
     return remote_call(
         backward_kernel,
         2,
-        {name: (value, ANY if name in in_hbm else VMEM) for name, value in operands.items()},
+        direct,
         dict(
             output=((64, 2048), BF, VMEM),
             d_inputs=((64, 2048), F32, VMEM),
-            out_last=((2, 2, 32, 3 * HALF), BF, VMEM),
-            out_tail=((2, 2, 32, 2 * HALF), BF, VMEM),
-            out_one=((4, 32, 6 * HALF), BF, VMEM),
-            out_two=((4, 32, 3 * HALF), BF, VMEM),
+            last_out=((2, 2, 32, 3 * HALF), BF, VMEM),
+            tail_out=((2, 2, 32, 2 * HALF), BF, VMEM),
+            units_out=((4, 32, FFN), BF, VMEM),
             small_out=((24, 2304), F32, VMEM),
             tiny_out=((8, 2048), F32, VMEM),
+            out_grads=((4, 4, 128, FFN), BF, ANY),
         ),
         scratch,
+        loaded={name: operands[name] for name in order},
     )
 
 
-def results_kernel(
-    out, d_in, last, tail, one, two, small, tiny, output, d_inputs, norm1, q, k, v, g, o, down, up, bias, head, norm2, fg, fu, fd
-):
+def results_kernel(*refs):
+    sources, outs, held, sems = refs[:7], refs[7:23], refs[23:30], refs[30]
+    copies = [
+        pltpu.make_async_copy(src, dst, sems.at[n]) for n, (src, dst) in enumerate(zip(sources, held))
+    ]
+    for copy in copies:
+        copy.start()
+    for copy in copies:
+        copy.wait()
+    out, d_in, last, tail, units, small, tiny = held
+    output, d_inputs, norm1, q, k, v, g, o, down, up, bias, head, norm2, fg, fu, fd = outs
     output[...] = out[...]
     d_inputs[...] = d_in[...]
     for j in range(2):
@@ -1365,14 +1523,11 @@
             for m, ref in enumerate((q, k, v)):
                 ref[:, at] = last[j, n, :, m * HALF : (m + 1) * HALF].astype(F32)
             g[:, at] = tail[j, n, :, 0:HALF].astype(F32)
-            row = lax.broadcasted_iota(jnp.int32, (HALF, HALF), 0)
-            col = lax.broadcasted_iota(jnp.int32, (HALF, HALF), 1)
-            o[at, :] = nt((row == col).astype(BF), tail[j, n, :, HALF : 2 * HALF])
+            o[:, at] = tail[j, n, :, HALF : 2 * HALF].astype(F32)
     for n in range(4):
         at = slice(n * UNITS, (n + 1) * UNITS)
-        fg[:, at] = one[n, :, 0:UNITS].astype(F32)
-        fu[:, at] = one[n, :, UNITS_PAD : UNITS_PAD + UNITS].astype(F32)
-        fd[:, at] = two[n, :, 0:UNITS].astype(F32)
+        for m, ref in enumerate((fg, fu, fd)):
+            ref[:, at] = units[n, :, m * UNITS_PAD : m * UNITS_PAD + UNITS].astype(F32)
     norm1[...] = tiny[0:1, :]
     norm2[...] = small[17:18, 0:2048]
     head[...] = small[18:19, 0:512]
@@ -1383,17 +1538,19 @@
 
 def results(b):
     shapes = [((64, 2048), BF), ((64, 2048), F32), ((1, 2048), F32)]
-    shapes += [((32, 1024), F32)] * 4 + [((1024, 32), F32), ((16, 2048), F32), ((16, 256), F32)]
+    shapes += [((32, 1024), F32)] * 5 + [((16, 2048), F32), ((16, 256), F32)]
     shapes += [((1, 256), F32), ((1, 512), F32), ((1, 2048), F32)] + [((32, 4 * UNITS), F32)] * 3
-    names = ("output", "d_inputs", "out_last", "out_tail", "out_one", "out_two")
-    names += ("small_out", "tiny_out")
+    names = ("output", "d_inputs", "last_out", "tail_out", "units_out", "small_out", "tiny_out")
+    sources = [b[name] for name in names]
     call = pl.pallas_call(
         results_kernel,
         out_shape=[jax.ShapeDtypeStruct(shape, dtype) for shape, dtype in shapes],
-        compiler_params=pltpu.CompilerParams(vmem_limit_bytes=32 * 2**20),
+        in_specs=[ANY] * 7,
+        scratch_shapes=[pltpu.VMEM(v.shape, v.dtype) for v in sources] + [DMA((7,))],
+        compiler_params=pltpu.CompilerParams(vmem_limit_bytes=63 * 2**20),
     )
-    out = list(call(*[b[name] for name in names]))
-    out[8] = out[8].T
+    out = list(call(*sources))
+    out[7], out[8] = out[7].T, out[8].T
     for n in (2, 10, 11, 12):
         out[n] = out[n][0]
     return tuple(out)
@@ -1435,14 +1592,14 @@
             key_weight=key_weight,
             value_weight=value_weight,
             gate_weight=gate_weight,
-            out_weight=out_weight,
+            out_weight=out_weight.T,
             ffn_gate=ffn_gate,
             ffn_up=ffn_up,
             ffn_down=ffn_down,
             inputs=inputs,
             rows_b=cotangent,
             offsets=offsets[None],
-            low_down=low_down,
+            low_down=low_down.T,
             low_up=low_up,
             forget_bias=forget_bias[None],
             norm1_gain=gain1,
@@ -1451,39 +1608,17 @@
         )
     )
 
-    second, cot = f["second"].reshape(512, 2048), f["cot"].reshape(512, 2048)
-    wide_f = f["wide_f"].reshape(2048, FFN)
-    w_gate, w_up, w_down = (wide_f[:, n * UNITS_PAD : (n + 1) * UNITS_PAD] for n in range(3))
-    act_gate, act_up = dot(second, w_gate), dot(second, w_up)
-    sig = jax.nn.sigmoid(act_gate)
-    silu = act_gate * sig
-    hidden = (silu * act_up).astype(BF)
-    grad_hidden = dot(cot, w_down)
-    grad_gate = (grad_hidden * act_up * sig * (1 + act_gate * (1 - sig))).astype(BF)
-    grad_up = (grad_hidden * silu).astype(BF)
-    ffn_part = nt(hidden, w_down).astype(BF).reshape(2, 4, 64, 2048)
-    grad_acts = jnp.concatenate([grad_gate, grad_up], axis=1)
-    second_part = nt(grad_acts, wide_f[:, : 2 * UNITS_PAD]).astype(BF).reshape(2, 4, 64, 2048)
-    grads_one = tn(second, grad_acts).astype(BF).reshape(4, 4, 128, 2 * UNITS_PAD)
-    grads_two = tn(cot, hidden).astype(BF).reshape(4, 4, 128, UNITS_PAD)
-
-    done = ("wide_f", "cot", "second")
-    operands = {name: value for name, value in f.items() if name not in done}
-    operands.update(
-        grads_one=grads_one,
-        grads_two=grads_two,
-        second_part=second_part,
-        ffn_part=ffn_part,
+    operands = dict(
+        f,
         cot_own=cotangent,
         inputs=inputs,
-        up=low_up.astype(F32).reshape(16, 4, SLOTS).transpose(1, 0, 2),
-        down=low_down.astype(F32).T,
+        up=low_up,
+        down=low_down.T,
         norm1_gain=gain1,
         norm2_gain=gain2,
         head_gain=gain_head,
     )
     b = backward(operands)
-
     return results(b)
 
 

time: 319 us -> 282 us (0.88)
  matrix products: 27.1 us -> 0 us
  local copies, waits for them, and re-layouts: 13.4 us -> 0 us
  Pallas kernels: 276 us -> 281 us
    dot_general x7 -> x0, matrix products: 27.1 us -> none  [dot(): lax.dot_general(left, right, (dims, ((), ())), precision=precision, prefe...]
    unnamed x29 -> x0, local copies, waits for them, and re-layouts: 12.7 us -> none
where the time goes in v4:
time: 282 us; the launch traced here: 281 us
  Pallas kernels  281 us (100%)
    pallas_call x2, Pallas kernels, remote_call(): pl.pallas_call(run, out_shape=[jax.ShapeDtypeStruct(shape, dtype) for sha...  277 us

profile of v4, /device:TPU:1, one launch (start us, length us, event | category | flops | bytes accessed | tf_op | source)
XLA Modules:
  0.0 281.4 jit_solution(9460646265672744347)
XLA Ops:
  0.6 140.5 %shard_map.288 = (bf16[64,2048]{1,0:T(8,128)(2,1)}, f32[64,16]{1,0:T(8,128)}, f32[64,2048]{1,0:T(8,128)}, bf16[4,4,128,512]{3,2,1,0:T(8,128)(2,1)}, bf16[4,4,128...) custom-call(bf16[32,1024]{1,0:T(8,128)(2,1)} %refs_0_.1, ...), custom_call_target="tpu_custom_call" | custom-call | tf_op jit(solution)/shard_map/pallas_call | solution.py:121
  141.2 136.9 %shard_map.289 = (bf16[64,2048]{1,0:T(8,128)(2,1)}, f32[64,2048]{1,0:T(8,128)}, bf16[2,2,32,768]{3,2,1,0:T(8,128)(2,1)}, bf16[2,2,32,512]{3,2,1,0:T(8,128)(2,1)}...) custom-call(bf16[2,4,64,2048]{3,2,1,0:T(8,128)(2,1)} %get-tuple-elem, ...), custom_call_target="tpu_custom_call" | custom-call | tf_op jit(solution)/shard_map/pallas_call | solution.py:121
  278.0 3.2 %shard_map.290 = (bf16[64,2048]{1,0:T(8,128)(2,1)}, f32[64,2048]{1,0:T(8,128)}, f32[1,2048]{1,0:T(1,128)}, f32[32,1024]{1,0:T(8,128)}, f32[32,1024]{1,0:T(8,128)...) custom-call(bf16[64,2048]{1,0:T(8,128)(2,1)} %get-tuple-element.87.r, ...), custom_call_target="tpu_custom_call" | custom-call | tf_op jit(solution)/shard_map/pallas_call | solution.py:1552

commit v5 on v4

--- a/solution.py
+++ b/solution.py
@@ -132,71 +132,93 @@
 
 
 class Spread:
-    def __init__(self, r, name, ref, start, width):
-        self.ref, self.start, self.half = ref, start, width // 2
+    def __init__(self, r, name, ref, start, width, ring=True):
+        self.ref, self.start, self.half, self.ring = ref, start, width // 2, ring
         self.sems = sems_of(r, name, 4)
-        self.nears, self.fars = {}, []
-
-    def block(self, side, k):
+        self.nears, self.fars, self.arrived = {}, {}, set()
+
+    def block(self, side, k, d=0, rows=slice(None)):
         x, y, z, c = here()
         part = pl.ds(self.start + side * self.half, self.half)
         if side == 0:
-            return self.ref.at[x, wrap(y - k), :, part]
-        return self.ref.at[wrap(x - k), y, :, part]
+            return self.ref.at[wrap(x + d), wrap(y - k), rows, part]
+        return self.ref.at[wrap(x - k), wrap(y + d), rows, part]
+
+    def peer(self, side, d):
+        x, y, z, c = here()
+        return (wrap(x + d), y, z, c) if side == 0 else (x, wrap(y + d), z, c)
 
     def near(self):
-        x, y, z, c = here()
         for d in range(1, 4):
             for side in range(2):
                 block = self.block(side, 0)
-                peer = (x, wrap(y + d), z, c) if side == 0 else (wrap(x + d), y, z, c)
                 self.nears[side, d] = push(
-                    block, block, self.sems[0].at[side, d - 1], self.sems[1].at[side, d - 1], peer
+                    block,
+                    block,
+                    self.sems[0].at[side, d - 1],
+                    self.sems[1].at[side, d - 1],
+                    self.peer(1 - side, d),
                 )
 
+    def pass_on(self, key, block, d):
+        side, k, n = key
+        self.fars[key] = push(
+            block, block, self.sems[2].at[side, k, n], self.sems[3].at[side, k, n], self.peer(side, d)
+        )
+
     def far(self, *steps):
-        x, y, z, c = here()
         for k in steps:
             for side in range(2):
                 if k > 0:
                     self.nears[side, k].wait_recv()
-                block = self.block(side, k)
-                for d in range(1, 4):
-                    peer = (wrap(x + d), y, z, c) if side == 0 else (x, wrap(y + d), z, c)
-                    self.fars.append(
-                        push(
-                            block,
-                            block,
-                            self.sems[2].at[side, k, d - 1],
-                            self.sems[3].at[side, k, d - 1],
-                            peer,
-                        )
-                    )
+                for d in (1, 3) if self.ring else (1, 3, 2):
+                    self.pass_on((side, k, d - 1), self.block(side, k), d)
+
+    def wait(self, key):
+        if key not in self.arrived:
+            self.arrived.add(key)
+            self.fars[key].wait_recv()
+
+    def relay(self, *steps):
+        for k in steps:
+            for side in range(2):
+                self.wait((side, k, 0))
+                self.pass_on((side, k, 1), self.block(side, k, -1, pl.ds(0, 64)), 1)
+                self.wait((side, k, 2))
+                self.pass_on((side, k, 3), self.block(side, k, 1, pl.ds(64, 64)), 3)
 
     def arrive(self):
-        for copy in self.fars:
-            copy.wait_recv()
+        for key in self.fars:
+            self.wait(key)
 
     def done(self):
-        for copy in list(self.nears.values()) + self.fars:
+        for copy in list(self.nears.values()) + list(self.fars.values()):
             copy.wait_send()
 
 
 def spread_sems(name):
-    kinds = ((2, 3), (2, 3), (2, 4, 3), (2, 4, 3))
+    kinds = ((2, 3), (2, 3), (2, 4, 4), (2, 4, 4))
     return {f"{name}{n}": DMA(shape) for n, shape in enumerate(kinds)}
 
 
 def rows_start(src, out, sems):
     x, y, z, c = here()
     hop_s, hop_r, pair_s, pair_r, own = sems
+    half = src.shape[0] // 2
     mine = pltpu.make_async_copy(src, out.at[c, z], own)
     mine.start()
-    hops = [
-        push(src, out.at[c, z], hop_s.at[d - 1], hop_r.at[d - 1], (x, y, wrap(z + d), c))
-        for d in range(1, 4)
-    ]
-    pairs = [push(src, out.at[c, z], pair_s.at[0], pair_r.at[0], (x, y, z, 1 - c))]
+    hops = {}
+    for h in range(2):
+        rows = pl.ds(h * half, half)
+        for d in range(1, 4):
+            hops[h, d] = push(
+                src.at[rows],
+                out.at[c, z, rows],
+                hop_s.at[h, d - 1],
+                hop_r.at[h, d - 1],
+                (x, y, wrap(z + d), c),
+            )
+    pairs = [push(src, out.at[c, z], pair_s.at[0, 3], pair_r.at[0, 3], (x, y, z, 1 - c))]
     return mine, hops, pairs
 
 
@@ -204,15 +226,23 @@
     x, y, z, c = here()
     hop_s, hop_r, pair_s, pair_r, own = sems
     mine, hops, pairs = started
-    for d in range(1, 4):
-        hops[d - 1].wait_recv()
-        block = out.at[c, wrap(z - d)]
-        pairs.append(push(block, block, pair_s.at[d], pair_r.at[d], (x, y, z, 1 - c)))
+    half = out.shape[2] // 2
+    for h, d in hops:
+        hops[h, d].wait_recv()
+        block = out.at[c, wrap(z - d), pl.ds(h * half, half)]
+        pairs.append(
+            push(block, block, pair_s.at[h, d - 1], pair_r.at[h, d - 1], (x, y, z, 1 - c))
+        )
     mine.wait()
-    for copy in hops:
+    for copy in hops.values():
         copy.wait_send()
     for copy in pairs:
         copy.wait()
+
+
+def rows_sems(name):
+    kinds = ((2, 3), (2, 3), (2, 4), (2, 4), ())
+    return {f"{name}{n}": DMA(shape) for n, shape in enumerate(kinds)}
 
 
 def group_peers():
@@ -234,11 +264,6 @@
 
 def all_peers():
     return group_peers() + plane_peers()
-
-
-def rows_sems(name):
-    kinds = ((3,), (3,), (4,), (4,), ())
-    return {f"{name}{n}": DMA(shape) for n, shape in enumerate(kinds)}
 
 
 def sems_of(r, name, count):
@@ -715,7 +740,7 @@
     greet(all_peers())
     prepare(r)
     greeted(all_peers())
-    kv = Spread(r, "kv_spread", r.wide_k, 0, 2 * HALF)
+    kv = Spread(r, "kv_spread", r.wide_k, 0, 2 * HALF, ring=False)
     mix = Spread(r, "m_spread", r.wide_m, 0, 3 * HALF)
     down = Spread(r, "d_spread", r.wide_f, 2 * UNITS_PAD, UNITS_PAD)
     acts = Spread(r, "f_spread", r.wide_f, 0, 2 * UNITS_PAD)
@@ -727,15 +752,15 @@
     a_rows = rows_start(r.first_own, r.first, a_sems)
     gates = shuffle_start(lambda k: r.packed.at[k], r.gates.at[z], *sems_of(r, "gate", 3))
     m_deal = deal_start(r.wm, r.wide_m, r.m_send, r.m_recv)
+    kv.far(1, 2, 3)
+    deal_wait(r.wm, r.wide_m, r.m_recv)
+    mix.near()
+    rows_finish(a_rows, r.first, a_sems)
     f_deal = shuffle_start(
         lambda k: r.wf.at[k],
         r.wide_f.at[x, y, pl.ds(pl.multiple_of(z * 32, 32), 32), :],
         *sems_of(r, "deal", 3),
     )
-    kv.far(1, 2, 3)
-    deal_wait(r.wm, r.wide_m, r.m_recv)
-    mix.near()
-    rows_finish(a_rows, r.first, a_sems)
     shuffle_wait(gates)
     for n in range(4):
         for kind in range(4):
@@ -759,6 +784,7 @@
     )
     r.qkv[c, :, :, key_value] = r.proj[c, :, :, key_value]
     shuffle_wait(f_deal)
+    down.near()
     swap.wait()
 
     @pl.loop(0, 4)
@@ -771,9 +797,10 @@
         r.decays[n] = ends[:, 1024:1152]
 
     scan.pair()
+    mix.relay(0, 1, 2, 3)
     scan.send()
-    down.near()
     acts.near()
+    acts.far(0)
     b_rows = rows_start(r.rows_b, r.cot, b_sems)
     mix.arrive()
     r.save("wide_m")
@@ -802,8 +829,8 @@
         )
 
     scan.fold(r.states)
+    acts.far(1, 2, 3)
     down.far(1, 2, 3)
-    acts.far(0, 1, 2, 3)
 
     @pl.loop(0, 4)
     def _(n):
@@ -826,6 +853,8 @@
     r.save("cum", "decays", "states", "near", "far", "probs", "mixing", "mixed", "gate_lin")
     rows_finish(b_rows, r.cot, b_sems)
     r.save("cot")
+    acts.relay(0)
+    down.relay(0)
     swap2.wait()
     sums = RowSum(r, "mix", r.parts, lambda k: r.parts[c, k])
     for core in (1 - c, c):
@@ -846,6 +875,8 @@
     r.resid1[...] = resid1
     r.second_own[...] = rms(resid1, r.norm2_gain[...]).astype(BF)
     s_rows = rows_start(r.second_own, r.second, s_sems)
+    down.relay(1, 2, 3)
+    acts.relay(1, 2, 3)
     down.arrive()
 
     @pl.loop(0, 3)
@@ -966,20 +997,21 @@
 class WeightSum:
     def __init__(self, r, name, grads, cols, loaded):
         self.grads, self.cols, self.half, self.loaded = grads, cols, cols // 2, loaded
-        self.far, self.landed, self.ready = sems_of(r, name + "b", 3)
-        self.own = getattr(r, name + "own") if loaded else None
-        self.sems = sems_of(r, name + "s", 4)
-        self.own_sem = getattr(r, name + "own_s") if loaded else None
-        self.fars, self.nears, self.owns = {}, {}, {}
+        self.far, self.landed, self.ready, self.past = sems_of(r, name + "b", 4)
+        self.sems = sems_of(r, name + "s", 6)
+        if loaded:
+            self.own, self.own_sem = getattr(r, name + "own"), getattr(r, name + "own_s")
+            self.held, self.held_sem = getattr(r, name + "held"), getattr(r, name + "held_s")
+        self.fars, self.nears, self.owns, self.pasts = {}, {}, {}, {}
 
     def part(self, side):
         return pl.ds(side * self.half, self.half)
 
-    def block(self, side, k, d):
+    def block(self, side, k, d, rows=slice(None)):
         x, y, z, c = here()
         if side == 0:
-            return self.grads.at[wrap(x + d), wrap(y + k), :, self.part(0)]
-        return self.grads.at[wrap(x + k), wrap(y + d), :, self.part(1)]
+            return self.grads.at[wrap(x + d), wrap(y + k), rows, self.part(0)]
+        return self.grads.at[wrap(x + k), wrap(y + d), rows, self.part(1)]
 
     def peer(self, side, d):
         x, y, z, c = here()
@@ -995,14 +1027,28 @@
             )
             self.owns[side, k].start()
 
-    def push_one(self, side, k, d):
-        self.fars[side, k, d] = push(
-            self.block(side, k, d),
-            self.far.at[side, k, d - 1],
-            self.sems[0].at[side, k, d - 1],
-            self.sems[1].at[side, k, d - 1],
+    def push_far(self, src, side, k, d, n, rows):
+        self.fars[side, k, n] = push(
+            src,
+            self.far.at[side, k, d // 2, rows],
+            self.sems[0].at[side, k, n],
+            self.sems[1].at[side, k, n],
             self.peer(side, d),
         )
+
+    def push_one(self, side, k, d):
+        if d == 2:
+            for n, to in enumerate((1, 3)):
+                self.pasts[side, k, n] = push(
+                    self.block(side, k, 2, pl.ds(n * 64, 64)),
+                    self.past.at[side, k, n],
+                    self.sems[4].at[side, k, n],
+                    self.sems[5].at[side, k, n],
+                    self.peer(side, to),
+                )
+        else:
+            rows = pl.ds(64 if d == 1 else 0, 64)
+            self.push_far(self.block(side, k, d, rows), side, k, d, d // 2, rows)
 
     def send(self, e):
         for k in (1, 2, 3, 0):
@@ -1014,15 +1060,49 @@
                 self.push_one(1, e, k)
         self.load(1, e)
 
+    def relay(self, order):
+        keys = [(side, k, n) for k in order for side in range(2) for n in range(2)]
+        loads = {}
+
+        def block(at):
+            side, k, n = keys[at]
+            return self.block(side, k, 2 * n + 1, pl.ds(n * 64, 64))
+
+        def fetch(at):
+            loads[at] = pltpu.make_async_copy(
+                block(at), self.held.at[at % 4], self.held_sem.at[at % 4]
+            )
+            loads[at].start()
+
+        if self.loaded:
+            for at in range(4):
+                fetch(at)
+        for at, (side, k, n) in enumerate(keys):
+            if self.loaded:
+                loads[at].wait()
+            self.pasts[side, k, n].wait_recv()
+            mine = self.held.at[at % 4] if self.loaded else block(at)
+
+            @pl.loop(0, 4)
+            def _(t):
+                rows = pl.ds(pl.multiple_of(t * 16, 16), 16)
+                both = self.past[side, k, n, rows, :].astype(F32) + mine[rows, :].astype(F32)
+                self.past[side, k, n, rows, :] = both.astype(BF)
+
+            rows = pl.ds(n * 64, 64)
+            self.push_far(self.past.at[side, k, n], side, k, 2 * n + 1, 2 + n, rows)
+            if self.loaded and at + 4 < len(keys):
+                fetch(at + 4)
+
     def arrive(self, side, k):
         if self.loaded:
             self.owns[side, k].wait()
-        for d in range(1, 4):
-            self.fars[side, k, d].wait_recv()
+        for n in range(4):
+            self.fars[side, k, n].wait_recv()
 
     def total(self, side, k, rows):
         value = self.mine(side, k)[rows, :].astype(F32)
-        for d in range(3):
+        for d in range(2):
             value = value + self.far[side, k, d, rows, :].astype(F32)
         return value
 
@@ -1058,24 +1138,26 @@
                 self.ready[rows, self.part(side)] = value.astype(BF)
 
     def done(self):
-        for copy in list(self.fars.values()) + list(self.nears.values()):
-            copy.wait_send()
+        for copies in (self.fars, self.nears, self.pasts):
+            for copy in copies.values():
+                copy.wait_send()
 
 
 def weight_scratch(name, cols, loaded):
     half = cols // 2
     out = {
-        f"{name}b0": pltpu.VMEM((2, 4, 3, 128, half), BF),
+        f"{name}b0": pltpu.VMEM((2, 4, 2, 128, half), BF),
         f"{name}b1": pltpu.VMEM((2, 3, 128, half), BF),
         f"{name}b2": pltpu.VMEM((128, cols), BF),
-        f"{name}s0": DMA((2, 4, 3)),
-        f"{name}s1": DMA((2, 4, 3)),
-        f"{name}s2": DMA((2, 3)),
-        f"{name}s3": DMA((2, 3)),
+        f"{name}b3": pltpu.VMEM((2, 4, 2, 64, half), BF),
     }
+    kinds = ((2, 4, 4), (2, 4, 4), (2, 3), (2, 3), (2, 4, 2), (2, 4, 2))
+    out.update({f"{name}s{n}": DMA(shape) for n, shape in enumerate(kinds)})
     if loaded:
         out[f"{name}own"] = pltpu.VMEM((2, 4, 128, half), BF)
         out[f"{name}own_s"] = DMA((2, 4))
+        out[f"{name}held"] = pltpu.VMEM((4, 64, half), BF)
+        out[f"{name}held_s"] = DMA((4,))
     return out
 
 
@@ -1114,82 +1196,44 @@
 
 
 class SmallSum:
-    def __init__(self, r, name, src, out):
-        self.src, self.out = src, out
-        self.held, self.now = sems_of(r, name + "b", 2)
-        self.sems = sems_of(r, name + "s", 4)
-        self.sends = []
-
-    def half(self, k):
-        width = self.src.shape[1] // 2
-        return pl.ds(pl.multiple_of(k * width, 128), width)
-
-    def pair(self):
-        x, y, z, c = here()
-        self.copy = push(
-            self.src.at[:, self.half(1 - c)],
-            self.held.at[0, c],
-            self.sems[0].at[0],
-            self.sems[1].at[0],
-            (x, y, z, 1 - c),
-        )
-        self.held[0, c] = self.src[:, self.half(c)]
-
-    def send(self, stage):
-        x, y, z, c = here()
-        if stage == 0:
-            self.copy.wait()
-            self.now[...] = self.held[0, 0] + self.held[0, 1]
-        else:
-            self.collect(stage)
-        at = (z, y, x)[stage]
-        self.held[stage + 1, at] = self.now[...]
+    def __init__(self, r, name, axes):
+        self.now, self.held, self.send, self.recv = sems_of(r, name, 4)
+        self.axes, self.sent = axes, []
+
+    def start(self, n):
+        place = dict(zip("xyzc", here()))
+        axis, at = self.axes[n], place[self.axes[n]]
+        size = 2 if axis == "c" else 4
+        self.held[n, at] = self.now[...]
         self.sent = []
-        for d in range(1, 4):
-            peer = [x, y, z, c]
-            peer[2 - stage] = wrap(at + d)
+        for d in range(1, size):
+            peer = dict(place)
+            peer[axis] = wrap(at + d, size)
             self.sent.append(
                 push(
-                    self.held.at[stage + 1, at],
-                    self.held.at[stage + 1, at],
-                    self.sems[2].at[stage, d - 1],
-                    self.sems[3].at[stage, d - 1],
-                    tuple(peer),
+                    self.held.at[n, at],
+                    self.held.at[n, at],
+                    self.send.at[n, d - 1],
+                    self.recv.at[n, d - 1],
+                    tuple(peer.values()),
                 )
             )
 
-    def collect(self, stage):
+    def collect(self, n):
         for copy in self.sent:
             copy.wait()
-        value = self.held[stage, 0]
-        for k in range(1, 4):
-            value = value + self.held[stage, k]
+        value = self.held[n, 0]
+        for k in range(1, 2 if self.axes[n] == "c" else 4):
+            value = value + self.held[n, k]
         self.now[...] = value
 
-    def close(self):
-        x, y, z, c = here()
-        self.collect(3)
-        self.out[:, self.half(c)] = self.now[...]
-        self.copy = push(
-            self.now,
-            self.out.at[:, self.half(c)],
-            self.sems[0].at[1],
-            self.sems[1].at[1],
-            (x, y, z, 1 - c),
-        )
-
-    def done(self):
-        self.copy.wait()
-
-
-def small_scratch(name, rows, cols):
+
+def small_scratch(name, rows, count):
     return {
-        f"{name}b0": pltpu.VMEM((4, 4, rows, cols // 2), F32),
-        f"{name}b1": pltpu.VMEM((rows, cols // 2), F32),
-        f"{name}s0": DMA((2,)),
-        f"{name}s1": DMA((2,)),
-        f"{name}s2": DMA((3, 3)),
-        f"{name}s3": DMA((3, 3)),
+        f"{name}0": pltpu.VMEM((rows, HALF), F32),
+        f"{name}1": pltpu.VMEM((count, 4, rows, HALF), F32),
+        f"{name}2": DMA((count, 3)),
+        f"{name}3": DMA((count, 3)),
     }
 
 
@@ -1233,8 +1277,16 @@
     mine = pltpu.make_async_copy(r.ffn_part.at[c], r.mine, r.mine_s.at[1])
     mine.start()
     grad, d_norm2 = rms_back(r.resid1[...], r.norm2_gain[...], e)
-    r.small[...] = jnp.zeros_like(r.small)
-    r.small[17:18, 0:2048] = d_norm2
+    group = SmallSum(r, "group", ("c", "z"))
+    plane = SmallSum(r, "plane", ("y", "x"))
+    tiny = SmallSum(r, "tiny", ("c", "z", "y", "x"))
+    group.now[...] = jnp.zeros_like(group.now)
+
+    def split_rows(dst, start, value):
+        for n in range(value.shape[1] // HALF):
+            dst[start + n : start + n + 1, :] = value[:, n * HALF : (n + 1) * HALF]
+
+    split_rows(group.now, 16, d_norm2)
     grad_resid1 = r.cot_own[...].astype(F32) + grad
     r.attn_own[...] = grad_resid1.astype(BF)
     r.grad_resid1[...] = grad_resid1
@@ -1242,6 +1294,7 @@
     a_rows = rows_start(r.attn_own, r.attn, a_sems)
     rows_finish(a_rows, r.attn, a_sems)
     ffn.pairs()
+    units.relay((1, 2, 3, 0))
 
     r.need("wide_m", "gate_lin", "headnorm")
     grad_branch = dot(all_rows(r.attn), columns(r.wide_m, pl.ds(2 * HALF, HALF)))
@@ -1252,6 +1305,17 @@
     r.grad_out[...] = (grad_branch * lin * sig).reshape(2, 4, 64, HALF)
     swap = push(r.grad_out.at[1 - c], r.grad_norm.at[c], r.swap_s.at[0], r.swap_r.at[0], partner)
     r.grad_norm[c] = r.grad_out[c]
+    r.need("first", "branch")
+
+    @pl.loop(0, 4)
+    def _(n):
+        got = tn(r.first[:, :, :, tile(n, 512)].reshape(512, 512), all_rows(r.grad_lin))
+        r.grads_tail[n, :, :, 0:HALF] = got.astype(BF).reshape(4, 128, HALF)
+        got = tn(r.attn[:, :, :, tile(n, 512)].reshape(512, 512), all_rows(r.branch))
+        r.grads_tail[n, :, :, HALF : 2 * HALF] = got.astype(BF).reshape(4, 128, HALF)
+
+    for e in (1, 2, 3, 0):
+        tail.send(e)
     r.need("mixed", "qkv", "cum", "gate", "probs", "states", "decays")
     swap.wait()
     mine.wait()
@@ -1280,11 +1344,10 @@
         r.every[c, n] = jnp.concatenate([ends_k, ends_v, r.decays[n]], axis=1)
 
     scan.pair()
-    r.small[18:19, 0:512] = r.d_head[0:1]
+    split_rows(group.now, 24, r.d_head[0:1])
     scan.send()
 
-    @pl.loop(0, 4)
-    def _(n):
+    def pairs_of(n):
         r.daff[n], r.fresh[n] = chunk_pairs(
             features(r.qkv, n, 0),
             features(r.qkv, n, 1),
@@ -1296,22 +1359,14 @@
             r.probs[n],
         )
 
+    pl.loop(0, 2)(pairs_of)
     scan.middle()
+    tail.relay((1, 2, 3, 0))
+    pl.loop(2, 4)(pairs_of)
     for k in range(1, 4):
         units.turn(k)
-    r.need("first", "branch")
-
-    @pl.loop(0, 4)
-    def _(n):
-        got = tn(r.first[:, :, :, tile(n, 512)].reshape(512, 512), all_rows(r.grad_lin))
-        r.grads_tail[n, :, :, 0:HALF] = got.astype(BF).reshape(4, 128, HALF)
-        got = tn(r.attn[:, :, :, tile(n, 512)].reshape(512, 512), all_rows(r.branch))
-        r.grads_tail[n, :, :, HALF : 2 * HALF] = got.astype(BF).reshape(4, 128, HALF)
-
     r.need("near", "far", "mixing")
     scan.fold(r.nexts)
-    for e in (1, 2, 3, 0):
-        tail.send(e)
     r.output[...] = (r.resid1[...] + ffn.result()).astype(BF)
     ffn.done()
 
@@ -1356,7 +1411,21 @@
         got = tn(r.first[:, :, :, tile(at, 512)].reshape(512, 512), all_rows(r.dqkv))
         r.grads_last[at] = got.astype(BF).reshape(4, 128, 3 * HALF)
         last.send(e)
-    r.need("wide_k")
+
+    shuffle_wait(logits)
+    r.need("lowrank", "up", "down", "inputs", "wide_k")
+    low = jnp.zeros((64, 16), F32)
+    bias = []
+    for h in range(4):
+        dl = r.dl[h]
+        low = low + nt(dl, r.up[:, h * SLOTS : (h + 1) * SLOTS].astype(F32), HIGH)
+        group.now[0:16, h * SLOTS : (h + 1) * SLOTS] = tn(r.lowrank[...], dl, HIGH)
+        bias.append(jnp.sum(dl, axis=0, keepdims=True))
+    split_rows(group.now, 26, jnp.concatenate(bias, axis=1))
+    r.low_own[...] = low
+    l_sems, d_sems = sems_of(r, "rows_l_", 5), sems_of(r, "rows_d_", 5)
+    l_rows = rows_start(r.low_own, r.lows, l_sems)
+    group.start(0)
     first_part = r.attn
     first = RowSum(r, "fst", first_part, lambda k: first_part[c, k])
     for core in (1 - c, c):
@@ -1371,51 +1440,54 @@
 
         if core is not c:
             first.pairs()
-
-    shuffle_wait(logits)
+            group.collect(0)
+            group.start(1)
+
     first.hops()
     for k in range(1, 4):
         tail.turn(k)
-
-    r.need("lowrank", "up", "down", "first_own", "inputs")
-    low = jnp.zeros((64, 16), F32)
-    bias = []
-    for h in range(4):
-        dl = r.dl[h]
-        low = low + nt(dl, r.up[:, h * SLOTS : (h + 1) * SLOTS].astype(F32), HIGH)
-        r.small[0:16, 2048 + h * 64 : 2112 + h * 64] = tn(r.lowrank[...], dl, HIGH)
-        bias.append(jnp.sum(dl, axis=0, keepdims=True))
-    r.small[18:19, 512:768] = jnp.concatenate(bias, axis=1)
-    r.small[0:16, 0:2048] = tn(low, r.first_own[...].astype(F32), HIGH)
-    small = SmallSum(r, "sml", r.small, r.small_out)
-    small.pair()
-    small.send(0)
+    last.relay((1, 2, 3, 0))
+    rows_finish(l_rows, r.lows, l_sems)
+    group.collect(1)
+    at = 2 * z + c
+    plane.now[0:32] = group.now[...]
+    plane.now[32:48] = tn(
+        r.lows[...].reshape(512, 16), all_rows(r.first, slice(None), slice(None), slice(None), tile(at)).astype(F32), HIGH
+    )
+    plane.start(0)
     units.finish()
     units_back = shuffle_start(
         lambda k: units.ready.at[pl.ds(pl.multiple_of(k * 32, 32), 32), :],
         r.units_out.at[z],
         *sems_of(r, "back", 3),
     )
+    tail.finish()
+    tail_back = return_start(tail.ready, r.tail_out, r.tail_send, r.tail_recv)
     grad_first = first.result() + dot(low, r.down[...].astype(F32), precision=HIGH)
     grad, d_norm1 = rms_back(r.inputs[...].astype(F32), r.norm1_gain[...], grad_first)
+    split_rows(tiny.now, 0, d_norm1)
+    tiny.start(0)
     r.d_inputs[...] = r.grad_resid1[...] + grad
-    r.tiny[...] = jnp.zeros_like(r.tiny)
-    r.tiny[0:1, :] = d_norm1
-    tiny = SmallSum(r, "tny", r.tiny, r.tiny_out)
-    tiny.pair()
-    tiny.send(0)
-    small.send(1)
-    for k in range(1, 4):
-        last.turn(k)
-    tiny.send(1)
-    tail.finish()
-    tail_back = return_start(tail.ready, r.tail_out, r.tail_send, r.tail_recv)
-    small.send(2)
+    tiny.collect(0)
+    tiny.start(1)
+    last.turn(1)
+    last.turn(2)
+    last.turn(3)
+    plane.collect(0)
+    plane.start(1)
+    tiny.collect(1)
+    tiny.start(2)
     last.finish()
     last_back = return_start(last.ready, r.last_out, r.last_send, r.last_recv)
-    tiny.send(2)
-    small.close()
-    tiny.close()
+    plane.collect(1)
+    r.down_own[...] = plane.now[32:48]
+    d_rows = rows_start(r.down_own, r.down_out, d_sems)
+    tiny.collect(2)
+    tiny.start(3)
+    rows_finish(d_rows, r.down_out, d_sems)
+    tiny.collect(3)
+    r.small_out[0:32] = plane.now[0:32]
+    r.small_out[32:40] = tiny.now[...]
     shuffle_wait(units_back)
     shuffle_done(units_back)
     shuffle_done(logits)
@@ -1423,8 +1495,6 @@
     return_wait(last.ready, r.last_out, r.last_recv)
     deal_done(tail_back)
     deal_done(last_back)
-    small.done()
-    tiny.done()
     for part in (first, units, tail, last, scan):
         part.done()
 
@@ -1433,8 +1503,9 @@
     rows = (2, 4, 64, 2048)
     small = pltpu.VMEM((4, 64, 64), F32)
     scratch = dict(
-        small=pltpu.VMEM((24, 2304), F32),
-        tiny=pltpu.VMEM((8, 2048), F32),
+        low_own=pltpu.VMEM((64, 16), F32),
+        lows=pltpu.VMEM((2, 4, 64, 16), F32),
+        down_own=pltpu.VMEM((16, HALF), F32),
         attn_own=pltpu.VMEM((64, 2048), BF),
         grad_resid1=pltpu.VMEM((64, 2048), F32),
         attn=pltpu.VMEM(rows, BF),
@@ -1477,8 +1548,10 @@
         scratch.update(shuffle_sems(name))
     scratch.update(rows_sems("rows_a_"))
     scratch.update(scan_scratch())
-    scratch.update(small_scratch("sml", 24, 2304))
-    scratch.update(small_scratch("tny", 8, 2048))
+    for name in ("rows_l_", "rows_d_"):
+        scratch.update(rows_sems(name))
+    for name, height, count in (("group", 32, 2), ("plane", 48, 2), ("tiny", 8, 4)):
+        scratch.update(small_scratch(name, height, count))
     in_hbm = ("second_part", "ffn_part")
     in_vmem = ("norm1_gain", "norm2_gain", "head_gain")
     order = ("acts", "second", "cot", "resid1", "cot_own", "wide_m", "gate_lin", "headnorm")
@@ -1495,8 +1568,8 @@
             last_out=((2, 2, 32, 3 * HALF), BF, VMEM),
             tail_out=((2, 2, 32, 2 * HALF), BF, VMEM),
             units_out=((4, 32, FFN), BF, VMEM),
-            small_out=((24, 2304), F32, VMEM),
-            tiny_out=((8, 2048), F32, VMEM),
+            small_out=((40, HALF), F32, VMEM),
+            down_out=((2, 4, 16, HALF), F32, VMEM),
             out_grads=((4, 4, 128, FFN), BF, ANY),
         ),
         scratch,
@@ -1513,7 +1586,7 @@
         copy.start()
     for copy in copies:
         copy.wait()
-    out, d_in, last, tail, units, small, tiny = held
+    out, d_in, last, tail, units, small, factor = held
     output, d_inputs, norm1, q, k, v, g, o, down, up, bias, head, norm2, fg, fu, fd = outs
     output[...] = out[...]
     d_inputs[...] = d_in[...]
@@ -1528,19 +1601,22 @@
         at = slice(n * UNITS, (n + 1) * UNITS)
         for m, ref in enumerate((fg, fu, fd)):
             ref[:, at] = units[n, :, m * UNITS_PAD : m * UNITS_PAD + UNITS].astype(F32)
-    norm1[...] = tiny[0:1, :]
-    norm2[...] = small[17:18, 0:2048]
-    head[...] = small[18:19, 0:512]
-    bias[...] = small[18:19, 512:768]
-    up[...] = small[0:16, 2048:2304]
-    down[...] = small[0:16, 0:2048]
+    up[...] = small[0:16]
+    for n in range(8):
+        cols = slice(n * HALF, (n + 1) * HALF)
+        norm2[:, cols] = small[16 + n : 17 + n]
+        norm1[:, cols] = small[32 + n : 33 + n]
+        down[:, cols] = factor[n % 2, n // 2]
+    for n in range(2):
+        head[:, n * HALF : (n + 1) * HALF] = small[24 + n : 25 + n]
+    bias[...] = small[26:27]
 
 
 def results(b):
     shapes = [((64, 2048), BF), ((64, 2048), F32), ((1, 2048), F32)]
     shapes += [((32, 1024), F32)] * 5 + [((16, 2048), F32), ((16, 256), F32)]
     shapes += [((1, 256), F32), ((1, 512), F32), ((1, 2048), F32)] + [((32, 4 * UNITS), F32)] * 3
-    names = ("output", "d_inputs", "last_out", "tail_out", "units_out", "small_out", "tiny_out")
+    names = ("output", "d_inputs", "last_out", "tail_out", "units_out", "small_out", "down_out")
     sources = [b[name] for name in names]
     call = pl.pallas_call(
         results_kernel,
@@ -1609,7 +1685,7 @@
     )
 
     operands = dict(
-        f,
+        {name: value for name, value in f.items() if name != "first_own"},
         cot_own=cotangent,
         inputs=inputs,
         up=low_up,

time: 282 us -> 256 us (0.908)
  Pallas kernels: 281 us -> 255 us
    pallas_call x2, Pallas kernels: 277 us -> 252 us  [remote_call(): pl.pallas_call(run, out_shape=[jax.ShapeDtypeStruct(shape, dtype) for sha...]
where the time goes in v5:
time: 256 us
  Pallas kernels  255 us (100%)
    pallas_call x2, Pallas kernels, remote_call(): pl.pallas_call(run, out_shape=[jax.ShapeDtypeStruct(shape, dtype) for sha...  252 us

profile of v5, /device:TPU:1, one launch (start us, length us, event | category | flops | bytes accessed | tf_op | source)
XLA Modules:
  0.0 256.2 jit_solution(15362244961316458608)
XLA Ops:
  0.6 129.8 %shard_map.288 = (bf16[64,2048]{1,0:T(8,128)(2,1)}, f32[64,16]{1,0:T(8,128)}, f32[64,2048]{1,0:T(8,128)}, bf16[4,4,128,512]{3,2,1,0:T(8,128)(2,1)}, bf16[4,4,128...) custom-call(bf16[32,1024]{1,0:T(8,128)(2,1)} %refs_0_.1, ...), custom_call_target="tpu_custom_call" | custom-call | tf_op jit(solution)/shard_map/pallas_call | solution.py:121
  130.4 122.4 %shard_map.289 = (bf16[64,2048]{1,0:T(8,128)(2,1)}, f32[64,2048]{1,0:T(8,128)}, bf16[2,2,32,768]{3,2,1,0:T(8,128)(2,1)}, bf16[2,2,32,512]{3,2,1,0:T(8,128)(2,1)}...) custom-call(bf16[2,4,64,2048]{3,2,1,0:T(8,128)(2,1)} %get-tuple-elem, ...), custom_call_target="tpu_custom_call" | custom-call | tf_op jit(solution)/shard_map/pallas_call | solution.py:121
  252.9 3.1 %shard_map.290 = (bf16[64,2048]{1,0:T(8,128)(2,1)}, f32[64,2048]{1,0:T(8,128)}, f32[1,2048]{1,0:T(1,128)}, f32[32,1024]{1,0:T(8,128)}, f32[32,1024]{1,0:T(8,128)...) custom-call(bf16[64,2048]{1,0:T(8,128)(2,1)} %get-tuple-element.85.r, ...), custom_call_target="tpu_custom_call" | custom-call | tf_op jit(solution)/shard_map/pallas_call | solution.py:1628

commit v6 on v5

--- a/solution.py
+++ b/solution.py
@@ -64,6 +64,33 @@
     )
     copy.start()
     return copy
+
+
+class Pieces:
+    def __init__(self, src, dst, send, recv, peer):
+        self.args = (src, dst, send, recv, peer)
+
+    def copy(self, n):
+        src, dst, send, recv, peer = self.args
+        return pltpu.make_async_remote_copy(
+            src_ref=src(n),
+            dst_ref=dst(n),
+            send_sem=send.at[n],
+            recv_sem=recv.at[n],
+            device_id=peer,
+            device_id_type=MESH,
+        )
+
+    def start(self, n):
+        self.copy(n).start()
+
+    def wait_recv(self, count):
+        for n in range(count):
+            self.copy(n).wait_recv()
+
+    def wait_send(self, count):
+        for n in range(count):
+            self.copy(n).wait_send()
 
 
 class Refs:
@@ -402,7 +429,15 @@
         self.back, self.every = back, r.every
         self.total, self.rows, self.cols, self.entry = r.total, r.scan_y, r.scan_x, r.entry
         self.lead_b, self.lead_a = r.lead_b, r.lead_a
+        x, y, z, c = here()
         self.sems = sems_of(r, "scan", 8)
+        self.swap = Pieces(
+            lambda n: self.every.at[c, n],
+            lambda n: self.every.at[c, n],
+            self.sems[0],
+            self.sems[1],
+            (x, y, z, 1 - c),
+        )
         self.order = [(n, k) for n in range(4) for k in range(2)]
         self.line = list(range(4))
         if back:
@@ -413,26 +448,24 @@
 
     def pack(self, block, state, decay):
         block[:, 0:512] = state.astype(BF)
-        high = decay.astype(BF)
-        block[:, 512:640] = high
-        block[:, 640:768] = (decay - high.astype(F32)).astype(BF)
+        high = decay[:, 0:64].astype(BF).astype(F32)
+        both = jnp.concatenate([high, decay[:, 0:64] - high], axis=1)
+        block[:, 512:640] = both.astype(BF)
 
     def unpack(self, block):
-        keep = block[:, 512:640].astype(F32) + block[:, 640:768].astype(F32)
-        return block[:, 0:512].astype(F32), keep
+        both = block[:, 512:640].astype(F32)
+        keep = both[:, 0:64] + both[:, 64:128]
+        return block[:, 0:512].astype(F32), jnp.concatenate([keep, keep], axis=1)
 
     def factor(self, k, n, width):
         return jnp.concatenate([self.every[k, n, :, 1024:1152]] * (width // 128), axis=1)
 
-    def pair(self):
-        x, y, z, c = here()
-        self.swap = push(
-            self.every.at[c], self.every.at[c], self.sems[0], self.sems[1], (x, y, z, 1 - c)
-        )
+    def pair(self, n):
+        self.swap.start(n)
 
     def send(self):
         x, y, z, c = here()
-        self.swap.wait_recv()
+        self.swap.wait_recv(4)
         half = pl.ds(pl.multiple_of(c * DK, DK), DK)
         n, k = self.order[0]
         state = self.every[k, n, :, half]
@@ -506,7 +539,8 @@
                 state = self.factor(k, n, DK) * state + self.every[k, n, :, cols]
 
     def done(self):
-        for copy in self.far + [self.swap, self.last]:
+        self.swap.wait_send(4)
+        for copy in self.far + [self.last]:
             copy.wait_send()
 
 
@@ -514,13 +548,13 @@
     out = dict(
         every=pltpu.VMEM((2, 4, SLOTS, 1152), F32),
         total=pltpu.VMEM((SLOTS, DK), F32),
-        scan_y=pltpu.VMEM((4, SLOTS, 768), BF),
-        scan_x=pltpu.VMEM((4, SLOTS, 768), BF),
+        scan_y=pltpu.VMEM((4, SLOTS, 640), BF),
+        scan_x=pltpu.VMEM((4, SLOTS, 640), BF),
         lead_b=pltpu.VMEM((SLOTS, DK), F32),
         lead_a=pltpu.VMEM((SLOTS, 128), F32),
         entry=pltpu.VMEM((2, SLOTS, DK), F32),
     )
-    kinds = ((), (), (3,), (3,), (), (), (3,), (3,))
+    kinds = ((4,), (4,), (3,), (3,), (), (), (3,), (3,))
     out.update({f"scan{n}": DMA(shape) for n, shape in enumerate(kinds)})
     return out
 
@@ -769,23 +803,24 @@
     mix.far(0, 1, 2, 3)
     r.save("wide_k", "first", "gate")
 
+    swap = Pieces(
+        lambda n: r.proj.at[1 - c, :, :, tile(n, start=HALF)],
+        lambda n: r.qkv.at[c, :, :, tile(n, start=HALF)],
+        r.swap_s,
+        r.swap_r,
+        partner,
+    )
+
     @pl.loop(0, 2)
     def _(n):
         got = dot(all_rows(r.first), columns(r.wide_k, tile(n)))
         r.proj[:, :, :, tile(n, start=HALF)] = got.astype(BF).reshape(2, 4, 64, HALF)
-
-    key_value = pl.ds(HALF, 2 * HALF)
-    swap = push(
-        r.proj.at[1 - c, :, :, key_value],
-        r.qkv.at[c, :, :, key_value],
-        r.swap_s.at[0],
-        r.swap_r.at[0],
-        partner,
-    )
-    r.qkv[c, :, :, key_value] = r.proj[c, :, :, key_value]
+        swap.start(n)
+        r.qkv[c, :, :, tile(n, start=HALF)] = r.proj[c, :, :, tile(n, start=HALF)]
+
     shuffle_wait(f_deal)
     down.near()
-    swap.wait()
+    swap.wait_recv(2)
 
     @pl.loop(0, 4)
     def _(n):
@@ -795,8 +830,8 @@
         r.cum[n] = cum
         r.every[c, n] = ends
         r.decays[n] = ends[:, 1024:1152]
-
-    scan.pair()
+        scan.pair(n)
+
     mix.relay(0, 1, 2, 3)
     scan.send()
     acts.near()
@@ -810,8 +845,8 @@
     swap_q = push(
         r.proj.at[1 - c, :, :, query],
         r.qkv.at[c, :, :, query],
-        r.swap_s.at[1],
-        r.swap_r.at[1],
+        r.swap_s.at[2],
+        r.swap_r.at[2],
         partner,
     )
     r.qkv[c, :, :, query] = r.proj[c, :, :, query]
@@ -831,6 +866,13 @@
     scan.fold(r.states)
     acts.far(1, 2, 3)
     down.far(1, 2, 3)
+    swap2 = Pieces(
+        lambda n: r.normed.at[1 - c, n],
+        lambda n: r.headnorm.at[c, n],
+        r.norm_s,
+        r.norm_r,
+        partner,
+    )
 
     @pl.loop(0, 4)
     def _(n):
@@ -847,15 +889,15 @@
         normed = rms(mixed, r.head_gain[...])
         for s in range(2):
             r.normed[s, n] = normed[:, s * HALF : (s + 1) * HALF]
-
-    swap2 = push(r.normed.at[1 - c], r.headnorm.at[c], r.swap_s.at[2], r.swap_r.at[2], partner)
+        swap2.start(n)
+
     r.headnorm[c] = r.normed[c]
     r.save("cum", "decays", "states", "near", "far", "probs", "mixing", "mixed", "gate_lin")
     rows_finish(b_rows, r.cot, b_sems)
     r.save("cot")
     acts.relay(0)
     down.relay(0)
-    swap2.wait()
+    swap2.wait_recv(4)
     sums = RowSum(r, "mix", r.parts, lambda k: r.parts[c, k])
     for core in (1 - c, c):
         lin = r.gate_lin[core].reshape(256, HALF)
@@ -919,6 +961,8 @@
         r.ffn_part[:, :, :, tile(n, 512)] = got.astype(BF).reshape(2, 4, 64, 512)
 
     r.save("ffn_part")
+    swap.wait_send(2)
+    swap2.wait_send(4)
     for sent in (k_deal, m_deal):
         deal_done(sent)
     for sent in (gates, f_deal):
@@ -949,6 +993,8 @@
         m_recv=DMA((4,)),
         swap_s=DMA((3,)),
         swap_r=DMA((3,)),
+        norm_s=DMA((4,)),
+        norm_r=DMA((4,)),
     )
     for name in ("rows_a_", "rows_b_", "rows_s_"):
         scratch.update(rows_sems(name))
@@ -1342,8 +1388,8 @@
         )
         r.dmix[n], r.dfar[n], r.dnear[n], r.dscore[n] = dmix, dfar, dnear, dscore
         r.every[c, n] = jnp.concatenate([ends_k, ends_v, r.decays[n]], axis=1)
-
-    scan.pair()
+        scan.pair(n)
+
     split_rows(group.now, 24, r.d_head[0:1])
     scan.send()
 
@@ -1369,6 +1415,9 @@
     scan.fold(r.nexts)
     r.output[...] = (r.resid1[...] + ffn.result()).astype(BF)
     ffn.done()
+    swap2 = Pieces(
+        lambda n: r.dproj.at[1 - c, n], lambda n: r.dqkv.at[c, n], r.dqkv_s, r.dqkv_r, partner
+    )
 
     @pl.loop(0, 4)
     def _(n):
@@ -1399,12 +1448,12 @@
                 r.dproj[s, n, :, pl.ds(m * HALF, HALF)] = part[
                     :, s * HALF : (s + 1) * HALF
                 ].astype(BF)
+        swap2.start(n)
         r.dlogit[n] = dlogit
 
-    swap2 = push(r.dproj.at[1 - c], r.dqkv.at[c], r.swap_s.at[1], r.swap_r.at[1], partner)
     r.dqkv[c] = r.dproj[c]
     logits = shuffle_start(lambda k: r.dlogit.at[k], r.dl.at[z], *sems_of(r, "gate", 3))
-    swap2.wait()
+    swap2.wait_recv(4)
 
     for e in (1, 2, 3, 0):
         at = wrap(x + e)
@@ -1488,6 +1537,7 @@
     tiny.collect(3)
     r.small_out[0:32] = plane.now[0:32]
     r.small_out[32:40] = tiny.now[...]
+    swap2.wait_send(4)
     shuffle_wait(units_back)
     shuffle_done(units_back)
     shuffle_done(logits)
@@ -1530,8 +1580,10 @@
         stage_s=DMA((3,)),
         grads_tail=pltpu.VMEM((4, 4, 128, 2 * HALF), BF),
         grads_last=pltpu.VMEM((4, 4, 128, 3 * HALF), BF),
-        swap_s=DMA((2,)),
-        swap_r=DMA((2,)),
+        swap_s=DMA((1,)),
+        swap_r=DMA((1,)),
+        dqkv_s=DMA((4,)),
+        dqkv_r=DMA((4,)),
         tail_send=DMA((4,)),
         tail_recv=DMA((2, 2)),
         last_send=DMA((4,)),

time: 256 us -> 254 us (level)
  no operation moved by 1% of the time
where the time goes in v6:
time: 254 us
  Pallas kernels  253 us (100%)
    pallas_call x2, Pallas kernels, remote_call(): pl.pallas_call(run, out_shape=[jax.ShapeDtypeStruct(shape, dtype) for sha...  250 us

profile of v6, /device:TPU:1, one launch (start us, length us, event | category | flops | bytes accessed | tf_op | source)
XLA Modules:
  0.0 253.8 jit_solution(5864433812289725794)
XLA Ops:
  0.6 129.1 %shard_map.288 = (bf16[64,2048]{1,0:T(8,128)(2,1)}, f32[64,16]{1,0:T(8,128)}, f32[64,2048]{1,0:T(8,128)}, bf16[4,4,128,512]{3,2,1,0:T(8,128)(2,1)}, bf16[4,4,128...) custom-call(bf16[32,1024]{1,0:T(8,128)(2,1)} %refs_0_.1, ...), custom_call_target="tpu_custom_call" | custom-call | tf_op jit(solution)/shard_map/pallas_call | solution.py:148
  129.7 120.8 %shard_map.289 = (bf16[64,2048]{1,0:T(8,128)(2,1)}, f32[64,2048]{1,0:T(8,128)}, bf16[2,2,32,768]{3,2,1,0:T(8,128)(2,1)}, bf16[2,2,32,512]{3,2,1,0:T(8,128)(2,1)}...) custom-call(bf16[2,4,64,2048]{3,2,1,0:T(8,128)(2,1)} %get-tuple-elem, ...), custom_call_target="tpu_custom_call" | custom-call | tf_op jit(solution)/shard_map/pallas_call | solution.py:148
  250.5 3.1 %shard_map.290 = (bf16[64,2048]{1,0:T(8,128)(2,1)}, f32[64,2048]{1,0:T(8,128)}, f32[1,2048]{1,0:T(1,128)}, f32[32,1024]{1,0:T(8,128)}, f32[32,1024]{1,0:T(8,128)...) custom-call(bf16[64,2048]{1,0:T(8,128)(2,1)} %get-tuple-element.85.r, ...), custom_call_target="tpu_custom_call" | custom-call | tf_op jit(solution)/shard_map/pallas_call | solution.py:1680

commit v7 on v6

--- a/solution.py
+++ b/solution.py
@@ -237,7 +237,7 @@
     hops = {}
     for h in range(2):
         rows = pl.ds(h * half, half)
-        for d in range(1, 4):
+        for d in (2, 1, 3):
             hops[h, d] = push(
                 src.at[rows],
                 out.at[c, z, rows],
@@ -254,7 +254,7 @@
     hop_s, hop_r, pair_s, pair_r, own = sems
     mine, hops, pairs = started
     half = out.shape[2] // 2
-    for h, d in hops:
+    for h, d in [(h, d) for h in range(2) for d in (1, 3, 2)]:
         hops[h, d].wait_recv()
         block = out.at[c, wrap(z - d), pl.ds(h * half, half)]
         pairs.append(
@@ -374,33 +374,31 @@
 
     def pairs(self):
         x, y, z, c = here()
-        self.pair = [
-            push(
+        self.pair = {
+            k: push(
                 self.parts.at[1 - c, wrap(z + 1 + k)],
                 self.theirs.at[k],
                 self.sems[0].at[k],
                 self.sems[1].at[k],
                 (x, y, z, 1 - c),
             )
-            for k in range(4)
-        ]
+            for k in (1, 0, 2, 3)
+        }
 
     def hops(self):
         x, y, z, c = here()
-        self.hop = []
-        for k in range(3):
+        self.hop = {}
+        for k in (1, 0, 2):
             to = wrap(z + 1 + k)
             self.pair[k].wait_recv()
             both = self.own(to).astype(F32) + self.theirs[k].astype(F32)
             self.theirs[k] = both.astype(BF)
-            self.hop.append(
-                push(
-                    self.theirs.at[k],
-                    self.landed.at[k],
-                    self.sems[2].at[k],
-                    self.sems[3].at[k],
-                    (x, y, to, c),
-                )
+            self.hop[k] = push(
+                self.theirs.at[k],
+                self.landed.at[k],
+                self.sems[2].at[k],
+                self.sems[3].at[k],
+                (x, y, to, c),
             )
 
     def result(self):
@@ -413,7 +411,7 @@
         return value
 
     def done(self):
-        for copy in self.pair + self.hop:
+        for copy in list(self.pair.values()) + list(self.hop.values()):
             copy.wait_send()
 
 

time: 254 us -> 253 us (level)
  no operation moved by 1% of the time
where the time goes in v7:
time: 253 us
  Pallas kernels  252 us (100%)
    pallas_call x2, Pallas kernels, remote_call(): pl.pallas_call(run, out_shape=[jax.ShapeDtypeStruct(shape, dtype) for sha...  249 us

profile of v7, /device:TPU:1, one launch (start us, length us, event | category | flops | bytes accessed | tf_op | source)
XLA Modules:
  0.0 253.0 jit_solution(6095215041863875346)
XLA Ops:
  0.6 128.8 %shard_map.288 = (bf16[64,2048]{1,0:T(8,128)(2,1)}, f32[64,16]{1,0:T(8,128)}, f32[64,2048]{1,0:T(8,128)}, bf16[4,4,128,512]{3,2,1,0:T(8,128)(2,1)}, bf16[4,4,128...) custom-call(bf16[32,1024]{1,0:T(8,128)(2,1)} %refs_0_.1, ...), custom_call_target="tpu_custom_call" | custom-call | tf_op jit(solution)/shard_map/pallas_call | solution.py:148
  129.4 120.2 %shard_map.289 = (bf16[64,2048]{1,0:T(8,128)(2,1)}, f32[64,2048]{1,0:T(8,128)}, bf16[2,2,32,768]{3,2,1,0:T(8,128)(2,1)}, bf16[2,2,32,512]{3,2,1,0:T(8,128)(2,1)}...) custom-call(bf16[2,4,64,2048]{3,2,1,0:T(8,128)(2,1)} %get-tuple-elem, ...), custom_call_target="tpu_custom_call" | custom-call | tf_op jit(solution)/shard_map/pallas_call | solution.py:148
  249.7 3.1 %shard_map.290 = (bf16[64,2048]{1,0:T(8,128)(2,1)}, f32[64,2048]{1,0:T(8,128)}, f32[1,2048]{1,0:T(1,128)}, f32[32,1024]{1,0:T(8,128)}, f32[32,1024]{1,0:T(8,128)...) custom-call(bf16[64,2048]{1,0:T(8,128)(2,1)} %get-tuple-element.85.r, ...), custom_call_target="tpu_custom_call" | custom-call | tf_op jit(solution)/shard_map/pallas_call | solution.py:1678
